TPU v7x, 32 devices: a whole 2x2x4 slice. The times are simulated.
32 devices in a mesh: section: 4 (over y, core), dp: 8 (over z, x).
Axes of the slice: x: 2, y: 2, z: 4, core: 2. Of those that a mesh axis runs over, the one named last changes fastest.
Arguments:
- w_in: bfloat16 [4, 5120, 4096], P('section', 'dp'), may hold values from -0.09375 to 0.09375
- w_out: bfloat16 [4, 5120, 4096], P('section', 'dp'), may hold values from -0.078125 to 0.078125
- input_stash: bfloat16 [4, 2, 128, 4096], P('section', None, 'dp'), may hold values from -6 to 6
- hidden_stash: bfloat16 [4, 2, 128, 5120], P('section', None, None, 'dp'), may hold values from -6 to 6
- gate_stash: float32 [4, 2, 128], P('section'), may hold values from 0.25 to 1
- block_pick: int32 [4, 2], P('section'), may hold values from 0 to 1
- slot_order: int32 [4, 2], P('section'), may hold values from 0 to 1, each once within a row
- arriving: bfloat16 [4, 2, 128, 4096], P('section', None, 'dp'), may hold values from -6 to 6
- loss_grads: bfloat16 [1, 2, 128, 4096], P(None, None, 'dp'), may hold values from -6 to 6
Outputs:
- passed: bfloat16 [4, 2, 2, 128, 4096], P('section', None, None, 'dp')
- grad_in: bfloat16 [4, 5120, 4096], P('section', 'dp')
- grad_out: bfloat16 [4, 5120, 4096], P('section', 'dp')
- gate_grads: float32 [4, 2, 128], P('section')
Inputs may be any that keep to these rules, and one draw needn't show every extreme that they name: Each row of slot_order holds every slot 0 to 1 once.
All inputs are finite; a program needn't handle non-finite values.
Results may differ from a plain program's by a relative error of at most 0.0055.
Values may be sent and summed in bfloat16 or wider, within the bound.
No kernel may reach another device: no remote copies, remote signals or barrier semaphores. Data moves between devices by JAX's collectives and lax.ppermute only.
A program may use at most 128 MiB of HBM per device.

v0:
```python
import jax
import jax.numpy as jnp
from jax import lax
from jax.sharding import PartitionSpec as P


def shifted_2(block, axis, distance):
    devices = range(lax.axis_size(axis))
    route = [(i - distance, i) for i in devices if i - distance in devices]
    return lax.ppermute(block, axis, route)


def per_device(
    w_in, w_out, input_stash, hidden_stash, gate_stash, block_pick, slot_order, arriving, loss_grads
):
    in_weight = w_in[0]
    out_weight = w_out[0]
    ticks = slot_order.shape[1]
    blocks = arriving.shape[1]
    is_top = lax.axis_index("section") == lax.axis_size("section") - 1
    contract = (((0,), (0,)), ((), ()))

    def section_tick(incoming, tick_index):
        slot_id = slot_order[0, tick_index]
        block_id = block_pick[0, slot_id]
        gate_vals = gate_stash[0, slot_id]
        pre_act = hidden_stash[0, slot_id]
        own_rows = incoming[block_id]
        rows_input, rows_grad = (
            lax.all_gather(input_stash[0, slot_id], "dp", axis=0, tiled=True),
            lax.all_gather(own_rows, "dp", axis=0, tiled=True),
        )
        upstream = lax.dot_general(
            rows_grad, out_weight, (((1,), (1,)), ((), ())), preferred_element_type=jnp.float32
        )
        active = jnp.maximum(pre_act.astype(jnp.float32), 0.0)
        hid_grad = jnp.where(pre_act > 0, upstream * gate_vals[:, None], 0.0).astype(jnp.bfloat16)
        input_part = lax.psum_scatter(
            jnp.dot(hid_grad, in_weight, preferred_element_type=jnp.float32),
            "dp",
            scatter_dimension=0,
            tiled=True,
        )
        placed = jnp.where((jnp.arange(blocks) == block_id)[:, None, None], input_part[None], 0.0)
        updated = (incoming.astype(jnp.float32) + placed).astype(jnp.bfloat16)
        gate_part = jnp.sum(active * upstream, axis=1)
        gate_part = lax.psum(gate_part, "dp")
        weighted = (active * gate_vals[:, None]).astype(jnp.bfloat16)
        return (updated, gate_part, (rows_grad, weighted, hid_grad, rows_input))

    def weight_terms(pieces):
        rows_grad, weighted, hid_grad, rows_input = pieces
        out_term = lax.dot_general(
            weighted, rows_grad, contract, preferred_element_type=jnp.float32
        )
        in_term = lax.dot_general(
            hid_grad, rows_input, contract, preferred_element_type=jnp.float32
        )
        return (out_term, in_term)

    start_sums = (jnp.zeros(out_weight.shape, jnp.float32), jnp.zeros(in_weight.shape, jnp.float32))

    def advance(carry, extra):
        incoming, sums = carry
        tick_index, loss_rows = extra
        updated, gate_part, pieces = section_tick(incoming, tick_index)
        terms = weight_terms(pieces)
        sums = (sums[0] + terms[0], sums[1] + terms[1])
        shifted = shifted_2(updated, "section", -1)
        following = jnp.where(is_top, loss_rows, shifted)
        return ((following, sums), (updated, gate_part))

    (last_in, sums), (early_out, early_gate) = lax.scan(
        advance, (arriving[0], start_sums), (jnp.arange(ticks - 1), loss_grads)
    )
    last_out, last_gate, last_pieces = section_tick(last_in, ticks - 1)
    terms = weight_terms(last_pieces)
    out_sum = sums[0] + terms[0]
    in_sum = sums[1] + terms[1]
    passed = jnp.concatenate([early_out, last_out[None]], axis=0)
    gate_parts = jnp.concatenate([early_gate, last_gate[None]], axis=0)
    onehot = (slot_order[0][:, None] == jnp.arange(ticks)[None, :]).astype(jnp.float32)
    gate_grads = jnp.einsum("tp,tr->pr", onehot, gate_parts, precision=lax.Precision.HIGHEST)
    return (
        passed[None],
        in_sum.astype(jnp.bfloat16)[None],
        out_sum.astype(jnp.bfloat16)[None],
        gate_grads[None],
    )


def solution(mesh):
    placed = (
        P("section", "dp", None),
        P("section", "dp", None),
        P("section", None, "dp", None),
        P("section", None, None, "dp"),
        P("section", None, None),
        P("section", None),
        P("section", None),
        P("section", None, "dp", None),
        P(None, None, "dp", None),
    )
    return jax.shard_map(
        per_device,
        mesh=mesh,
        in_specs=placed,
        out_specs=(
            P("section", None, None, "dp", None),
            P("section", "dp", None),
            P("section", "dp", None),
            P("section", None, None),
        ),
        check_vma=False,
    )
```

profile of v0, /device:TPU:0, one launch (start us, length us, event | category | flops | bytes accessed | tf_op | source)
XLA Modules:
  0.0 343.4 jit_solution(15895706886522332823)
XLA Ops:
  7.2 0.0 all-gather.9.cloned.1.call-start
  7.2 1.3 fusion.45
  12.4 1.3 constant_dynamic-slice_fusion.4
  15.7 1.6 constant_dynamic-slice_fusion.6
  17.2 0.0 all-gather.9.cloned.1.call-update
  17.3 0.0 reduce-scatter.3.cloned.1.call-start
  17.3 0.8 fusion.40
  18.1 42.2 %all-gather.9.cloned.1.call-done = bf16[1,1,128,4096]{3,2,1,0:T(8,128)(2,1)} async-done(((bf16[1,1,16,4096]{3,2,1,0:T(8,128)(2,1)}), bf16[1,1,128,4096]{3,2,1,0:T(8,128)(2,1)}) %all-gather.9.cloned.1.call-update) | async-done | bytes 1048592 | tf_op jit(solution)/shard_map/while/body/eval_jaxpr/all_gather | solution.py:31
  60.3 4.7 %select_convert_fusion.1 = (bf16[128,640]{1,0:T(8,128)(2,1)S(1)}, f32[128,640]{1,0:T(8,128)S(1)}) fusion(f32[128]{0:T(128)S(1)} %get-tuple-element.42, bf16[1,2,128,640]{3,2,1,0:T(8,128)(2,1)} %param.12, s32[]{:T(128)S(6)} %select_n.57, bf16[1,640,4096]{2,1,0:T(8,128)(2,1)} %param.10, bf16[1,1,128,4096]{3,2,1,0:T(8,128)(2,1)} %all-gather.9.cloned.1.call-done), kind=kOutput, calls=%fused_computation.39 | convolution fusion | flops 671416320 | bytes 6947332 | tf_op jit(solution)/shard_map/while/body/eval_jaxpr/dot_general | solution.py:33
  65.0 0.0 copy-done
  65.0 0.0 copy-start.4
  65.0 0.0 copy-start.7
  65.0 0.0 copy-start.6
  65.0 0.0 copy-start.3
  65.0 2.3 fusion.4
  67.3 0.0 reduce-scatter.3.cloned.1.call-update
  67.4 0.0 all-gather.11.cloned.1.call-start
  67.4 0.7 iota_compare_fusion.1
  68.1 66.1 %reduce-scatter.3.cloned.1.call-done = f32[16,4096]{1,0:T(8,128)} async-done(((f32[128,4096]{1,0:T(8,128)}), f32[16,4096]{1,0:T(8,128)}) %reduce-scatter.3.cloned.1.call-update) | async-done | bytes 262160 | tf_op jit(solution)/shard_map/while/body/eval_jaxpr/reduce_scatter | solution.py:38
  134.1 1.1 fusion.20
  135.2 1.3 collective-permute-start
  138.5 0.2 collective-permute-done
  138.7 0.7 constant_dynamic-slice_fusion.3
  139.4 0.0 all-gather.11.cloned.1.call-update
  139.4 0.0 all-gather.13.cloned.1.call-start
  139.4 0.7 constant_dynamic-slice_fusion
  140.2 0.0 all-gather.13.cloned.1.call-update
  140.2 0.0 all-gather.15.cloned.1.call-start
  140.2 0.5 all-gather.15.cloned.1.call-update
  140.8 0.0 reduce-scatter.5.cloned.1.call-start
  140.8 40.7 %all-gather.11.cloned.1.call-done = bf16[1,128,4096]{2,1,0:T(8,128)(2,1)} async-done(((bf16[1,16,4096]{2,1,0:T(8,128)(2,1)}), bf16[1,128,4096]{2,1,0:T(8,128)(2,1)}) %all-gather.11.cloned.1.call-update) | async-done | bytes 1048592 | tf_op jit(solution)/shard_map/all_gather | solution.py:31
  181.5 4.7 %fusion.24 = (f32[128]{0:T(128)S(1)}, f32[128]{0:T(128)S(1)}, bf16[128,640]{1,0:T(8,128)(2,1)S(1)}) fusion(f32[128,640]{1,0:T(8,128)S(1)} %get-tuple-element.63, bf16[1,2,128,640]{3,2,1,0:T(8,128)(2,1)S(1)} %copy-done.3, s32[]{:T(128)S(6)} %select_n.57, s32[]{:T(128)S(6)} %select_n.64, f32[128]{0:T(128)S(1)} %get-tuple-element.41, ...), kind=kOutput, calls=%fused_computation.35 | convolution fusion | flops 672071424 | bytes 7112200 | tf_op jit(solution)/shard_map/dot_general | solution.py:33
  186.2 4.9 %fusion.2 = f32[128,4096]{1,0:T(8,128)} fusion(bf16[128,640]{1,0:T(8,128)(2,1)S(1)} %get-tuple-element.38, bf16[1,640,4096]{2,1,0:T(8,128)(2,1)} %param.9), kind=kOutput, calls=%fused_computation.4 | convolution fusion | flops 671088640 | bytes 7503872 | tf_op jit(solution)/shard_map/dot_general | solution.py:39
  191.1 0.0 reduce-scatter.5.cloned.1.call-update
  191.1 0.7 iota_compare_fusion
  191.8 5.5 %fusion.15 = f32[640,4096]{1,0:T(8,128)} fusion(bf16[1,1,128,4096]{3,2,1,0:T(8,128)(2,1)S(1)} %copy-done.1, f32[128]{0:T(128)S(1)} %get-tuple-element.42, bf16[1,2,128,640]{3,2,1,0:T(8,128)(2,1)S(1)} %copy-done.3, s32[]{:T(128)S(6)} %select_n.57), kind=kOutput, calls=%fused_computation.18 | convolution fusion | flops 671416320 | bytes 11698692 | tf_op jit(solution)/shard_map/while/body/eval_jaxpr/dot_general | solution.py:53
  197.3 25.8 %all-gather.13.cloned.1.call-done = bf16[1,1,128,4096]{3,2,1,0:T(8,128)(2,1)} async-done(((bf16[1,1,16,4096]{3,2,1,0:T(8,128)(2,1)}), bf16[1,1,128,4096]{3,2,1,0:T(8,128)(2,1)}) %all-gather.13.cloned.1.call-update) | async-done | bytes 1048592 | tf_op jit(solution)/shard_map/while/body/eval_jaxpr/all_gather | solution.py:30
  223.1 6.8 %fusion.11 = f32[640,4096]{1,0:T(8,128)} fusion(bf16[128,640]{1,0:T(8,128)(2,1)S(1)} %get-tuple-element.62, bf16[1,1,128,4096]{3,2,1,0:T(8,128)(2,1)} %all-gather.13.cloned.1.call-done), kind=kOutput, calls=%fused_computation.14 | convolution fusion | flops 671088640 | bytes 11698176 | tf_op jit(solution)/shard_map/while/body/eval_jaxpr/dot_general | solution.py:56
  229.8 0.0 copy-done.5
  229.8 0.1 fusion.18
  230.0 19.3 %all-reduce = (f32[1,128]{1,0:T(1,128)S(1)}, f32[1,128]{1,0:T(1,128)S(1)}) all-reduce(f32[1,128]{1,0:T(1,128)S(1)} %bitcast.89, f32[1,128]{1,0:T(1,128)S(1)} %bitcast.88), channel_id=1, replica_groups=mesh['section'=4,'dp'=8] {'dp'}, use_global_device_ids=true, to_apply=%region_5.6 | all-reduce | flops 256 | bytes 2048 | tf_op jit(solution)/shard_map/psum | solution.py:47
  249.3 0.8 convolution_bitcast_fusion
  250.1 8.0 %fusion.1 = bf16[1,640,4096]{2,1,0:T(8,128)(2,1)} fusion(f32[640,4096]{1,0:T(8,128)} %fusion.15, bf16[1,128,4096]{2,1,0:T(8,128)(2,1)S(1)} %copy-done.2, f32[128]{0:T(128)S(1)} %get-tuple-element.41, bf16[1,2,128,640]{3,2,1,0:T(8,128)(2,1)S(1)} %copy-done.3, s32[]{:T(128)S(6)} %select_n.64), kind=kOutput, calls=%fused_computation.3 | convolution fusion | flops 676659200 | bytes 16941572 | tf_op jit(solution)/shard_map/dot_general | solution.py:53
  258.0 6.5 %all-gather.15.cloned.1.call-done = bf16[1,1,128,4096]{3,2,1,0:T(8,128)(2,1)} async-done(((bf16[1,1,16,4096]{3,2,1,0:T(8,128)(2,1)}), bf16[1,1,128,4096]{3,2,1,0:T(8,128)(2,1)}) %all-gather.15.cloned.1.call-update) | async-done | bytes 1048592 | tf_op jit(solution)/shard_map/all_gather | solution.py:30
  264.6 8.2 %fusion = bf16[1,640,4096]{2,1,0:T(8,128)(2,1)} fusion(f32[640,4096]{1,0:T(8,128)} %fusion.11, bf16[128,640]{1,0:T(8,128)(2,1)S(1)} %get-tuple-element.38, bf16[1,1,128,4096]{3,2,1,0:T(8,128)(2,1)} %all-gather.15.cloned.1.call-done), kind=kOutput, calls=%fused_computation.2 | convolution fusion | flops 676331520 | bytes 16941056 | tf_op jit(solution)/shard_map/dot_general | solution.py:56
  272.8 61.8 %reduce-scatter.5.cloned.1.call-done = f32[16,4096]{1,0:T(8,128)} async-done(((f32[128,4096]{1,0:T(8,128)}), f32[16,4096]{1,0:T(8,128)}) %reduce-scatter.5.cloned.1.call-update) | async-done | bytes 262160 | tf_op jit(solution)/shard_map/reduce_scatter | solution.py:38
  334.6 1.1 fusion.25
  335.7 0.8 maximum_bitcast_fusion
  (13 shorter events, 0.1 us)
Async XLA Ops:
  7.2 53.1 %all-gather.9.cloned.1.call-start = ((), (), s32[]{:S(2)}) async-start(), calls=%async_computation.4 | async-start | bytes 1179648 | tf_op jit(solution)/shard_map/while/body/eval_jaxpr/all_gather | solution.py:31
  17.3 116.9 %reduce-scatter.3.cloned.1.call-start = ((), (), s32[]{:S(2)}) async-start(), calls=%async_computation.2 | async-start | bytes 2359296 | tf_op jit(solution)/shard_map/while/body/eval_jaxpr/reduce_scatter | solution.py:38
  60.3 4.7 %copy-start = (bf16[1,640,4096]{2,1,0:T(8,128)(2,1)S(1)}, bf16[1,640,4096]{2,1,0:T(8,128)(2,1)}, u32[]{:S(2)}) copy-start(bf16[1,640,4096]{2,1,0:T(8,128)(2,1)} %param.9) | copy-start | bytes 15728644
  65.0 69.2 %copy-start.4 = (bf16[1,2,16,4096]{3,2,1,0:T(8,128)(2,1)S(1)}, bf16[1,2,16,4096]{3,2,1,0:T(8,128)(2,1)}, u32[]{:S(2)}) copy-start(bf16[1,2,16,4096]{3,2,1,0:T(8,128)(2,1)} %param.16) | copy-start | bytes 786436
  65.0 73.7 %copy-start.7 = (bf16[1,2,16,4096]{3,2,1,0:T(8,128)(2,1)S(1)}, bf16[1,2,16,4096]{3,2,1,0:T(8,128)(2,1)}, u32[]{:S(2)}) copy-start(bf16[1,2,16,4096]{3,2,1,0:T(8,128)(2,1)} %param.17) | copy-start | bytes 786436
  65.0 74.4 %copy-start.6 = (bf16[1,2,16,4096]{3,2,1,0:T(8,128)(2,1)S(1)}, bf16[1,2,16,4096]{3,2,1,0:T(8,128)(2,1)}, u32[]{:S(2)}) copy-start(bf16[1,2,16,4096]{3,2,1,0:T(8,128)(2,1)} %param.11) | copy-start | bytes 786436
  65.0 116.5 %copy-start.3 = (bf16[1,2,128,640]{3,2,1,0:T(8,128)(2,1)S(1)}, bf16[1,2,128,640]{3,2,1,0:T(8,128)(2,1)}, u32[]{:S(2)}) copy-start(bf16[1,2,128,640]{3,2,1,0:T(8,128)(2,1)} %param.12) | copy-start | bytes 983044
  67.4 114.1 %all-gather.11.cloned.1.call-start = ((), (), s32[]{:S(2)}) async-start(), calls=%async_computation.5 | async-start | bytes 1179648 | tf_op jit(solution)/shard_map/all_gather | solution.py:31
  135.2 3.4 collective-permute-start
  139.4 83.7 %all-gather.13.cloned.1.call-start = ((), (), s32[]{:S(2)}) async-start(), calls=%async_computation.6 | async-start | bytes 1179648 | tf_op jit(solution)/shard_map/while/body/eval_jaxpr/all_gather | solution.py:30
  140.2 124.4 %all-gather.15.cloned.1.call-start = ((), (), s32[]{:S(2)}) async-start(), calls=%async_computation.7 | async-start | bytes 1179648 | tf_op jit(solution)/shard_map/all_gather | solution.py:30
  140.8 193.9 %reduce-scatter.5.cloned.1.call-start = ((), (), s32[]{:S(2)}) async-start(), calls=%async_computation.3 | async-start | bytes 2359296 | tf_op jit(solution)/shard_map/reduce_scatter | solution.py:38
  186.2 5.6 %copy-start.1 = (bf16[1,1,128,4096]{3,2,1,0:T(8,128)(2,1)S(1)}, bf16[1,1,128,4096]{3,2,1,0:T(8,128)(2,1)}, u32[]{:S(2)}) copy-start(bf16[1,1,128,4096]{3,2,1,0:T(8,128)(2,1)} %all-gather.9.cloned.1.call-done) | copy-start | bytes 3145732
  197.2 32.6 %copy-start.5 = (f32[16,4096]{1,0:T(8,128)S(1)}, f32[16,4096]{1,0:T(8,128)}, u32[]{:S(2)}) copy-start(f32[16,4096]{1,0:T(8,128)} %reduce-scatter.3.cloned.1.call-done) | copy-start | bytes 786436
  197.3 52.0 %copy-start.8 = (s32[1,2]{1,0:T(1,128)S(1)}, s32[1,2]{1,0:T(1,128)}, u32[]{:S(2)}) copy-start(s32[1,2]{1,0:T(1,128)} %param.15) | copy-start | bytes 28
  197.3 52.8 %copy-start.2 = (bf16[1,128,4096]{2,1,0:T(8,128)(2,1)S(1)}, bf16[1,128,4096]{2,1,0:T(8,128)(2,1)}, u32[]{:S(2)}) copy-start(bf16[1,128,4096]{2,1,0:T(8,128)(2,1)} %all-gather.11.cloned.1.call-done) | copy-start | bytes 3145732
Sparse Core Ops, SparseCore 0:
  17.4 42.8 all-gather.8
  67.5 66.6 reduce-scatter.2
  139.5 41.9 all-gather.10
  184.1 38.9 all-gather.12
  225.6 38.9 all-gather.14
  268.0 66.6 reduce-scatter.4
where the time goes:
time: 344 us; the launch traced here: 343 us
  waiting for transfers between devices  244 us (71%)
  matrix products  45.8 us (13%)
  between operations  22 us (6%)
  blocking collectives  19.3 us (6%)
  local copies, waits for them, and re-layouts  6.42 us (2%)
  other arithmetic  4.47 us (1%)
    reduce_scatter x2, waiting for transfers between devices, section_tick(): lax.psum_scatter(jnp.dot(hid_grad, in_weight, preferred_element_type=jnp....  128 us
    all_gather x2, waiting for transfers between devices, section_tick(): lax.all_gather(own_rows, 'dp', axis=0, tiled=True)  82.9 us
    all_gather x2, waiting for transfers between devices, section_tick(): lax.all_gather(input_stash[0, slot_id], 'dp', axis=0, tiled=True)  32.4 us
    psum x1, blocking collectives, section_tick(): gate_part = lax.psum(gate_part, 'dp')  19.3 us
    dot_general x2, matrix products, weight_terms(): lax.dot_general(hid_grad, rows_input, contract, preferred_element_type=jn...  15 us
    dot_general x2, matrix products, weight_terms(): lax.dot_general(weighted, rows_grad, contract, preferred_element_type=jnp...  13.4 us
    dot_general x2, matrix products, section_tick(): lax.dot_general(rows_grad, out_weight, (((1,), (1,)), ((), ())), preferre...  9.35 us
    dot_general x2, matrix products, section_tick(): jnp.dot(hid_grad, in_weight, preferred_element_type=jnp.float32)  7.23 us
  transfers between devices with their start and end apart: 7, of which 7 were waited for; matrix products, arithmetic and copies ran while one was open for 12% of the time, Pallas kernels for 0%

commit v1 on v0

v1 whole, which is shorter than its diff:
```python
import functools

import jax
import jax.numpy as jnp
from jax import lax
from jax.experimental import pallas as pl
from jax.experimental.pallas import tpu as pltpu
from jax.sharding import PartitionSpec as P

BF16 = jnp.bfloat16
F32 = jnp.float32
VMEM = pl.BlockSpec(memory_space=pltpu.VMEM)
SMEM = pl.BlockSpec(memory_space=pltpu.SMEM)
ANY = pl.BlockSpec(memory_space=pl.ANY)
PARAMS = pltpu.CompilerParams(vmem_limit_bytes=32 * 2**20)


def column_tile(width):
    return 512 if width % 512 == 0 else width


def expert_kernel(devices, inner, scalars, *refs):
    chunks = refs[:devices]
    w_out, w_in, hidden, gates = refs[devices : devices + 4]
    parts = refs[devices + 4 : 2 * devices + 4]
    rows_ref, weighted_ref, hid_ref, gate_ref, pre_ref, scale_ref = refs[2 * devices + 4 :]
    rows = chunks[0].shape[0]
    me, slot = scalars[0], scalars[1]
    for k in range(devices):
        own = pl.ds(k * rows, rows)
        rows_ref[own, :] = chunks[k][...]
        pre_ref[own, :] = hidden[slot, me ^ k]
        scale_ref[own, :] = gates[slot, me ^ k]
    upstream = lax.dot_general(
        rows_ref[...], w_out[...], (((1,), (1,)), ((), ())), preferred_element_type=F32
    )
    pre = pre_ref[...].astype(F32)
    scale = scale_ref[...]
    active = jnp.maximum(pre, 0.0)
    gate_sum = jnp.sum(active * upstream, axis=1, keepdims=True)
    weighted_ref[...] = (active * scale).astype(BF16)
    hid_grad = jnp.where(pre > 0, upstream * scale, 0.0).astype(BF16)
    outer = devices // inner
    for k in range(devices):
        peer = me ^ k
        gate_ref[peer] = gate_sum[k * rows : (k + 1) * rows]
        place = (peer % inner) * outer + peer // inner
        hid_ref[place] = hid_grad[k * rows : (k + 1) * rows]
    width = w_in.shape[1]
    tile = column_tile(width)
    for start in range(0, width, tile):
        cols = pl.ds(start, tile)
        part = jnp.dot(hid_grad, w_in[:, cols], preferred_element_type=F32).astype(BF16)
        for k in range(devices):
            parts[k][:, cols] = part[k * rows : (k + 1) * rows]


def expert(chunks, w_out, w_in, hidden, gates, scalars, inner):
    devices = len(chunks)
    rows, width = chunks[0].shape
    units = w_out.shape[0]
    tokens = devices * rows
    chunk = jax.ShapeDtypeStruct((rows, width), BF16)
    flops = 4 * tokens * units * width
    return pl.pallas_call(
        functools.partial(expert_kernel, devices, inner),
        in_specs=[SMEM] + [VMEM] * (devices + 4),
        out_specs=[VMEM] * (devices + 4),
        out_shape=[chunk] * devices
        + [
            jax.ShapeDtypeStruct((tokens, width), BF16),
            jax.ShapeDtypeStruct((tokens, units), BF16),
            jax.ShapeDtypeStruct((devices, rows, units), BF16),
            jax.ShapeDtypeStruct((devices, rows, 1), F32),
        ],
        scratch_shapes=[pltpu.VMEM((tokens, units), BF16), pltpu.VMEM((tokens, 1), F32)],
        compiler_params=PARAMS,
        cost_estimate=pl.CostEstimate(flops=flops, bytes_accessed=2 * 2**20, transcendentals=0),
        name="expert_tick",
    )(scalars, *chunks, w_out, w_in, hidden, gates)


def grads_kernel(ticks, slots, saved, *refs):
    rows_refs = refs[:ticks]
    weighted_refs = refs[ticks : 2 * ticks]
    hid_refs = refs[2 * ticks : 3 * ticks]
    grad_in, grad_out, hid_all, hid_t, weighted_t, in_buf, out_buf, sems = refs[3 * ticks :]
    devices, rows, units = hid_refs[0].shape
    tokens = devices * rows
    for t in range(ticks):
        for d in range(devices):
            hid_all[d * ticks + slots[0, t]] = hid_refs[t][d]
        weighted_t[:, t * tokens : (t + 1) * tokens] = weighted_refs[t][...].T
    hid_t[...] = hid_all[...].reshape(ticks * tokens, units).T
    width = grad_in.shape[1]
    tile = column_tile(width)
    steps = width // tile
    copies = []
    for step in range(steps):
        cols = pl.ds(step * tile, tile)
        buf = step % 2
        if step >= 2:
            for copy in copies[2 * (step - 2) : 2 * (step - 1)]:
                copy.wait()
        in_buf[buf] = jnp.dot(hid_t[...], saved[:, cols], preferred_element_type=F32).astype(BF16)
        first = pltpu.make_async_copy(in_buf.at[buf], grad_in.at[:, cols], sems.at[0, buf])
        first.start()
        total = jnp.dot(
            weighted_t[...],
            jnp.concatenate([ref[:, cols] for ref in rows_refs], axis=0),
            preferred_element_type=F32,
        )
        out_buf[buf] = total.astype(BF16)
        second = pltpu.make_async_copy(out_buf.at[buf], grad_out.at[:, cols], sems.at[1, buf])
        second.start()
        copies += [first, second]
    for copy in copies[2 * max(steps - 2, 0) :]:
        copy.wait()


def weight_grads(slots, saved, rows_list, weighted_list, hid_list):
    ticks = len(rows_list)
    tokens, width = rows_list[0].shape
    devices, rows, units = hid_list[0].shape
    tile = column_tile(width)
    out = jax.ShapeDtypeStruct((units, width), BF16)
    return pl.pallas_call(
        functools.partial(grads_kernel, ticks),
        in_specs=[SMEM] + [VMEM] * (3 * ticks + 1),
        out_specs=[ANY, ANY],
        out_shape=[out, out],
        scratch_shapes=[
            pltpu.VMEM((devices * ticks, rows, units), BF16),
            pltpu.VMEM((units, ticks * tokens), BF16),
            pltpu.VMEM((units, ticks * tokens), BF16),
            pltpu.VMEM((2, units, tile), BF16),
            pltpu.VMEM((2, units, tile), BF16),
            pltpu.SemaphoreType.DMA((2, 2)),
        ],
        compiler_params=PARAMS,
        cost_estimate=pl.CostEstimate(
            flops=4 * ticks * tokens * units * width, bytes_accessed=4 * units * width, transcendentals=0
        ),
        name="weight_grads",
    )(slots, saved, *rows_list, *weighted_list, *hid_list)


def hand_on_kernel(count, scalars, *refs):
    sums = refs[:count]
    base, loss, done_ref, next_ref, pick_ref = refs[count:]
    above, mine, top = scalars[0], scalars[1], scalars[2]
    total = sums[0][...].astype(F32)
    for ref in sums[1:]:
        total = total + ref[...].astype(F32)
    done = (base[above].astype(F32) + total).astype(BF16)
    done_ref[...] = done
    for b in range(base.shape[0]):
        from_above = jnp.where(above == b, done, base[b])
        next_ref[b] = jnp.where(top == 1, loss[b], from_above)
    pick_ref[...] = next_ref[mine]


def hand_on(sums, base, loss, scalars):
    rows, width = sums[0].shape
    chunk = jax.ShapeDtypeStruct((rows, width), BF16)
    return pl.pallas_call(
        functools.partial(hand_on_kernel, len(sums)),
        in_specs=[SMEM] + [VMEM] * (len(sums) + 2),
        out_specs=[VMEM] * 3,
        out_shape=[chunk, jax.ShapeDtypeStruct(base.shape, BF16), chunk],
        compiler_params=PARAMS,
        name="hand_on",
    )(scalars, *sums, base, loss)


def finish_kernel(count, ticks, picks, *refs):
    sums = refs[:count]
    incoming = refs[count : count + ticks]
    done = refs[count + ticks : count + 2 * ticks - 1]
    passed = refs[-1]
    for t in range(ticks):
        for b in range(passed.shape[1]):
            passed[t, b] = incoming[t][b]
        if t < ticks - 1:
            passed[t, picks[t]] = done[t][...]
    total = sums[0][...].astype(F32)
    for ref in sums[1:]:
        total = total + ref[...].astype(F32)
    last = picks[ticks - 1]
    passed[ticks - 1, last] = (incoming[ticks - 1][last].astype(F32) + total).astype(BF16)


def finish(sums, incoming, done, picks):
    ticks = len(incoming)
    return pl.pallas_call(
        functools.partial(finish_kernel, len(sums), ticks),
        in_specs=[SMEM] + [VMEM] * (len(sums) + 2 * ticks - 1),
        out_specs=VMEM,
        out_shape=jax.ShapeDtypeStruct((ticks,) + incoming[0].shape, BF16),
        compiler_params=PARAMS,
        name="finish",
    )(picks, *sums, *incoming, *done)


def per_device(
    sections, devices, w_in, w_out, input_stash, hidden_stash, gate_stash, block_pick, slot_order, arriving, loss_grads
):
    ticks = slot_order.shape[1]
    rows = arriving.shape[2]
    inner = 2 ** ((devices.bit_length() - 1) // 2)
    outer = devices // inner
    me = lax.axis_index("dp")
    top = (lax.axis_index("section") == sections - 1).astype(jnp.int32)

    def swap(value, step):
        return lax.ppermute(value, "dp", [(i, i ^ step) for i in range(devices)])

    def shift(value, distance, step=0):
        route = [
            (s * devices + i, (s + distance) % sections * devices + (i ^ step))
            for s in range(sections)
            for i in range(devices)
        ]
        return lax.ppermute(value, ("section", "dp"), route)

    def gather(own):
        chunks = {0: own}
        for a in range(outer - 1, 0, -1):
            chunks[a * inner] = swap(own, a * inner)
        for a in range(outer):
            for b in range(1, inner):
                chunks[a * inner + b] = swap(chunks[a * inner], b)
        return [chunks[k] for k in range(devices)]

    def reduce_inner(parts):
        sums = {}
        for a in range(outer - 1, -1, -1):
            got = [swap(parts[a * inner + b], b).astype(F32) for b in range(1, inner)]
            sums[a] = sum(got, parts[a * inner].astype(F32)).astype(BF16)
        return sums

    slots = slot_order[0]
    picks = jnp.stack(
        [
            sum(jnp.where(slots[t] == p, block_pick[0, p], 0) for p in range(ticks))
            for t in range(ticks)
        ]
    )
    own = sum(
        jnp.where(picks[0] == b, arriving[0, b], jnp.zeros((), BF16)) for b in range(arriving.shape[1])
    )
    hidden = hidden_stash[0].reshape(ticks, devices, rows, -1)
    gates = gate_stash[0].reshape(ticks, devices, rows, 1)

    z_groups = [[a * inner + b for a in range(outer)] for b in range(inner)]
    x_groups = [[a * inner + b for b in range(inner)] for a in range(outer)]
    saved = lax.all_gather(input_stash[0], "dp", axis_index_groups=z_groups)
    saved = lax.all_gather(saved, "dp", axis_index_groups=x_groups)
    saved = saved.reshape(ticks * devices * rows, -1)

    above_picks = shift(picks, -1)
    incoming = [arriving[0]]
    done = []
    gate_parts = []
    rows_list, weighted_list, hid_list = [], [], []
    for t in range(ticks):
        chunks = gather(own)
        results = expert(
            chunks, w_out[0], w_in[0], hidden, gates, jnp.stack([me.astype(jnp.int32), slots[t]]), inner
        )
        parts = results[:devices]
        rows_list.append(results[devices])
        weighted_list.append(results[devices + 1])
        hid_list.append(results[devices + 2])
        gate_parts.append(results[devices + 3])
        sums = reduce_inner(parts)
        if t < ticks - 1:
            base = shift(incoming[t], -1)
            sums = [shift(sums[a], -1, a * inner) for a in range(outer - 1, -1, -1)]
            above_done, following, own = hand_on(
                sums, base, loss_grads[t], jnp.stack([above_picks[t], picks[t + 1], top])
            )
            done.append(shift(above_done, 1))
            incoming.append(following)
        else:
            sums = [swap(sums[a], a * inner) for a in range(outer - 1, 0, -1)] + [sums[0]]
    grad_in, grad_out = weight_grads(slot_order, saved, rows_list, weighted_list, hid_list)
    gate = jnp.stack(gate_parts).reshape(ticks, devices * rows)
    step = 1
    while step < devices:
        gate = gate + swap(gate, step)
        step *= 2
    gate = jnp.stack([sum(jnp.where(slots[t] == p, gate[t], 0.0) for t in range(ticks)) for p in range(ticks)])
    passed = finish(sums, incoming, done, picks)
    return passed[None], grad_in[None], grad_out[None], gate[None]


def solution(mesh):
    placed = (
        P("section", "dp", None),
        P("section", "dp", None),
        P("section", None, "dp", None),
        P("section", None, None, "dp"),
        P("section", None, None),
        P("section", None),
        P("section", None),
        P("section", None, "dp", None),
        P(None, None, "dp", None),
    )
    return jax.shard_map(
        functools.partial(per_device, mesh.shape["section"], mesh.shape["dp"]),
        mesh=mesh,
        in_specs=placed,
        out_specs=(
            P("section", None, None, "dp", None),
            P("section", "dp", None),
            P("section", "dp", None),
            P("section", None, None),
        ),
        check_vma=False,
    )
```

time: 344 us -> 193 us (0.56)
  waiting for transfers between devices: 244 us -> 94.7 us
  matrix products: 45.8 us -> 0 us
  starting transfers between devices: 1.54 us -> 35.5 us
  blocking collectives: 19.3 us -> 0 us
  Pallas kernels: 0 us -> 16.4 us
  local copies, waits for them, and re-layouts: 6.42 us -> 22.5 us
    reduce_scatter x2 -> x0, waiting for transfers between devices: 128 us -> none  [section_tick(): lax.psum_scatter(jnp.dot(hid_grad, in_weight, preferred_element_type=jnp....]
    all_gather x4 -> x2, waiting for transfers between devices: 115 us -> 41.3 us  [the longest x1 23.7 us: per_device(): saved = lax.all_gather(saved, 'dp', axis_index_groups=x_groups)]
    ppermute x1 -> x35, waiting for transfers between devices: 0.19 us -> 53.3 us  [the longest x28 45.4 us: swap(): return lax.ppermute(value, 'dp', [(i, i ^ step) for i in range(devices)])]
    dot_general x9 -> x0, matrix products: 45.8 us -> none  [the longest x2 15 us: weight_terms(): lax.dot_general(hid_grad, rows_input, contract, preferred_element_type=jn...]
    ppermute x1 -> x35, starting transfers between devices: 1.29 us -> 35.4 us  [the longest x28 31.6 us: swap(): return lax.ppermute(value, 'dp', [(i, i ^ step) for i in range(devices)])]
    psum x1 -> x0, blocking collectives: 19.3 us -> none  [section_tick(): gate_part = lax.psum(gate_part, 'dp')]
    unnamed x18 -> x34, local copies, waits for them, and re-layouts: 0.04 us -> 18.9 us
    pallas_call x0 -> x5, Pallas kernels: none -> 16.4 us  [the longest x2 7.58 us: expert(): pl.pallas_call(functools.partial(expert_kernel, devices, inner), in_specs...]
  transfers between devices with their start and end apart: 7 -> 37, of which waited for: 7 -> 21; matrix products, arithmetic and copies ran while one was open for 12% -> 2% of each run, Pallas kernels for 0% -> 1%
where the time goes in v1:
time: 193 us; the launch traced here: 192 us
  waiting for transfers between devices  94.7 us (49%)
  starting transfers between devices  35.5 us (18%)
  local copies, waits for them, and re-layouts  22.5 us (12%)
  between operations  19.6 us (10%)
  Pallas kernels  16.4 us (8%)
  other arithmetic  3.67 us (2%)
    ppermute x28, waiting for transfers between devices, swap(): return lax.ppermute(value, 'dp', [(i, i ^ step) for i in range(devices)])  45.4 us
    ppermute x28, starting transfers between devices, swap(): return lax.ppermute(value, 'dp', [(i, i ^ step) for i in range(devices)])  31.6 us
    all_gather x1, waiting for transfers between devices, per_device(): saved = lax.all_gather(saved, 'dp', axis_index_groups=x_groups)  23.7 us
    unnamed x34, local copies, waits for them, and re-layouts  18.9 us
    all_gather x1, waiting for transfers between devices, per_device(): saved = lax.all_gather(input_stash[0], 'dp', axis_index_groups=z_groups)  17.6 us
    ppermute x7, waiting for transfers between devices, shift(): return lax.ppermute(value, ('section', 'dp'), route)  7.88 us
    pallas_call x2, Pallas kernels, expert(): pl.pallas_call(functools.partial(expert_kernel, devices, inner), in_specs...  7.58 us
    pallas_call x1, Pallas kernels, weight_grads(): pl.pallas_call(functools.partial(grads_kernel, ticks), in_specs=[SMEM] +...  6.66 us
  transfers between devices with their start and end apart: 37, of which 21 were waited for; matrix products, arithmetic and copies ran while one was open for 2% of the time, Pallas kernels for 1%

profile of v1, /device:TPU:0, one launch (start us, length us, event | category | flops | bytes accessed | tf_op | source)
XLA Modules:
  0.0 192.4 jit_solution(14420896127889760917)
XLA Ops:
  7.2 1.3 fusion.4
  8.5 1.3 fusion.3
  12.5 1.0 add_bitcast_fusion.refs_0_
  13.5 5.1 %collective-permute-start.6 = (bf16[16,4096]{1,0:T(8,128)(2,1)S(1)}, bf16[16,4096]{1,0:T(8,128)(2,1)S(1)}, u32[]{:S(2)}, u32[]{:S(2)}) collective-permute-start(bf16[16,4096]{1,0:T(8,128)(2,1)S(1)} %add_bitcast_fusion.refs_0_), channel_id=1, source_target_pairs={{0,6},{1,7},{2,4},{3,5},{4,2},{5,3},{6,0},{7,1},{8,14},{9,15},{10,... | collective-permute-start | bytes 393224 | tf_op jit(solution)/shard_map/ppermute | solution.py:216
  19.2 1.6 collective-permute-start.1
  20.9 2.1 %collective-permute-done.6.refs_6_ = bf16[16,4096]{1,0:T(8,128)(2,1)S(1)} collective-permute-done((bf16[16,4096]{1,0:T(8,128)(2,1)S(1)}, bf16[16,4096]{1,0:T(8,128)(2,1)S(1)}, u32[]{:S(2)}, u32[]{:S(2)}) %collective-permute-start.6) | collective-permute-done | bytes 131104 | tf_op jit(solution)/shard_map/ppermute | solution.py:216
  23.0 1.7 collective-permute-start.7
  24.7 5.0 %collective-permute-done.4.refs_4_ = bf16[16,4096]{1,0:T(8,128)(2,1)S(1)} collective-permute-done((bf16[16,4096]{1,0:T(8,128)(2,1)S(1)}, bf16[16,4096]{1,0:T(8,128)(2,1)S(1)}, u32[]{:S(2)}, u32[]{:S(2)}) %collective-permute-start.4) | collective-permute-done | bytes 131104 | tf_op jit(solution)/shard_map/ppermute | solution.py:216
  29.7 1.5 collective-permute-start.5
  33.3 2.3 %collective-permute-done.5.refs_5_ = bf16[16,4096]{1,0:T(8,128)(2,1)S(1)} collective-permute-done((bf16[16,4096]{1,0:T(8,128)(2,1)S(1)}, bf16[16,4096]{1,0:T(8,128)(2,1)S(1)}, u32[]{:S(2)}, u32[]{:S(2)}) %collective-permute-start.5) | collective-permute-done | bytes 131104 | tf_op jit(solution)/shard_map/ppermute | solution.py:216
  35.6 1.4 collective-permute-done.3.refs_3_
  37.0 2.5 %copy-done = bf16[1,640,4096]{2,1,0:T(8,128)(2,1)S(1)} copy-done((bf16[1,640,4096]{2,1,0:T(8,128)(2,1)S(1)}, bf16[1,640,4096]{2,1,0:T(8,128)(2,1)}, u32[]{:S(2)}) %copy-start) | copy-done | bytes 5242904
  39.5 2.5 %copy-done.2 = bf16[1,640,4096]{2,1,0:T(8,128)(2,1)S(1)} copy-done((bf16[1,640,4096]{2,1,0:T(8,128)(2,1)S(1)}, bf16[1,640,4096]{2,1,0:T(8,128)(2,1)}, u32[]{:S(2)}) %copy-start.2) | copy-done | bytes 5242904
  42.0 1.0 copy-done.4
  43.0 3.8 %expert_tick.2 = (bf16[16,4096]{1,0:T(8,128)(2,1)S(1)}, bf16[16,4096]{1,0:T(8,128)(2,1)S(1)}, bf16[16,4096]{1,0:T(8,128)(2,1)S(1)}, bf16[16,4096]{1,0:T(8,128)(2...) custom-call(s32[2]{0:T(128)S(1)} %pad_add_fusion.3.scalars, ...), custom_call_target="tpu_custom_call" | custom-call | flops 1342177280 | bytes 2097152 | tf_op jit(solution)/shard_map/expert_tick/pallas_call | solution.py:65
  47.8 1.5 collective-permute-start.8
  52.0 1.6 collective-permute-start.16
  54.1 1.5 collective-permute-start.12
  56.2 3.8 %collective-permute-done.10 = bf16[16,4096]{1,0:T(8,128)(2,1)S(1)} collective-permute-done((bf16[16,4096]{1,0:T(8,128)(2,1)S(1)}, bf16[16,4096]{1,0:T(8,128)(2,1)S(1)}, u32[]{:S(2)}, u32[]{:S(2)}) %collective-permute-start.10) | collective-permute-done | bytes 131104 | tf_op jit(solution)/shard_map/ppermute | solution.py:216
  60.1 2.1 %collective-permute-done.12 = bf16[16,4096]{1,0:T(8,128)(2,1)S(1)} collective-permute-done((bf16[16,4096]{1,0:T(8,128)(2,1)S(1)}, bf16[16,4096]{1,0:T(8,128)(2,1)S(1)}, u32[]{:S(2)}, u32[]{:S(2)}) %collective-permute-start.12) | collective-permute-done | bytes 131104 | tf_op jit(solution)/shard_map/ppermute | solution.py:216
  62.2 1.4 collective-permute-done.14
  63.6 1.8 collective-permute-start.13
  65.9 1.6 collective-permute-done.9.refs_0_
  67.5 6.3 %collective-permute-done.11.refs_1_ = bf16[16,4096]{1,0:T(8,128)(2,1)S(1)} collective-permute-done((bf16[16,4096]{1,0:T(8,128)(2,1)S(1)}, bf16[16,4096]{1,0:T(8,128)(2,1)S(1)}, u32[]{:S(2)}, u32[]{:S(2)}) %collective-permute-start.11) | collective-permute-done | bytes 131104 | tf_op jit(solution)/shard_map/ppermute | solution.py:224
  74.5 2.4 %collective-permute-start.22 = (bf16[16,4096]{1,0:T(8,128)(2,1)S(1)}, bf16[16,4096]{1,0:T(8,128)(2,1)S(1)}, u32[]{:S(2)}, u32[]{:S(2)}) collective-permute-start(bf16[16,4096]{1,0:T(8,128)(2,1)S(1)} %get-tuple-element.41.refs_0_), channel_id=1, source_target_pairs={{0,6},{1,7},{2,4},{3,5},{4,2},{5,3},{6,0},{7,1},{8,14},{9,15},{10,... | collective-permute-start | bytes 393224 | tf_op jit(solution)/shard_map/ppermute | solution.py:216
  76.9 2.1 %collective-permute-start.18 = (bf16[16,4096]{1,0:T(8,128)(2,1)S(1)}, bf16[16,4096]{1,0:T(8,128)(2,1)S(1)}, u32[]{:S(2)}, u32[]{:S(2)}) collective-permute-start(bf16[16,4096]{1,0:T(8,128)(2,1)S(1)} %get-tuple-element.41.refs_0_), channel_id=1, source_target_pairs={{0,2},{1,3},{2,0},{3,1},{4,6},{5,7},{6,4},{7,5},{8,10},{9,11},{10,... | collective-permute-start | bytes 393224 | tf_op jit(solution)/shard_map/ppermute | solution.py:216
  79.5 3.3 %collective-permute-done.22.refs_6_ = bf16[16,4096]{1,0:T(8,128)(2,1)S(1)} collective-permute-done((bf16[16,4096]{1,0:T(8,128)(2,1)S(1)}, bf16[16,4096]{1,0:T(8,128)(2,1)S(1)}, u32[]{:S(2)}, u32[]{:S(2)}) %collective-permute-start.22) | collective-permute-done | bytes 131104 | tf_op jit(solution)/shard_map/ppermute | solution.py:216
  83.3 4.1 %collective-permute-done.20.refs_4_ = bf16[16,4096]{1,0:T(8,128)(2,1)S(1)} collective-permute-done((bf16[16,4096]{1,0:T(8,128)(2,1)S(1)}, bf16[16,4096]{1,0:T(8,128)(2,1)S(1)}, u32[]{:S(2)}, u32[]{:S(2)}) %collective-permute-start.20) | collective-permute-done | bytes 131104 | tf_op jit(solution)/shard_map/ppermute | solution.py:216
  88.0 1.5 collective-permute-start.19
  90.4 3.3 %collective-permute-done.21.refs_5_ = bf16[16,4096]{1,0:T(8,128)(2,1)S(1)} collective-permute-done((bf16[16,4096]{1,0:T(8,128)(2,1)S(1)}, bf16[16,4096]{1,0:T(8,128)(2,1)S(1)}, u32[]{:S(2)}, u32[]{:S(2)}) %collective-permute-start.21) | collective-permute-done | bytes 131104 | tf_op jit(solution)/shard_map/ppermute | solution.py:216
  93.7 1.4 collective-permute-done.19.refs_3_
  95.1 2.5 %copy-done.1 = bf16[1,640,4096]{2,1,0:T(8,128)(2,1)S(1)} copy-done((bf16[1,640,4096]{2,1,0:T(8,128)(2,1)S(1)}, bf16[1,640,4096]{2,1,0:T(8,128)(2,1)}, u32[]{:S(2)}) %copy-start.1) | copy-done | bytes 5242904
  97.6 2.5 %copy-done.3 = bf16[1,640,4096]{2,1,0:T(8,128)(2,1)S(1)} copy-done((bf16[1,640,4096]{2,1,0:T(8,128)(2,1)S(1)}, bf16[1,640,4096]{2,1,0:T(8,128)(2,1)}, u32[]{:S(2)}) %copy-start.3) | copy-done | bytes 5242904
  100.1 3.8 %expert_tick.3 = (bf16[16,4096]{1,0:T(8,128)(2,1)S(1)}, bf16[16,4096]{1,0:T(8,128)(2,1)S(1)}, bf16[16,4096]{1,0:T(8,128)(2,1)S(1)}, bf16[16,4096]{1,0:T(8,128)(2...) custom-call(s32[2]{0:T(128)S(1)} %pad_add_fusion.1.scalars, ...), custom_call_target="tpu_custom_call" | custom-call | flops 1342177280 | bytes 2097152 | tf_op jit(solution)/shard_map/expert_tick/pallas_call | solution.py:65
  107.6 3.0 %collective-permute-done.32 = f32[2,128]{1,0:T(2,128)S(1)} collective-permute-done((f32[2,128]{1,0:T(2,128)S(1)}, f32[2,128]{1,0:T(2,128)S(1)}, u32[]{:S(2)}, u32[]{:S(2)}) %collective-permute-start.32) | collective-permute-done | bytes 1056 | tf_op jit(solution)/shard_map/ppermute | solution.py:216
  111.0 3.3 %collective-permute-done.33 = f32[2,128]{1,0:T(2,128)S(1)} collective-permute-done((f32[2,128]{1,0:T(2,128)S(1)}, f32[2,128]{1,0:T(2,128)S(1)}, u32[]{:S(2)}, u32[]{:S(2)}) %collective-permute-start.33) | collective-permute-done | bytes 1056 | tf_op jit(solution)/shard_map/ppermute | solution.py:216
  115.3 1.5 collective-permute-start.26
  117.3 1.6 collective-permute-done.34
  120.9 2.8 %collective-permute-start.25 = (bf16[16,4096]{1,0:T(8,128)(2,1)S(1)}, bf16[16,4096]{1,0:T(8,128)(2,1)S(1)}, u32[]{:S(2)}, u32[]{:S(2)}) collective-permute-start(bf16[16,4096]{1,0:T(8,128)(2,1)S(1)} %add_convert_fusion.3), channel_id=1, source_target_pairs={{0,6},{1,7},{2,4},{3,5},{4,2},{5,3},{6,0},{7,1},{8,14},{9,15},{10,... | collective-permute-start | bytes 393224 | tf_op jit(solution)/shard_map/ppermute | solution.py:216
  123.7 17.6 %all-gather.4.cloned.1.call-done = bf16[4,2,16,4096]{3,2,1,0:T(8,128)(2,1)} async-done(((bf16[1,2,16,4096]{3,2,1,0:T(8,128)(2,1)}), bf16[4,2,16,4096]{3,2,1,0:T(8,128)(2,1)}) %all-gather.4.cloned.1.call-update) | async-done | bytes 1048592 | tf_op jit(solution)/shard_map/all_gather | solution.py:257
  141.5 1.6 collective-permute-start.29
  143.2 5.9 %collective-permute-done.27.refs_1_ = bf16[16,4096]{1,0:T(8,128)(2,1)S(1)} collective-permute-done((bf16[16,4096]{1,0:T(8,128)(2,1)S(1)}, bf16[16,4096]{1,0:T(8,128)(2,1)S(1)}, u32[]{:S(2)}, u32[]{:S(2)}) %collective-permute-start.27) | collective-permute-done | bytes 131104 | tf_op jit(solution)/shard_map/ppermute | solution.py:216
  149.6 1.5 finish.1
  151.1 23.7 %all-gather.6.cloned.1.call-done = bf16[8,2,16,4096]{3,2,1,0:T(8,128)(2,1)} async-done(((bf16[4,2,16,4096]{3,2,1,0:T(8,128)(2,1)}), bf16[8,2,16,4096]{3,2,1,0:T(8,128)(2,1)}) %all-gather.6.cloned.1.call-update) | async-done | bytes 2097168 | tf_op jit(solution)/shard_map/all_gather | solution.py:258
  174.8 1.6 copy-done.9
  176.4 1.2 copy-done.11
  177.6 1.2 copy-done.13
  178.9 6.7 %weight_grads.1 = (bf16[640,4096]{1,0:T(8,128)(2,1)}, bf16[640,4096]{1,0:T(8,128)(2,1)}) custom-call(s32[1,2]{1,0:T(1,128)S(1)} %copy-done.8, bf16[256,4096]{1,0:T(8,128)(2,1)S(1)} %bitcast.35, bf16[128,4096]{1,0:T(8,128)(2,1)S(1)} %copy-done.11, bf16[128,4096]{1,0:T(8,128)(2,1)S(1)} %copy-done.13, bf16[128,640]{1,0:T(8,128)(2,1)S(1)} %get-tuple-element.54.refs_2_, ...), custom_call_target="tpu_custom_call" | custom-call | flops 2684354560 | bytes 10485760 | tf_op jit(solution)/shard_map/weight_grads/pallas_call | solution.py:127
  (93 shorter events, 17.1 us)
Async XLA Ops:
  7.2 134.1 %all-gather.4.cloned.1.call-start = ((), (), s32[]{:S(2)}) async-start(), calls=%async_computation | async-start | bytes 1310720 | tf_op jit(solution)/shard_map/all_gather | solution.py:257
  13.5 9.5 %collective-permute-start.6 = (bf16[16,4096]{1,0:T(8,128)(2,1)S(1)}, bf16[16,4096]{1,0:T(8,128)(2,1)S(1)}, u32[]{:S(2)}, u32[]{:S(2)}) collective-permute-start(bf16[16,4096]{1,0:T(8,128)(2,1)S(1)} %add_bitcast_fusion.refs_0_), channel_id=1, source_target_pairs={{0,6},{1,7},{2,4},{3,5},{4,2},{5,3},{6,0},{7,1},{8,14},{9,15},{10,... | collective-permute-start | bytes 393224 | tf_op jit(solution)/shard_map/ppermute | solution.py:216
  18.6 11.1 %collective-permute-start.4 = (bf16[16,4096]{1,0:T(8,128)(2,1)S(1)}, bf16[16,4096]{1,0:T(8,128)(2,1)S(1)}, u32[]{:S(2)}, u32[]{:S(2)}) collective-permute-start(bf16[16,4096]{1,0:T(8,128)(2,1)S(1)} %add_bitcast_fusion.refs_0_), channel_id=1, source_target_pairs={{0,4},{1,5},{2,6},{3,7},{4,0},{5,1},{6,2},{7,3},{8,12},{9,13},{10,... | collective-permute-start | bytes 393224 | tf_op jit(solution)/shard_map/ppermute | solution.py:216
  18.6 12.6 %collective-permute-start.2 = (bf16[16,4096]{1,0:T(8,128)(2,1)S(1)}, bf16[16,4096]{1,0:T(8,128)(2,1)S(1)}, u32[]{:S(2)}, u32[]{:S(2)}) collective-permute-start(bf16[16,4096]{1,0:T(8,128)(2,1)S(1)} %add_bitcast_fusion.refs_0_), channel_id=1, source_target_pairs={{0,2},{1,3},{2,0},{3,1},{4,6},{5,7},{6,4},{7,5},{8,10},{9,11},{10,... | collective-permute-start | bytes 393224 | tf_op jit(solution)/shard_map/ppermute | solution.py:216
  19.2 14.1 %collective-permute-start.1 = (bf16[16,4096]{1,0:T(8,128)(2,1)S(1)}, bf16[16,4096]{1,0:T(8,128)(2,1)S(1)}, u32[]{:S(2)}, u32[]{:S(2)}) collective-permute-start(bf16[16,4096]{1,0:T(8,128)(2,1)S(1)} %add_bitcast_fusion.refs_0_), channel_id=1, source_target_pairs={{0,1},{1,0},{2,3},{3,2},{4,5},{5,4},{6,7},{7,6},{8,9},{9,8},{10,11... | collective-permute-start | bytes 393224 | tf_op jit(solution)/shard_map/ppermute | solution.py:216
  23.0 10.3 %collective-permute-start.7 = (bf16[16,4096]{1,0:T(8,128)(2,1)S(1)}, bf16[16,4096]{1,0:T(8,128)(2,1)S(1)}, u32[]{:S(2)}, u32[]{:S(2)}) collective-permute-start(bf16[16,4096]{1,0:T(8,128)(2,1)S(1)} %collective-permute-done.6.refs_6_), channel_id=1, source_target_pairs={{0,1},{1,0},{2,3},{3,2},{4,5},{5,4},{6,7},{7,6},{8,9},{9,8},{10,11... | collective-permute-start | bytes 393224 | tf_op jit(solution)/shard_map/ppermute | solution.py:216
  29.7 6.0 %collective-permute-start.5 = (bf16[16,4096]{1,0:T(8,128)(2,1)S(1)}, bf16[16,4096]{1,0:T(8,128)(2,1)S(1)}, u32[]{:S(2)}, u32[]{:S(2)}) collective-permute-start(bf16[16,4096]{1,0:T(8,128)(2,1)S(1)} %collective-permute-done.4.refs_4_), channel_id=1, source_target_pairs={{0,1},{1,0},{2,3},{3,2},{4,5},{5,4},{6,7},{7,6},{8,9},{9,8},{10,11... | collective-permute-start | bytes 393224 | tf_op jit(solution)/shard_map/ppermute | solution.py:216
  31.2 5.9 %collective-permute-start.3 = (bf16[16,4096]{1,0:T(8,128)(2,1)S(1)}, bf16[16,4096]{1,0:T(8,128)(2,1)S(1)}, u32[]{:S(2)}, u32[]{:S(2)}) collective-permute-start(bf16[16,4096]{1,0:T(8,128)(2,1)S(1)} %collective-permute-done.2.refs_2_), channel_id=1, source_target_pairs={{0,1},{1,0},{2,3},{3,2},{4,5},{5,4},{6,7},{7,6},{8,9},{9,8},{10,11... | collective-permute-start | bytes 393224 | tf_op jit(solution)/shard_map/ppermute | solution.py:216
  37.0 2.5 %copy-start = (bf16[1,640,4096]{2,1,0:T(8,128)(2,1)S(1)}, bf16[1,640,4096]{2,1,0:T(8,128)(2,1)}, u32[]{:S(2)}) copy-start(bf16[1,640,4096]{2,1,0:T(8,128)(2,1)} %param.10) | copy-start | bytes 15728644
  39.5 2.5 %copy-start.2 = (bf16[1,640,4096]{2,1,0:T(8,128)(2,1)S(1)}, bf16[1,640,4096]{2,1,0:T(8,128)(2,1)}, u32[]{:S(2)}) copy-start(bf16[1,640,4096]{2,1,0:T(8,128)(2,1)} %param.9) | copy-start | bytes 15728644
  43.0 9.0 %copy-start.6 = (bf16[1,2,16,4096]{3,2,1,0:T(8,128)(2,1)S(1)}, bf16[1,2,16,4096]{3,2,1,0:T(8,128)(2,1)}, u32[]{:S(2)}) copy-start(bf16[1,2,16,4096]{3,2,1,0:T(8,128)(2,1)} %param.16) | copy-start | bytes 786436
  43.0 30.8 %copy-start.7 = (bf16[1,2,16,4096]{3,2,1,0:T(8,128)(2,1)S(1)}, bf16[1,2,16,4096]{3,2,1,0:T(8,128)(2,1)}, u32[]{:S(2)}) copy-start(bf16[1,2,16,4096]{3,2,1,0:T(8,128)(2,1)} %param.17) | copy-start | bytes 786436
  43.0 52.1 %copy-start.5 = (bf16[1,2,128,640]{3,2,1,0:T(8,128)(2,1)S(1)}, bf16[1,2,128,640]{3,2,1,0:T(8,128)(2,1)}, u32[]{:S(2)}) copy-start(bf16[1,2,128,640]{3,2,1,0:T(8,128)(2,1)} %param.12) | copy-start | bytes 983044
  47.8 7.9 %collective-permute-start.8 = (bf16[16,4096]{1,0:T(8,128)(2,1)S(1)}, bf16[16,4096]{1,0:T(8,128)(2,1)S(1)}, u32[]{:S(2)}, u32[]{:S(2)}) collective-permute-start(bf16[16,4096]{1,0:T(8,128)(2,1)S(1)} %get-tuple-element.34), channel_id=1, source_target_pairs={{0,1},{1,0},{2,3},{3,2},{4,5},{5,4},{6,7},{7,6},{8,9},{9,8},{10,11... | collective-permute-start | bytes 393224 | tf_op jit(solution)/shard_map/ppermute | solution.py:216
  52.0 13.5 %collective-permute-start = (s32[2]{0:T(128)S(1)}, s32[2]{0:T(128)S(1)}, u32[]{:S(2)}, u32[]{:S(2)}) collective-permute-start(s32[2]{0:T(128)S(1)} %pad_add_fusion.picks), channel_id=1, source_target_pairs={{0,24},{1,25},{2,26},{3,27},{4,28},{5,29},{6,30},{7,31},{8,0},{9,1... | collective-permute-start | bytes 32 | tf_op jit(solution)/shard_map/ppermute | solution.py:224
  52.0 13.9 %collective-permute-start.16 = (bf16[2,16,4096]{2,1,0:T(8,128)(2,1)S(1)}, bf16[2,16,4096]{2,1,0:T(8,128)(2,1)S(1)}, u32[]{:S(2)}, u32[]{:S(2)}) collective-permute-start(bf16[2,16,4096]{2,1,0:T(8,128)(2,1)S(1)} %bitcast.32), channel_id=1, source_target_pairs={{0,24},{1,25},{2,26},{3,27},{4,28},{5,29},{6,30},{7,31},{8,0},{9,1... | collective-permute-start | bytes 786440 | tf_op jit(solution)/shard_map/ppermute | solution.py:224
  53.6 6.4 %collective-permute-start.10 = (bf16[16,4096]{1,0:T(8,128)(2,1)S(1)}, bf16[16,4096]{1,0:T(8,128)(2,1)S(1)}, u32[]{:S(2)}, u32[]{:S(2)}) collective-permute-start(bf16[16,4096]{1,0:T(8,128)(2,1)S(1)} %get-tuple-element.36), channel_id=1, source_target_pairs={{0,1},{1,0},{2,3},{3,2},{4,5},{5,4},{6,7},{7,6},{8,9},{9,8},{10,11... | collective-permute-start | bytes 393224 | tf_op jit(solution)/shard_map/ppermute | solution.py:216
  54.1 8.0 %collective-permute-start.12 = (bf16[16,4096]{1,0:T(8,128)(2,1)S(1)}, bf16[16,4096]{1,0:T(8,128)(2,1)S(1)}, u32[]{:S(2)}, u32[]{:S(2)}) collective-permute-start(bf16[16,4096]{1,0:T(8,128)(2,1)S(1)} %get-tuple-element.38), channel_id=1, source_target_pairs={{0,1},{1,0},{2,3},{3,2},{4,5},{5,4},{6,7},{7,6},{8,9},{9,8},{10,11... | collective-permute-start | bytes 393224 | tf_op jit(solution)/shard_map/ppermute | solution.py:216
  55.6 7.9 %collective-permute-start.14 = (bf16[16,4096]{1,0:T(8,128)(2,1)S(1)}, bf16[16,4096]{1,0:T(8,128)(2,1)S(1)}, u32[]{:S(2)}, u32[]{:S(2)}) collective-permute-start(bf16[16,4096]{1,0:T(8,128)(2,1)S(1)} %get-tuple-element.40), channel_id=1, source_target_pairs={{0,1},{1,0},{2,3},{3,2},{4,5},{5,4},{6,7},{7,6},{8,9},{9,8},{10,11... | collective-permute-start | bytes 393224 | tf_op jit(solution)/shard_map/ppermute | solution.py:216
  60.0 7.4 %collective-permute-start.9 = (bf16[16,4096]{1,0:T(8,128)(2,1)S(1)}, bf16[16,4096]{1,0:T(8,128)(2,1)S(1)}, u32[]{:S(2)}, u32[]{:S(2)}) collective-permute-start(bf16[16,4096]{1,0:T(8,128)(2,1)S(1)} %add_convert_fusion.7), channel_id=1, source_target_pairs={{0,30},{1,31},{2,28},{3,29},{4,26},{5,27},{6,24},{7,25},{8,6},{9,7... | collective-permute-start | bytes 393224 | tf_op jit(solution)/shard_map/ppermute | solution.py:224
  62.2 11.6 %collective-permute-start.11 = (bf16[16,4096]{1,0:T(8,128)(2,1)S(1)}, bf16[16,4096]{1,0:T(8,128)(2,1)S(1)}, u32[]{:S(2)}, u32[]{:S(2)}) collective-permute-start(bf16[16,4096]{1,0:T(8,128)(2,1)S(1)} %add_convert_fusion.6), channel_id=1, source_target_pairs={{0,28},{1,29},{2,30},{3,31},{4,24},{5,25},{6,26},{7,27},{8,4},{9,5... | collective-permute-start | bytes 393224 | tf_op jit(solution)/shard_map/ppermute | solution.py:224
  63.6 10.2 %collective-permute-start.13 = (bf16[16,4096]{1,0:T(8,128)(2,1)S(1)}, bf16[16,4096]{1,0:T(8,128)(2,1)S(1)}, u32[]{:S(2)}, u32[]{:S(2)}) collective-permute-start(bf16[16,4096]{1,0:T(8,128)(2,1)S(1)} %add_convert_fusion.5), channel_id=1, source_target_pairs={{0,26},{1,27},{2,24},{3,25},{4,30},{5,31},{6,28},{7,29},{8,2},{9,3... | collective-permute-start | bytes 393224 | tf_op jit(solution)/shard_map/ppermute | solution.py:224
  65.5 8.3 %collective-permute-start.15 = (bf16[16,4096]{1,0:T(8,128)(2,1)S(1)}, bf16[16,4096]{1,0:T(8,128)(2,1)S(1)}, u32[]{:S(2)}, u32[]{:S(2)}) collective-permute-start(bf16[16,4096]{1,0:T(8,128)(2,1)S(1)} %add_convert_fusion.4), channel_id=1, source_target_pairs={{0,24},{1,25},{2,26},{3,27},{4,28},{5,29},{6,30},{7,31},{8,0},{9,1... | collective-permute-start | bytes 393224 | tf_op jit(solution)/shard_map/ppermute | solution.py:224
  74.5 8.3 %collective-permute-start.22 = (bf16[16,4096]{1,0:T(8,128)(2,1)S(1)}, bf16[16,4096]{1,0:T(8,128)(2,1)S(1)}, u32[]{:S(2)}, u32[]{:S(2)}) collective-permute-start(bf16[16,4096]{1,0:T(8,128)(2,1)S(1)} %get-tuple-element.41.refs_0_), channel_id=1, source_target_pairs={{0,6},{1,7},{2,4},{3,5},{4,2},{5,3},{6,0},{7,1},{8,14},{9,15},{10,... | collective-permute-start | bytes 393224 | tf_op jit(solution)/shard_map/ppermute | solution.py:216
  76.8 10.6 %collective-permute-start.20 = (bf16[16,4096]{1,0:T(8,128)(2,1)S(1)}, bf16[16,4096]{1,0:T(8,128)(2,1)S(1)}, u32[]{:S(2)}, u32[]{:S(2)}) collective-permute-start(bf16[16,4096]{1,0:T(8,128)(2,1)S(1)} %get-tuple-element.41.refs_0_), channel_id=1, source_target_pairs={{0,4},{1,5},{2,6},{3,7},{4,0},{5,1},{6,2},{7,3},{8,12},{9,13},{10,... | collective-permute-start | bytes 393224 | tf_op jit(solution)/shard_map/ppermute | solution.py:216
  76.9 11.1 %collective-permute-start.18 = (bf16[16,4096]{1,0:T(8,128)(2,1)S(1)}, bf16[16,4096]{1,0:T(8,128)(2,1)S(1)}, u32[]{:S(2)}, u32[]{:S(2)}) collective-permute-start(bf16[16,4096]{1,0:T(8,128)(2,1)S(1)} %get-tuple-element.41.refs_0_), channel_id=1, source_target_pairs={{0,2},{1,3},{2,0},{3,1},{4,6},{5,7},{6,4},{7,5},{8,10},{9,11},{10,... | collective-permute-start | bytes 393224 | tf_op jit(solution)/shard_map/ppermute | solution.py:216
  78.9 11.5 %collective-permute-start.17 = (bf16[16,4096]{1,0:T(8,128)(2,1)S(1)}, bf16[16,4096]{1,0:T(8,128)(2,1)S(1)}, u32[]{:S(2)}, u32[]{:S(2)}) collective-permute-start(bf16[16,4096]{1,0:T(8,128)(2,1)S(1)} %get-tuple-element.41.refs_0_), channel_id=1, source_target_pairs={{0,1},{1,0},{2,3},{3,2},{4,5},{5,4},{6,7},{7,6},{8,9},{9,8},{10,11... | collective-permute-start | bytes 393224 | tf_op jit(solution)/shard_map/ppermute | solution.py:216
  82.8 7.6 %collective-permute-start.23 = (bf16[16,4096]{1,0:T(8,128)(2,1)S(1)}, bf16[16,4096]{1,0:T(8,128)(2,1)S(1)}, u32[]{:S(2)}, u32[]{:S(2)}) collective-permute-start(bf16[16,4096]{1,0:T(8,128)(2,1)S(1)} %collective-permute-done.22.refs_6_), channel_id=1, source_target_pairs={{0,1},{1,0},{2,3},{3,2},{4,5},{5,4},{6,7},{7,6},{8,9},{9,8},{10,11... | collective-permute-start | bytes 393224 | tf_op jit(solution)/shard_map/ppermute | solution.py:216
  87.5 6.2 %collective-permute-start.21 = (bf16[16,4096]{1,0:T(8,128)(2,1)S(1)}, bf16[16,4096]{1,0:T(8,128)(2,1)S(1)}, u32[]{:S(2)}, u32[]{:S(2)}) collective-permute-start(bf16[16,4096]{1,0:T(8,128)(2,1)S(1)} %collective-permute-done.20.refs_4_), channel_id=1, source_target_pairs={{0,1},{1,0},{2,3},{3,2},{4,5},{5,4},{6,7},{7,6},{8,9},{9,8},{10,11... | collective-permute-start | bytes 393224 | tf_op jit(solution)/shard_map/ppermute | solution.py:216
  88.0 7.1 %collective-permute-start.19 = (bf16[16,4096]{1,0:T(8,128)(2,1)S(1)}, bf16[16,4096]{1,0:T(8,128)(2,1)S(1)}, u32[]{:S(2)}, u32[]{:S(2)}) collective-permute-start(bf16[16,4096]{1,0:T(8,128)(2,1)S(1)} %collective-permute-done.18.refs_2_), channel_id=1, source_target_pairs={{0,1},{1,0},{2,3},{3,2},{4,5},{5,4},{6,7},{7,6},{8,9},{9,8},{10,11... | collective-permute-start | bytes 393224 | tf_op jit(solution)/shard_map/ppermute | solution.py:216
  90.3 84.5 %copy-start.8 = (s32[1,2]{1,0:T(1,128)S(1)}, s32[1,2]{1,0:T(1,128)}, u32[]{:S(2)}) copy-start(s32[1,2]{1,0:T(1,128)} %slots.1) | copy-start | bytes 28
  95.1 2.5 %copy-start.1 = (bf16[1,640,4096]{2,1,0:T(8,128)(2,1)S(1)}, bf16[1,640,4096]{2,1,0:T(8,128)(2,1)}, u32[]{:S(2)}) copy-start(bf16[1,640,4096]{2,1,0:T(8,128)(2,1)} %param.10) | copy-start | bytes 15728644
  97.6 2.5 %copy-start.3 = (bf16[1,640,4096]{2,1,0:T(8,128)(2,1)S(1)}, bf16[1,640,4096]{2,1,0:T(8,128)(2,1)}, u32[]{:S(2)}) copy-start(bf16[1,640,4096]{2,1,0:T(8,128)(2,1)} %param.9) | copy-start | bytes 15728644
  107.0 3.6 %collective-permute-start.32 = (f32[2,128]{1,0:T(2,128)S(1)}, f32[2,128]{1,0:T(2,128)S(1)}, u32[]{:S(2)}, u32[]{:S(2)}) collective-permute-start(f32[2,128]{1,0:T(2,128)S(1)} %pad_maximum_fusion), channel_id=1, source_target_pairs={{0,1},{1,0},{2,3},{3,2},{4,5},{5,4},{6,7},{7,6},{8,9},{9,8},{10,11... | collective-permute-start | bytes 3080 | tf_op jit(solution)/shard_map/ppermute | solution.py:216
  107.6 67.2 %all-gather.6.cloned.1.call-start = ((), (), s32[]{:S(2)}) async-start(), calls=%async_computation.1 | async-start | bytes 3145728 | tf_op jit(solution)/shard_map/all_gather | solution.py:258
  110.6 3.6 %collective-permute-start.33 = (f32[2,128]{1,0:T(2,128)S(1)}, f32[2,128]{1,0:T(2,128)S(1)}, u32[]{:S(2)}, u32[]{:S(2)}) collective-permute-start(f32[2,128]{1,0:T(2,128)S(1)} %fusion.2), channel_id=1, source_target_pairs={{0,2},{1,3},{2,0},{3,1},{4,6},{5,7},{6,4},{7,5},{8,10},{9,11},{10,... | collective-permute-start | bytes 3080 | tf_op jit(solution)/shard_map/ppermute | solution.py:216
  114.3 4.6 %collective-permute-start.34 = (f32[2,128]{1,0:T(2,128)S(1)}, f32[2,128]{1,0:T(2,128)S(1)}, u32[]{:S(2)}, u32[]{:S(2)}) collective-permute-start(f32[2,128]{1,0:T(2,128)S(1)} %fusion.5), channel_id=1, source_target_pairs={{0,4},{1,5},{2,6},{3,7},{4,0},{5,1},{6,2},{7,3},{8,12},{9,13},{10,... | collective-permute-start | bytes 3080 | tf_op jit(solution)/shard_map/ppermute | solution.py:216
  114.7 28.5 %collective-permute-start.31 = (bf16[16,4096]{1,0:T(8,128)(2,1)S(1)}, bf16[16,4096]{1,0:T(8,128)(2,1)S(1)}, u32[]{:S(2)}, u32[]{:S(2)}) collective-permute-start(bf16[16,4096]{1,0:T(8,128)(2,1)S(1)} %get-tuple-element.51), channel_id=1, source_target_pairs={{0,8},{1,9},{2,10},{3,11},{4,12},{5,13},{6,14},{7,15},{8,16},{9,17... | collective-permute-start | bytes 393224 | tf_op jit(solution)/shard_map/ppermute | solution.py:224
  114.7 6.1 %collective-permute-start.24 = (bf16[16,4096]{1,0:T(8,128)(2,1)}, bf16[16,4096]{1,0:T(8,128)(2,1)S(1)}, u32[]{:S(2)}, u32[]{:S(2)}) collective-permute-start(bf16[16,4096]{1,0:T(8,128)(2,1)} %copy-done.16), channel_id=1, source_target_pairs={{0,1},{1,0},{2,3},{3,2},{4,5},{5,4},{6,7},{7,6},{8,9},{9,8},{10,11... | collective-permute-start | bytes 393224 | tf_op jit(solution)/shard_map/ppermute | solution.py:216
  115.3 26.1 %collective-permute-start.26 = (bf16[16,4096]{1,0:T(8,128)(2,1)}, bf16[16,4096]{1,0:T(8,128)(2,1)S(1)}, u32[]{:S(2)}, u32[]{:S(2)}) collective-permute-start(bf16[16,4096]{1,0:T(8,128)(2,1)} %copy-done.15), channel_id=1, source_target_pairs={{0,1},{1,0},{2,3},{3,2},{4,5},{5,4},{6,7},{7,6},{8,9},{9,8},{10,11... | collective-permute-start | bytes 393224 | tf_op jit(solution)/shard_map/ppermute | solution.py:216
  116.8 24.7 %collective-permute-start.28 = (bf16[16,4096]{1,0:T(8,128)(2,1)}, bf16[16,4096]{1,0:T(8,128)(2,1)S(1)}, u32[]{:S(2)}, u32[]{:S(2)}) collective-permute-start(bf16[16,4096]{1,0:T(8,128)(2,1)} %copy-done.14), channel_id=1, source_target_pairs={{0,1},{1,0},{2,3},{3,2},{4,5},{5,4},{6,7},{7,6},{8,9},{9,8},{10,11... | collective-permute-start | bytes 393224 | tf_op jit(solution)/shard_map/ppermute | solution.py:216
  118.9 24.3 %collective-permute-start.30 = (bf16[16,4096]{1,0:T(8,128)(2,1)S(1)}, bf16[16,4096]{1,0:T(8,128)(2,1)S(1)}, u32[]{:S(2)}, u32[]{:S(2)}) collective-permute-start(bf16[16,4096]{1,0:T(8,128)(2,1)S(1)} %get-tuple-element.49), channel_id=1, source_target_pairs={{0,1},{1,0},{2,3},{3,2},{4,5},{5,4},{6,7},{7,6},{8,9},{9,8},{10,11... | collective-permute-start | bytes 393224 | tf_op jit(solution)/shard_map/ppermute | solution.py:216
  120.9 22.3 %collective-permute-start.25 = (bf16[16,4096]{1,0:T(8,128)(2,1)S(1)}, bf16[16,4096]{1,0:T(8,128)(2,1)S(1)}, u32[]{:S(2)}, u32[]{:S(2)}) collective-permute-start(bf16[16,4096]{1,0:T(8,128)(2,1)S(1)} %add_convert_fusion.3), channel_id=1, source_target_pairs={{0,6},{1,7},{2,4},{3,5},{4,2},{5,3},{6,0},{7,1},{8,14},{9,15},{10,... | collective-permute-start | bytes 393224 | tf_op jit(solution)/shard_map/ppermute | solution.py:216
  141.4 7.7 %collective-permute-start.27 = (bf16[16,4096]{1,0:T(8,128)(2,1)S(1)}, bf16[16,4096]{1,0:T(8,128)(2,1)S(1)}, u32[]{:S(2)}, u32[]{:S(2)}) collective-permute-start(bf16[16,4096]{1,0:T(8,128)(2,1)S(1)} %add_convert_fusion.2), channel_id=1, source_target_pairs={{0,4},{1,5},{2,6},{3,7},{4,0},{5,1},{6,2},{7,3},{8,12},{9,13},{10,... | collective-permute-start | bytes 393224 | tf_op jit(solution)/shard_map/ppermute | solution.py:216
  141.5 8.1 %collective-permute-start.29 = (bf16[16,4096]{1,0:T(8,128)(2,1)S(1)}, bf16[16,4096]{1,0:T(8,128)(2,1)S(1)}, u32[]{:S(2)}, u32[]{:S(2)}) collective-permute-start(bf16[16,4096]{1,0:T(8,128)(2,1)S(1)} %add_convert_fusion.1), channel_id=1, source_target_pairs={{0,2},{1,3},{2,0},{3,1},{4,6},{5,7},{6,4},{7,5},{8,10},{9,11},{10,... | collective-permute-start | bytes 393224 | tf_op jit(solution)/shard_map/ppermute | solution.py:216
  174.8 1.6 copy-start.9
  176.4 1.2 copy-start.11
  177.6 1.2 copy-start.13
  (6 other events, 4.9 us)
Sparse Core Ops, SparseCore 0:
  107.7 33.5 all-gather.3
  142.8 31.9 all-gather.5

commit v2 on v0

v2 whole, which is shorter than its diff:
```python
import functools

import jax
import jax.numpy as jnp
from jax import lax
from jax.experimental import pallas as pl
from jax.experimental.pallas import tpu as pltpu
from jax.sharding import PartitionSpec as P

BF16 = jnp.bfloat16
F32 = jnp.float32
VMEM = pl.BlockSpec(memory_space=pltpu.VMEM)
SMEM = pl.BlockSpec(memory_space=pltpu.SMEM)
ANY = pl.BlockSpec(memory_space=pl.ANY)
HBM = pl.BlockSpec(memory_space=pltpu.HBM)
PARAMS = pltpu.CompilerParams(vmem_limit_bytes=16 * 2**20)


def in_hbm(array):
    return pltpu.with_memory_space_constraint(array, pltpu.HBM)


def column_tile(width):
    return 512 if width % 512 == 0 else width


def pick_kernel(slot_hbm, block_hbm, arriving, own_ref, info_ref, slot_order, block_pick, blocks, sems):
    ticks = slot_hbm.shape[1]
    copies = [
        pltpu.make_async_copy(source, target, sems.at[i])
        for i, (source, target) in enumerate(((slot_hbm, slot_order), (block_hbm, block_pick), (arriving, blocks)))
    ]
    for copy in copies:
        copy.start()
    for copy in copies:
        copy.wait()
    for t in range(ticks):
        info_ref[t] = slot_order[0, t]
        info_ref[ticks + t] = block_pick[0, slot_order[0, t]]
    own_ref[...] = blocks[block_pick[0, slot_order[0, 0]]]


def pick(slot_order, block_pick, arriving):
    return pl.pallas_call(
        pick_kernel,
        in_specs=[HBM, HBM, HBM],
        out_specs=[VMEM, SMEM],
        out_shape=[
            jax.ShapeDtypeStruct(arriving.shape[1:], BF16),
            jax.ShapeDtypeStruct((2 * slot_order.shape[1],), jnp.int32),
        ],
        scratch_shapes=[
            pltpu.SMEM(slot_order.shape, jnp.int32),
            pltpu.SMEM(block_pick.shape, jnp.int32),
            pltpu.VMEM(arriving.shape, BF16),
            pltpu.SemaphoreType.DMA((3,)),
        ],
        compiler_params=PARAMS,
        name="pick",
    )(in_hbm(slot_order), in_hbm(block_pick), in_hbm(arriving))


PIECES = 4


def as_column(row):
    return jnp.broadcast_to(row, (128, row.shape[1])).T[:, :1]


def as_row(column):
    return jnp.broadcast_to(column, (column.shape[0], 128)).T[:1]


def prepare_kernel(devices, info, hidden, gates, w_out, w_in, out_v, in_v, active_ref, scale_ref, weighted_ref, scales, sems):
    units = w_out.shape[0]
    piece = units // PIECES
    copies = []
    for w, (source, target) in enumerate(((w_out, out_v), (w_in, in_v))):
        for p in range(PIECES):
            rows = pl.ds(p * piece, piece)
            copies.append(pltpu.make_async_copy(source.at[rows], target.at[rows], sems.at[w, p]))
            copies[-1].start()
    ticks, _, rows, _ = hidden.shape
    me = lax.axis_index("dp")
    for t in range(ticks):
        slot = info[t]
        scales[...] = as_column(gates[0, pl.ds(slot, 1), :]).reshape(devices, rows, 1)
        for k in range(devices):
            peer = me ^ k
            own = pl.ds(k * rows, rows)
            active = jnp.maximum(hidden[slot, peer].astype(F32), 0.0)
            scale = scales[peer]
            active_ref[t, own, :] = active
            scale_ref[t, own, :] = scale
            weighted_ref[t, own, :] = (active * scale).astype(BF16)
    for copy in copies:
        copy.wait()


def prepare(info, hidden, gates, w_out, w_in):
    ticks, devices, rows, units = hidden.shape
    tokens = devices * rows
    return pl.pallas_call(
        functools.partial(prepare_kernel, devices),
        in_specs=[SMEM, VMEM, VMEM, HBM, HBM],
        out_specs=[VMEM] * 5,
        out_shape=[
            pltpu.VMEM(w_out.shape, BF16),
            pltpu.VMEM(w_in.shape, BF16),
            jax.ShapeDtypeStruct((ticks, tokens, units), F32),
            jax.ShapeDtypeStruct((ticks, tokens, 1), F32),
            jax.ShapeDtypeStruct((ticks, tokens, units), BF16),
        ],
        scratch_shapes=[pltpu.VMEM((devices, rows, 1), F32), pltpu.SemaphoreType.DMA((2, PIECES))],
        compiler_params=PARAMS,
        cost_estimate=pl.CostEstimate(
            flops=2 * ticks * tokens * units, bytes_accessed=4 * w_out.size, transcendentals=0
        ),
        name="prepare",
    )(info, hidden, gates, in_hbm(w_out), in_hbm(w_in))


def expert_kernel(devices, inner, tick, inputs, *refs):
    chunks = refs[:inputs]
    w_out, w_in, active_ref, scale_ref = refs[inputs : inputs + 4]
    parts = refs[inputs + 4 : -4]
    rows_ref, hid_ref, gate_ref, sums = refs[-4:]
    tokens = rows_ref.shape[0]
    rows = tokens // devices
    start = 0
    for chunk in chunks:
        rows_ref[pl.ds(start, chunk.shape[0]), :] = chunk[...]
        start += chunk.shape[0]
    upstream = lax.dot_general(
        rows_ref[...], w_out[...], (((1,), (1,)), ((), ())), preferred_element_type=F32
    )
    active = active_ref[tick]
    hid_grad = jnp.where(active > 0, upstream * scale_ref[tick], 0.0).astype(BF16)
    width = w_in.shape[1]
    tile = column_tile(width)
    for first in range(0, width, tile):
        cols = pl.ds(first, tile)
        part = jnp.dot(hid_grad, w_in[:, cols], preferred_element_type=F32).astype(BF16)
        start = 0
        for ref in parts:
            ref[:, cols] = part[start : start + ref.shape[0]]
            start += ref.shape[0]
    gate_sum = jnp.sum(active * upstream, axis=1, keepdims=True)
    outer = devices // inner
    me = lax.axis_index("dp")
    for k in range(devices):
        sums[me ^ k] = gate_sum[k * rows : (k + 1) * rows]
        hid_ref[k % inner * outer + k // inner] = hid_grad[k * rows : (k + 1) * rows]
    gate_ref[...] = as_row(sums[...].reshape(tokens, 1))


def expert(tick, chunks, w_out, w_in, active, scale, devices, inner):
    units, width = w_out.shape
    tokens = active.shape[1]
    rows = tokens // devices
    sizes = [inner * rows] * 2 + [rows] * (devices - 2 * inner)
    return pl.pallas_call(
        functools.partial(expert_kernel, devices, inner, tick, len(chunks)),
        in_specs=[VMEM] * (len(chunks) + 4),
        out_specs=[VMEM] * (len(sizes) + 3),
        out_shape=[jax.ShapeDtypeStruct((size, width), BF16) for size in sizes]
        + [
            jax.ShapeDtypeStruct((tokens, width), BF16),
            jax.ShapeDtypeStruct((devices, rows, units), BF16),
            jax.ShapeDtypeStruct((1, tokens), F32),
        ],
        scratch_shapes=[pltpu.VMEM((devices, rows, 1), F32)],
        compiler_params=PARAMS,
        cost_estimate=pl.CostEstimate(
            flops=4 * tokens * units * width, bytes_accessed=2 * 2**20, transcendentals=0
        ),
        name="expert_tick",
    )(*chunks, w_out, w_in, active, scale)


def product_by_columns(left_ref, right_of, out, first, last, bufs, sems):
    tile = bufs.shape[2]
    copies = []
    for step, start in enumerate(range(first, last, tile)):
        buf = step % 2
        if step >= 2:
            copies[step - 2].wait()
        bufs[buf] = jnp.dot(left_ref[...], right_of(start, tile), preferred_element_type=F32).astype(BF16)
        copies.append(pltpu.make_async_copy(bufs.at[buf], out.at[:, pl.ds(start, tile)], sems.at[buf]))
        copies[-1].start()
    for copy in copies[max(len(copies) - 2, 0) :]:
        copy.wait()


def grad_out_kernel(first, last, weighted, *refs):
    ticks, tokens, _ = weighted.shape
    rows_refs = refs[:ticks]
    out, left, bufs, sems = refs[-4:]
    for t in range(ticks):
        left[:, t * tokens : (t + 1) * tokens] = weighted[t].T

    def right_of(start, size):
        return jnp.concatenate([ref[:, pl.ds(start, size)] for ref in rows_refs], axis=0)

    product_by_columns(left, right_of, out, first, last, bufs, sems)


def grad_in_kernel(ticks, inner, pieces, first, last, info, *refs):
    hid_refs = refs[:ticks]
    groups = max(group for slot in pieces for _, _, group, _ in slot) + 1
    saved = refs[ticks : ticks + groups * inner]
    out, hid_all, left, bufs, sems = refs[-5:]
    devices, rows, units = hid_refs[0].shape
    tokens = devices * rows
    for t in range(ticks):
        hid_all[info[t]] = hid_refs[t][...]
    left[...] = hid_all[...].reshape(ticks * tokens, units).T

    def right_of(start, size):
        found = []
        for slot in pieces:
            for begin, end, group, offset in slot:
                if begin <= start < end:
                    cols = pl.ds(offset + start - begin, size)
                    for ref in saved[group * inner : (group + 1) * inner]:
                        found.append(ref[:, :, cols].reshape(-1, size))
        return jnp.concatenate(found, axis=0)

    product_by_columns(left, right_of, out, first, last, bufs, sems)


def grad_call(kernel, shape, depth, columns, args, name, scratch=(), scalars=0, onto=None):
    units, width = shape
    tile = column_tile(columns[1] - columns[0])
    more = [] if onto is None else [onto]
    return pl.pallas_call(
        kernel,
        in_specs=[SMEM] * scalars + [VMEM] * (len(args) - scalars) + [ANY] * len(more),
        out_specs=ANY,
        out_shape=jax.ShapeDtypeStruct(shape, BF16),
        scratch_shapes=list(scratch)
        + [
            pltpu.VMEM((units, depth), BF16),
            pltpu.VMEM((2, units, tile), BF16),
            pltpu.SemaphoreType.DMA((2,)),
        ],
        input_output_aliases={len(args): 0} if more else {},
        compiler_params=PARAMS,
        cost_estimate=pl.CostEstimate(
            flops=2 * depth * units * (columns[1] - columns[0]),
            bytes_accessed=2 * units * (columns[1] - columns[0]),
            transcendentals=0,
        ),
        name=name,
    )(*args, *more)


def total_of(sums, rows):
    total = sums[0][:rows].astype(F32)
    for ref in sums[1:]:
        total = total + ref[:rows].astype(F32)
    return total


def hand_on_kernel(tick, ticks, top, info, above_info, *refs):
    sums = refs[:-5]
    base, loss, done_ref, next_ref, pick_ref = refs[-5:]
    above, mine = above_info[ticks + tick], info[ticks + tick + 1]
    is_top = lax.axis_index("section") == top
    total = total_of(sums, done_ref.shape[0])
    done = (base[above].astype(F32) + total).astype(BF16)
    done_ref[...] = done
    for b in range(base.shape[0]):
        from_above = jnp.where(above == b, done, base[b])
        next_ref[b] = jnp.where(is_top, loss[b], from_above)
    pick_ref[...] = next_ref[mine]


def hand_on(tick, ticks, top, info, above_info, sums, base, loss):
    chunk = jax.ShapeDtypeStruct(base.shape[1:], BF16)
    return pl.pallas_call(
        functools.partial(hand_on_kernel, tick, ticks, top),
        in_specs=[SMEM] * 2 + [VMEM] * (len(sums) + 2),
        out_specs=[VMEM] * 3,
        out_shape=[chunk, jax.ShapeDtypeStruct(base.shape, BF16), chunk],
        compiler_params=PARAMS,
        name="hand_on",
    )(info, above_info, *sums, base, loss)


def finish_kernel(count, ticks, inner, info, *refs):
    sums = refs[:count]
    incoming = refs[count : count + ticks]
    done = refs[count + ticks : count + 2 * ticks - 1]
    gates = refs[count + 2 * ticks - 1 : -3]
    passed, gate_ref, ordered = refs[-3:]
    for t in range(ticks):
        for b in range(passed.shape[1]):
            passed[t, b] = incoming[t][b]
        if t < ticks - 1:
            passed[t, info[ticks + t]] = done[t][...]
    total = total_of(sums, passed.shape[2])
    last = info[2 * ticks - 1]
    passed[ticks - 1, last] = (incoming[ticks - 1][last].astype(F32) + total).astype(BF16)
    own = lax.axis_index("dp") // inner
    for a, ref in enumerate(gates):
        ordered[own ^ a] = ref[...]
    gate = ordered[0]
    for a in range(1, len(gates)):
        gate = gate + ordered[a]
    for t in range(ticks):
        gate_ref[info[t]] = gate[t : t + 1]


def finish(sums, incoming, done, gates, info, inner):
    ticks = len(incoming)
    return pl.pallas_call(
        functools.partial(finish_kernel, len(sums), ticks, inner),
        in_specs=[SMEM] + [VMEM] * (len(sums) + 2 * ticks - 1 + len(gates)),
        out_specs=[VMEM, VMEM],
        out_shape=[
            jax.ShapeDtypeStruct((ticks,) + incoming[0].shape, BF16),
            jax.ShapeDtypeStruct((ticks, 1, gates[0].shape[1]), F32),
        ],
        scratch_shapes=[pltpu.VMEM((len(gates),) + gates[0].shape, F32)],
        compiler_params=PARAMS,
        name="finish",
    )(info, *sums, *incoming, *done, *gates)


def after(value, *others):
    return lax.optimization_barrier((value,) + others)[0]


def per_device(
    sections, devices, w_in, w_out, input_stash, hidden_stash, gate_stash, block_pick, slot_order, arriving, loss_grads
):
    ticks = slot_order.shape[1]
    _, units, width = w_out.shape
    rows = arriving.shape[2]
    tokens = devices * rows
    half = width // 2
    inner = 2 ** ((devices.bit_length() - 1) // 2)
    outer = devices // inner
    far = list(range(outer - 1, 1, -1))

    def swap(value, step):
        return lax.ppermute(value, "dp", [(i, i ^ step) for i in range(devices)])

    def shift(value, distance, step=0):
        route = [
            (s * devices + i, (s + distance) % sections * devices + (i ^ step))
            for s in range(sections)
            for i in range(devices)
        ]
        return lax.ppermute(value, ("section", "dp"), route)

    def along_inner(own):
        return [own] + [swap(own, b) for b in range(1, inner)]

    own, info = pick(slot_order, block_pick, arriving[0])
    hidden = hidden_stash[0].reshape(ticks, devices, rows, -1)
    stash_groups = [
        jnp.concatenate([input_stash[0, p] for p in range(ticks - 1)], axis=1),
        input_stash[0, -1],
    ]
    pieces = [[(0, width, 0, p * width)] for p in range(ticks - 1)]
    pieces.append([(0, width, 1, 0)])

    incoming = [arriving[0]]
    done = []
    gate_parts = []
    rows_list, hid_list, saved = [], [], []
    for t in range(ticks):
        last = t == ticks - 1
        column = {a: swap(own, a * inner) for a in far}
        mine = along_inner(own)
        if not last:
            above_info = shift(after(info, own), -1)
            base = shift(after(incoming[t], own), -1)
        near = swap(jnp.concatenate(mine), inner)
        if t == 0:
            out_v, in_v, active, scale, weighted = prepare(
                after(info, mine[-1]), hidden, gate_stash, w_out[0], w_in[0]
            )
            column[far[-1]] = after(column[far[-1]], active)
        chunks = {a: along_inner(column[a]) for a in far}
        stash = None
        if t == 0 or last:
            stash = after(stash_groups[int(last)], column[far[-1]])
            stash = [stash] + [swap(stash, a * inner) for a in range(1, outer)]
        if not last:
            near = after(near, above_info, base)
        results = expert(
            t,
            mine + [near] + [chunk for a in far[::-1] for chunk in chunks[a]],
            out_v,
            in_v,
            active,
            scale,
            devices,
            inner,
        )
        parts = results[:-3]
        rows_list.append(results[-3])
        hid_list.append(results[-2])
        gate_parts.append(results[-1])

        def send(value, step):
            return swap(value, step) if last else shift(value, -1, step)

        direct = send(parts[1], inner)
        kept = parts[0] if last else send(parts[0], 0)
        sums = {}
        for a in far:
            pieces_a = parts[2 + (a - 2) * inner :][:inner]
            got = [swap(pieces_a[b], b).astype(F32) for b in range(1, inner)]
            sums[a] = sum(got, pieces_a[0].astype(F32)).astype(BF16)
        crossing = [
            swap((kept[b * rows :][:rows].astype(F32) + direct[b * rows :][:rows].astype(F32)).astype(BF16), b)
            for b in range(1, inner)
        ]
        if stash is not None:
            stash = jnp.stack(stash)
            sums[far[0]], stash = lax.optimization_barrier((sums[far[0]], stash))
            saved += along_inner(after(stash, sums[far[-1]]))
        totals = [send(sums[a], a * inner) for a in far] + [kept, direct] + crossing
        if not last:
            above_done, following, own = hand_on(
                t, ticks, sections - 1, info, above_info, totals, base, loss_grads[t]
            )
            done.append(above_done)
            incoming.append(following)
    done = [shift(after(value, sums[far[-1]]), 1) for value in done]
    depth = ticks * tokens
    gate = after(jnp.concatenate(gate_parts), sums[far[0]])
    step = 1
    while step < inner:
        gate = gate + swap(gate, step)
        step *= 2
    rows_list[-1] = after(rows_list[-1], done[0])
    grad_out = grad_call(
        functools.partial(grad_out_kernel, 0, width),
        (units, width),
        depth,
        (0, width),
        (weighted, *rows_list),
        "grad_out",
    )
    gate = after(gate, totals[0])
    gates = [gate] + [swap(gate, a * inner) for a in range(1, outer)]
    grad_in = grad_call(
        functools.partial(grad_in_kernel, ticks, inner, pieces, 0, width),
        (units, width),
        depth,
        (0, width),
        (info, *hid_list[:-1], hid_list[-1], *saved),
        "grad_in",
        scratch=[pltpu.VMEM((ticks, devices, rows, units), BF16)],
        scalars=1,
    )
    passed, gate_grads = finish(
        totals, incoming, done, gates, info, inner
    )
    return passed[None], grad_in[None], grad_out[None], gate_grads.reshape(1, ticks, tokens)


def solution(mesh):
    placed = (
        P("section", "dp", None),
        P("section", "dp", None),
        P("section", None, "dp", None),
        P("section", None, None, "dp"),
        P("section", None, None),
        P("section", None),
        P("section", None),
        P("section", None, "dp", None),
        P(None, None, "dp", None),
    )
    return jax.shard_map(
        functools.partial(per_device, mesh.shape["section"], mesh.shape["dp"]),
        mesh=mesh,
        in_specs=placed,
        out_specs=(
            P("section", None, None, "dp", None),
            P("section", "dp", None),
            P("section", "dp", None),
            P("section", None, None),
        ),
        check_vma=False,
    )
```

time: 344 us -> 120 us (0.35)
  waiting for transfers between devices: 244 us -> 36.7 us
  starting transfers between devices: 1.54 us -> 53.3 us
  matrix products: 45.8 us -> 0 us
  Pallas kernels: 0 us -> 25.8 us
  between operations: 22 us -> 0.97 us
  blocking collectives: 19.3 us -> 0 us
  local copies, waits for them, and re-layouts: 6.42 us -> 1.68 us
  other arithmetic: 4.47 us -> 0.39 us
    reduce_scatter x2 -> x0, waiting for transfers between devices: 128 us -> none  [section_tick(): lax.psum_scatter(jnp.dot(hid_grad, in_weight, preferred_element_type=jnp....]
    all_gather x4 -> x0, waiting for transfers between devices: 115 us -> none  [the longest x2 82.9 us: section_tick(): lax.all_gather(own_rows, 'dp', axis=0, tiled=True)]
    ppermute x1 -> x40, starting transfers between devices: 1.29 us -> 53.3 us  [the longest x33 45.4 us: swap(): return lax.ppermute(value, 'dp', [(i, i ^ step) for i in range(devices)])]
    dot_general x9 -> x0, matrix products: 45.8 us -> none  [the longest x2 15 us: weight_terms(): lax.dot_general(hid_grad, rows_input, contract, preferred_element_type=jn...]
    ppermute x1 -> x40, waiting for transfers between devices: 0.19 us -> 36.7 us  [the longest x33 29.9 us: swap(): return lax.ppermute(value, 'dp', [(i, i ^ step) for i in range(devices)])]
    pallas_call x0 -> x8, Pallas kernels: none -> 25.8 us  [the longest x2 10.7 us: grad_call(): pl.pallas_call(kernel, in_specs=[SMEM] * scalars + [VMEM] * (len(args) -...]
    psum x1 -> x0, blocking collectives: 19.3 us -> none  [section_tick(): gate_part = lax.psum(gate_part, 'dp')]
    dynamic_slice x4 -> x0, local copies, waits for them, and re-layouts: 4.29 us -> none  [the longest x2 2.24 us: section_tick(): own_rows = incoming[block_id]]
  transfers between devices with their start and end apart: 7 -> 40, of which waited for: 7 -> 17; matrix products, arithmetic and copies ran while one was open for 12% -> 0% of each run, Pallas kernels for 0% -> 15%
where the time goes in v2:
time: 120 us; the launch traced here: 119 us
  starting transfers between devices  53.3 us (44%)
  waiting for transfers between devices  36.7 us (31%)
  Pallas kernels  25.8 us (22%)
  local copies, waits for them, and re-layouts  1.68 us (1%)
    ppermute x33, starting transfers between devices, swap(): return lax.ppermute(value, 'dp', [(i, i ^ step) for i in range(devices)])  45.4 us
    ppermute x33, waiting for transfers between devices, swap(): return lax.ppermute(value, 'dp', [(i, i ^ step) for i in range(devices)])  29.9 us
    pallas_call x2, Pallas kernels, grad_call(): pl.pallas_call(kernel, in_specs=[SMEM] * scalars + [VMEM] * (len(args) -...  10.7 us
    ppermute x7, starting transfers between devices, shift(): return lax.ppermute(value, ('section', 'dp'), route)  7.84 us
    ppermute x7, waiting for transfers between devices, shift(): return lax.ppermute(value, ('section', 'dp'), route)  6.77 us
    pallas_call x2, Pallas kernels, expert(): pl.pallas_call(functools.partial(expert_kernel, devices, inner, tick, len...  6.49 us
    pallas_call x1, Pallas kernels, prepare(): pl.pallas_call(functools.partial(prepare_kernel, devices), in_specs=[SMEM...  4.77 us
  transfers between devices with their start and end apart: 40, of which 17 were waited for; matrix products, arithmetic and copies ran while one was open for 0% of the time, Pallas kernels for 15%

profile of v2, /device:TPU:0, one launch (start us, length us, event | category | flops | bytes accessed | tf_op | source)
XLA Modules:
  0.0 118.8 jit_solution(17438362934913188963)
XLA Ops:
  0.6 1.6 %pick.1 = (bf16[16,4096]{1,0:T(8,128)(2,1)S(1)}, s32[4]{0:T(128)S(1)}) custom-call(s32[1,2]{1,0:T(1,128)} %slot_hbm.1, s32[1,2]{1,0:T(1,128)} %block_hbm.1, bf16[2,16,4096]{2,1,0:T(8,128)(2,1)} %bitcast.21), custom_call_target="tpu_custom_call" | custom-call | tf_op jit(solution)/shard_map/pick/pallas_call | solution.py:44
  2.2 3.0 %collective-permute-start.1 = (bf16[16,4096]{1,0:T(8,128)(2,1)S(1)}, bf16[16,4096]{1,0:T(8,128)(2,1)S(1)}, u32[]{:S(2)}, u32[]{:S(2)}) collective-permute-start(bf16[16,4096]{1,0:T(8,128)(2,1)S(1)} %get-tuple-element.52.refs_0_), channel_id=1, source_target_pairs={{0,1},{1,0},{2,3},{3,2},{4,5},{5,4},{6,7},{7,6},{8,9},{9,8},{10,11... | collective-permute-start | bytes 393224 | tf_op jit(solution)/shard_map/ppermute | solution.py:348
  5.2 2.6 %collective-permute-start.4 = (bf16[16,4096]{1,0:T(8,128)(2,1)S(1)}, bf16[16,4096]{1,0:T(8,128)(2,1)S(1)}, u32[]{:S(2)}, u32[]{:S(2)}) collective-permute-start(bf16[16,4096]{1,0:T(8,128)(2,1)S(1)} %get-tuple-element.52.refs_0_), channel_id=1, source_target_pairs={{0,4},{1,5},{2,6},{3,7},{4,0},{5,1},{6,2},{7,3},{8,12},{9,13},{10,... | collective-permute-start | bytes 393224 | tf_op jit(solution)/shard_map/ppermute | solution.py:348
  7.8 1.3 %collective-permute-start.6 = (bf16[16,4096]{1,0:T(8,128)(2,1)S(1)}, bf16[16,4096]{1,0:T(8,128)(2,1)S(1)}, u32[]{:S(2)}, u32[]{:S(2)}) collective-permute-start(bf16[16,4096]{1,0:T(8,128)(2,1)S(1)} %get-tuple-element.52.refs_0_), channel_id=1, source_target_pairs={{0,6},{1,7},{2,4},{3,5},{4,2},{5,3},{6,0},{7,1},{8,14},{9,15},{10,... | collective-permute-start | bytes 393224 | tf_op jit(solution)/shard_map/ppermute | solution.py:348
  9.3 1.5 %collective-permute-start.3 = (bf16[2,16,4096]{2,1,0:T(8,128)(2,1)}, bf16[2,16,4096]{2,1,0:T(8,128)(2,1)S(1)}, u32[]{:S(2)}, u32[]{:S(2)}) collective-permute-start(bf16[2,16,4096]{2,1,0:T(8,128)(2,1)} %bitcast.22), channel_id=1, source_target_pairs={{0,24},{1,25},{2,26},{3,27},{4,28},{5,29},{6,30},{7,31},{8,0},{9,1... | collective-permute-start | bytes 786440 | tf_op jit(solution)/shard_map/ppermute | solution.py:356
  11.1 1.0 copy-done.1
  12.8 4.8 %prepare.1 = (bf16[640,4096]{1,0:T(8,128)(2,1)S(1)}, bf16[640,4096]{1,0:T(8,128)(2,1)S(1)}, f32[2,128,640]{2,1,0:T(8,128)S(1)}, f32[2,128,1]{2,1,0:T(8,128)S(1)}, bf16[2,128,640]{2,1,0:T(8,128)(2,1)S(1)}) custom-call(s32[4]{0:T(128)S(1)} %get-tuple-element.56.info, bf16[2,8,16,640]{3,2,1,0:T(8,128)(2,1)S(1)} %bitcast.24, f32[1,2,128]{2,1,0:T(2,128)S(1)} %copy-done.3, ...), custom_call_target="tpu_custom_call" | custom-call | flops 327680 | bytes 10485760 | tf_op jit(solution)/shard_map/prepare/pallas_call | solution.py:103
  18.6 1.3 %collective-permute-start.7 = (bf16[16,4096]{1,0:T(8,128)(2,1)S(1)}, bf16[16,4096]{1,0:T(8,128)(2,1)S(1)}, u32[]{:S(2)}, u32[]{:S(2)}) collective-permute-start(bf16[16,4096]{1,0:T(8,128)(2,1)S(1)} %collective-permute-done.6.refs_5_), channel_id=1, source_target_pairs={{0,1},{1,0},{2,3},{3,2},{4,5},{5,4},{6,7},{7,6},{8,9},{9,8},{10,11... | collective-permute-start | bytes 393224 | tf_op jit(solution)/shard_map/ppermute | solution.py:348
  20.0 1.6 %collective-permute-start.9 = (bf16[16,4096]{1,0:T(8,128)(2,1)S(1)}, bf16[16,4096]{1,0:T(8,128)(2,1)S(1)}, u32[]{:S(2)}, u32[]{:S(2)}) collective-permute-start(bf16[16,4096]{1,0:T(8,128)(2,1)S(1)} %get-tuple-element.64), channel_id=1, source_target_pairs={{0,2},{1,3},{2,0},{3,1},{4,6},{5,7},{6,4},{7,5},{8,10},{9,11},{10,... | collective-permute-start | bytes 393224 | tf_op jit(solution)/shard_map/ppermute | solution.py:348
  21.5 1.7 %collective-permute-start.10 = (bf16[16,4096]{1,0:T(8,128)(2,1)S(1)}, bf16[16,4096]{1,0:T(8,128)(2,1)S(1)}, u32[]{:S(2)}, u32[]{:S(2)}) collective-permute-start(bf16[16,4096]{1,0:T(8,128)(2,1)S(1)} %get-tuple-element.64), channel_id=1, source_target_pairs={{0,4},{1,5},{2,6},{3,7},{4,0},{5,1},{6,2},{7,3},{8,12},{9,13},{10,... | collective-permute-start | bytes 393224 | tf_op jit(solution)/shard_map/ppermute | solution.py:348
  23.2 2.3 %collective-permute-start.11 = (bf16[16,4096]{1,0:T(8,128)(2,1)S(1)}, bf16[16,4096]{1,0:T(8,128)(2,1)S(1)}, u32[]{:S(2)}, u32[]{:S(2)}) collective-permute-start(bf16[16,4096]{1,0:T(8,128)(2,1)S(1)} %get-tuple-element.64), channel_id=1, source_target_pairs={{0,6},{1,7},{2,4},{3,5},{4,2},{5,3},{6,0},{7,1},{8,14},{9,15},{10,... | collective-permute-start | bytes 393224 | tf_op jit(solution)/shard_map/ppermute | solution.py:348
  25.5 3.2 %expert_tick.2 = (bf16[32,4096]{1,0:T(8,128)(2,1)S(1)}, bf16[32,4096]{1,0:T(8,128)(2,1)S(1)}, bf16[16,4096]{1,0:T(8,128)(2,1)S(1)}, bf16[16,4096]{1,0:T(8,128)(2...) custom-call(bf16[16,4096]{1,0:T(8,128)(2,1)S(1)} %get-tuple-element., ...), custom_call_target="tpu_custom_call" | custom-call | flops 1342177280 | bytes 2097152 | tf_op jit(solution)/shard_map/expert_tick/pallas_call | solution.py:162
  29.2 5.2 %collective-permute-done.10 = bf16[16,4096]{1,0:T(8,128)(2,1)S(1)} collective-permute-done((bf16[16,4096]{1,0:T(8,128)(2,1)S(1)}, bf16[16,4096]{1,0:T(8,128)(2,1)S(1)}, u32[]{:S(2)}, u32[]{:S(2)}) %collective-permute-start.10) | collective-permute-done | bytes 131104 | tf_op jit(solution)/shard_map/ppermute | solution.py:348
  34.6 2.3 %collective-permute-start.16 = (bf16[32,4096]{1,0:T(8,128)(2,1)S(1)}, bf16[32,4096]{1,0:T(8,128)(2,1)S(1)}, u32[]{:S(2)}, u32[]{:S(2)}) collective-permute-start(bf16[32,4096]{1,0:T(8,128)(2,1)S(1)} %get-tuple-element.69), channel_id=1, source_target_pairs={{0,26},{1,27},{2,24},{3,25},{4,30},{5,31},{6,28},{7,29},{8,2},{9,3... | collective-permute-start | bytes 786440 | tf_op jit(solution)/shard_map/ppermute | solution.py:356
  36.9 1.5 %collective-permute-start.8 = (bf16[16,4096]{1,0:T(8,128)(2,1)S(1)}, bf16[16,4096]{1,0:T(8,128)(2,1)S(1)}, u32[]{:S(2)}, u32[]{:S(2)}) collective-permute-start(bf16[16,4096]{1,0:T(8,128)(2,1)S(1)} %get-tuple-element.63), channel_id=1, source_target_pairs={{0,1},{1,0},{2,3},{3,2},{4,5},{5,4},{6,7},{7,6},{8,9},{9,8},{10,11... | collective-permute-start | bytes 393224 | tf_op jit(solution)/shard_map/ppermute | solution.py:348
  38.4 1.5 %collective-permute-start.14 = (bf16[16,4096]{1,0:T(8,128)(2,1)S(1)}, bf16[16,4096]{1,0:T(8,128)(2,1)S(1)}, u32[]{:S(2)}, u32[]{:S(2)}) collective-permute-start(bf16[16,4096]{1,0:T(8,128)(2,1)S(1)} %add_convert_fusion.4), channel_id=1, source_target_pairs={{0,28},{1,29},{2,30},{3,31},{4,24},{5,25},{6,26},{7,27},{8,4},{9,5... | collective-permute-start | bytes 393224 | tf_op jit(solution)/shard_map/ppermute | solution.py:356
  39.9 2.2 %collective-permute-done.8 = bf16[16,4096]{1,0:T(8,128)(2,1)S(1)} collective-permute-done((bf16[16,4096]{1,0:T(8,128)(2,1)S(1)}, bf16[16,4096]{1,0:T(8,128)(2,1)S(1)}, u32[]{:S(2)}, u32[]{:S(2)}) %collective-permute-start.8) | collective-permute-done | bytes 131104 | tf_op jit(solution)/shard_map/ppermute | solution.py:348
  42.1 2.3 %collective-permute-start.12 = (bf16[16,4096]{1,0:T(8,128)(2,1)S(1)}, bf16[16,4096]{1,0:T(8,128)(2,1)S(1)}, u32[]{:S(2)}, u32[]{:S(2)}) collective-permute-start(bf16[16,4096]{1,0:T(8,128)(2,1)S(1)} %add_convert_fusion.5), channel_id=1, source_target_pairs={{0,30},{1,31},{2,28},{3,29},{4,26},{5,27},{6,24},{7,25},{8,6},{9,7... | collective-permute-start | bytes 393224 | tf_op jit(solution)/shard_map/ppermute | solution.py:356
  44.5 1.6 %collective-permute-done.16.refs_3_ = bf16[32,4096]{1,0:T(8,128)(2,1)S(1)} collective-permute-done((bf16[32,4096]{1,0:T(8,128)(2,1)S(1)}, bf16[32,4096]{1,0:T(8,128)(2,1)S(1)}, u32[]{:S(2)}, u32[]{:S(2)}) %collective-permute-start.16) | collective-permute-done | bytes 262176 | tf_op jit(solution)/shard_map/ppermute | solution.py:356
  46.6 3.8 %collective-permute-done.12.refs_0_ = bf16[16,4096]{1,0:T(8,128)(2,1)S(1)} collective-permute-done((bf16[16,4096]{1,0:T(8,128)(2,1)S(1)}, bf16[16,4096]{1,0:T(8,128)(2,1)S(1)}, u32[]{:S(2)}, u32[]{:S(2)}) %collective-permute-start.12) | collective-permute-done | bytes 131104 | tf_op jit(solution)/shard_map/ppermute | solution.py:356
  50.4 1.5 %collective-permute-done.17.refs_4_ = bf16[16,4096]{1,0:T(8,128)(2,1)S(1)} collective-permute-done((bf16[16,4096]{1,0:T(8,128)(2,1)S(1)}, bf16[16,4096]{1,0:T(8,128)(2,1)S(1)}, u32[]{:S(2)}, u32[]{:S(2)}) %collective-permute-start.17) | collective-permute-done | bytes 131104 | tf_op jit(solution)/shard_map/ppermute | solution.py:348
  53.4 3.8 %collective-permute-start.20 = (bf16[16,4096]{1,0:T(8,128)(2,1)S(1)}, bf16[16,4096]{1,0:T(8,128)(2,1)S(1)}, u32[]{:S(2)}, u32[]{:S(2)}) collective-permute-start(bf16[16,4096]{1,0:T(8,128)(2,1)S(1)} %get-tuple-element.70.refs_0_), channel_id=1, source_target_pairs={{0,4},{1,5},{2,6},{3,7},{4,0},{5,1},{6,2},{7,3},{8,12},{9,13},{10,... | collective-permute-start | bytes 393224 | tf_op jit(solution)/shard_map/ppermute | solution.py:348
  58.4 2.0 %collective-permute-start.19 = (bf16[32,4096]{1,0:T(8,128)(2,1)S(1)}, bf16[32,4096]{1,0:T(8,128)(2,1)S(1)}, u32[]{:S(2)}, u32[]{:S(2)}) collective-permute-start(bf16[32,4096]{1,0:T(8,128)(2,1)S(1)} %pad_maximum_fusion.3), channel_id=1, source_target_pairs={{0,2},{1,3},{2,0},{3,1},{4,6},{5,7},{6,4},{7,5},{8,10},{9,11},{10,... | collective-permute-start | bytes 786440 | tf_op jit(solution)/shard_map/ppermute | solution.py:348
  60.4 6.9 %collective-permute-done.20.refs_3_ = bf16[16,4096]{1,0:T(8,128)(2,1)S(1)} collective-permute-done((bf16[16,4096]{1,0:T(8,128)(2,1)S(1)}, bf16[16,4096]{1,0:T(8,128)(2,1)S(1)}, u32[]{:S(2)}, u32[]{:S(2)}) %collective-permute-start.20) | collective-permute-done | bytes 131104 | tf_op jit(solution)/shard_map/ppermute | solution.py:348
  68.2 1.1 collective-permute-start.23
  69.3 1.6 %collective-permute-start.25 = (bf16[16,4096]{1,0:T(8,128)(2,1)S(1)}, bf16[16,4096]{1,0:T(8,128)(2,1)S(1)}, u32[]{:S(2)}, u32[]{:S(2)}) collective-permute-start(bf16[16,4096]{1,0:T(8,128)(2,1)S(1)} %get-tuple-element.73), channel_id=1, source_target_pairs={{0,2},{1,3},{2,0},{3,1},{4,6},{5,7},{6,4},{7,5},{8,10},{9,11},{10,... | collective-permute-start | bytes 393224 | tf_op jit(solution)/shard_map/ppermute | solution.py:348
  70.9 1.3 %collective-permute-done.21.refs_4_ = bf16[16,4096]{1,0:T(8,128)(2,1)S(1)} collective-permute-done((bf16[16,4096]{1,0:T(8,128)(2,1)S(1)}, bf16[16,4096]{1,0:T(8,128)(2,1)S(1)}, u32[]{:S(2)}, u32[]{:S(2)}) %collective-permute-start.21) | collective-permute-done | bytes 131104 | tf_op jit(solution)/shard_map/ppermute | solution.py:348
  72.2 1.5 %collective-permute-start.27 = (bf16[16,4096]{1,0:T(8,128)(2,1)S(1)}, bf16[16,4096]{1,0:T(8,128)(2,1)S(1)}, u32[]{:S(2)}, u32[]{:S(2)}) collective-permute-start(bf16[16,4096]{1,0:T(8,128)(2,1)S(1)} %get-tuple-element.73), channel_id=1, source_target_pairs={{0,6},{1,7},{2,4},{3,5},{4,2},{5,3},{6,0},{7,1},{8,14},{9,15},{10,... | collective-permute-start | bytes 393224 | tf_op jit(solution)/shard_map/ppermute | solution.py:348
  73.7 1.5 %collective-permute-start.38 = (bf16[4,16,4096]{2,1,0:T(8,128)(2,1)S(1)}, bf16[4,16,4096]{2,1,0:T(8,128)(2,1)S(1)}, u32[]{:S(2)}, u32[]{:S(2)}) collective-permute-start(bf16[4,16,4096]{2,1,0:T(8,128)(2,1)S(1)} %pad_maximum_fusion.refs_2_), channel_id=1, source_target_pairs={{0,1},{1,0},{2,3},{3,2},{4,5},{5,4},{6,7},{7,6},{8,9},{9,8},{10,11... | collective-permute-start | bytes 1572872 | tf_op jit(solution)/shard_map/ppermute | solution.py:348
  75.2 3.2 %expert_tick.3 = (bf16[32,4096]{1,0:T(8,128)(2,1)S(1)}, bf16[32,4096]{1,0:T(8,128)(2,1)S(1)}, bf16[16,4096]{1,0:T(8,128)(2,1)S(1)}, bf16[16,4096]{1,0:T(8,128)(2...) custom-call(bf16[16,4096]{1,0:T(8,128)(2,1)S(1)} %get-tuple-element., ...), custom_call_target="tpu_custom_call" | custom-call | flops 1342177280 | bytes 2097152 | tf_op jit(solution)/shard_map/expert_tick/pallas_call | solution.py:162
  79.0 3.5 %collective-permute-done.26 = bf16[16,4096]{1,0:T(8,128)(2,1)S(1)} collective-permute-done((bf16[16,4096]{1,0:T(8,128)(2,1)S(1)}, bf16[16,4096]{1,0:T(8,128)(2,1)S(1)}, u32[]{:S(2)}, u32[]{:S(2)}) %collective-permute-start.26) | collective-permute-done | bytes 131104 | tf_op jit(solution)/shard_map/ppermute | solution.py:348
  82.6 1.0 collective-permute-start.29
  83.6 2.0 %collective-permute-start.31 = (bf16[32,4096]{1,0:T(8,128)(2,1)S(1)}, bf16[32,4096]{1,0:T(8,128)(2,1)S(1)}, u32[]{:S(2)}, u32[]{:S(2)}) collective-permute-start(bf16[32,4096]{1,0:T(8,128)(2,1)S(1)} %get-tuple-element.78), channel_id=1, source_target_pairs={{0,2},{1,3},{2,0},{3,1},{4,6},{5,7},{6,4},{7,5},{8,10},{9,11},{10,... | collective-permute-start | bytes 786440 | tf_op jit(solution)/shard_map/ppermute | solution.py:348
  85.5 4.4 %collective-permute-done.24 = bf16[16,4096]{1,0:T(8,128)(2,1)S(1)} collective-permute-done((bf16[16,4096]{1,0:T(8,128)(2,1)S(1)}, bf16[16,4096]{1,0:T(8,128)(2,1)S(1)}, u32[]{:S(2)}, u32[]{:S(2)}) %collective-permute-start.24) | collective-permute-done | bytes 131104 | tf_op jit(solution)/shard_map/ppermute | solution.py:348
  90.0 1.5 %collective-permute-start.28 = (bf16[16,4096]{1,0:T(8,128)(2,1)S(1)}, bf16[16,4096]{1,0:T(8,128)(2,1)S(1)}, u32[]{:S(2)}, u32[]{:S(2)}) collective-permute-start(bf16[16,4096]{1,0:T(8,128)(2,1)S(1)} %add_convert_fusion.2), channel_id=1, source_target_pairs={{0,6},{1,7},{2,4},{3,5},{4,2},{5,3},{6,0},{7,1},{8,14},{9,15},{10,... | collective-permute-start | bytes 393224 | tf_op jit(solution)/shard_map/ppermute | solution.py:348
  91.5 1.2 %collective-permute-start.34 = (f32[2,128]{1,0:T(2,128)S(1)}, f32[2,128]{1,0:T(2,128)S(1)}, u32[]{:S(2)}, u32[]{:S(2)}) collective-permute-start(f32[2,128]{1,0:T(2,128)S(1)} %pad_maximum_fusion.4), channel_id=1, source_target_pairs={{0,1},{1,0},{2,3},{3,2},{4,5},{5,4},{6,7},{7,6},{8,9},{9,8},{10,11... | collective-permute-start | bytes 3080 | tf_op jit(solution)/shard_map/ppermute | solution.py:348
  92.8 1.1 collective-permute-start.30
  93.9 1.2 collective-permute-done.34
  95.1 1.2 %collective-permute-start.39 = (bf16[4,16,4096]{2,1,0:T(8,128)(2,1)S(1)}, bf16[4,16,4096]{2,1,0:T(8,128)(2,1)S(1)}, u32[]{:S(2)}, u32[]{:S(2)}) collective-permute-start(bf16[4,16,4096]{2,1,0:T(8,128)(2,1)S(1)} %pad_maximum_fusion.1.refs_4_), channel_id=1, source_target_pairs={{0,1},{1,0},{2,3},{3,2},{4,5},{5,4},{6,7},{7,6},{8,9},{9,8},{10,11... | collective-permute-start | bytes 1572872 | tf_op jit(solution)/shard_map/ppermute | solution.py:348
  97.1 1.0 collective-permute-start.32
  98.1 1.4 %collective-permute-done.33.refs_7_ = bf16[16,4096]{1,0:T(8,128)(2,1)S(1)} collective-permute-done((bf16[16,4096]{1,0:T(8,128)(2,1)S(1)}, bf16[16,4096]{1,0:T(8,128)(2,1)S(1)}, u32[]{:S(2)}, u32[]{:S(2)}) %collective-permute-start.33) | collective-permute-done | bytes 131104 | tf_op jit(solution)/shard_map/ppermute | solution.py:356
  99.5 1.6 %collective-permute-start.35 = (f32[2,128]{1,0:T(2,128)S(1)}, f32[2,128]{1,0:T(2,128)S(1)}, u32[]{:S(2)}, u32[]{:S(2)}) collective-permute-start(f32[2,128]{1,0:T(2,128)S(1)} %add.27.refs_8_), channel_id=1, source_target_pairs={{0,2},{1,3},{2,0},{3,1},{4,6},{5,7},{6,4},{7,5},{8,10},{9,11},{10,... | collective-permute-start | bytes 3080 | tf_op jit(solution)/shard_map/ppermute | solution.py:348
  101.3 1.1 collective-permute-start.36
  103.0 2.4 %collective-permute-start.37 = (f32[2,128]{1,0:T(2,128)S(1)}, f32[2,128]{1,0:T(2,128)S(1)}, u32[]{:S(2)}, u32[]{:S(2)}) collective-permute-start(f32[2,128]{1,0:T(2,128)S(1)} %add.27.refs_8_), channel_id=1, source_target_pairs={{0,6},{1,7},{2,4},{3,5},{4,2},{5,3},{6,0},{7,1},{8,14},{9,15},{10,... | collective-permute-start | bytes 3080 | tf_op jit(solution)/shard_map/ppermute | solution.py:348
  105.4 5.0 %grad_out.1 = bf16[640,4096]{1,0:T(8,128)(2,1)} custom-call(bf16[2,128,640]{2,1,0:T(8,128)(2,1)S(1)} %get-tuple-element.93.weighted, bf16[128,4096]{1,0:T(8,128)(2,1)S(1)} %get-tuple-element.94.refs_0_, bf16[128,4096]{1,0:T(8,128)(2,1)S(1)} %get-tuple-element.96.refs_1_), custom_call_target="tpu_custom_call" | custom-call | flops 1342177280 | bytes 5242880 | tf_op jit(solution)/shard_map/grad_out/pallas_call | solution.py:236
  110.5 1.0 collective-permute-done.32.refs_4_
  111.4 1.5 %finish.1 = (bf16[2,2,16,4096]{3,2,1,0:T(8,128)(2,1)}, f32[2,1,128]{2,1,0:T(1,128)}) custom-call(s32[4]{0:T(128)S(1)} %get-tuple-element.56.info, bf16[16,4096]{1,0:T(8,128)(2,1)S(1)} %collective-permute-done.28.refs_0_, bf16[16,4096]{1,0:T(8,128)(2,1)S(1)} %collective-permute-done.30.refs_1_, bf16[32,4096]{1,0:T(8,128)(2,1)S(1)} %get-tuple-element.77.refs_2_, ...), custom_call_target="tpu_custom_call" | custom-call | tf_op jit(solution)/shard_map/finish/pallas_call | solution.py:317
  113.0 5.6 %grad_in.1 = bf16[640,4096]{1,0:T(8,128)(2,1)} custom-call(s32[4]{0:T(128)S(1)} %get-tuple-element.56.info, bf16[8,16,640]{2,1,0:T(8,128)(2,1)S(1)} %get-tuple-element.87.refs_0_, bf16[8,16,640]{2,1,0:T(8,128)(2,1)S(1)} %get-tuple-element.88.refs_1_, bf16[4,16,4096]{2,1,0:T(8,128)(2,1)S(1)} %pad_maximum_fusion.refs_2_, ...), custom_call_target="tpu_custom_call" | custom-call | flops 1342177280 | bytes 5242880 | tf_op jit(solution)/shard_map/grad_in/pallas_call | solution.py:236
  (63 shorter events, 9.4 us)
Async XLA Ops:
  2.2 8.6 %collective-permute-start.1 = (bf16[16,4096]{1,0:T(8,128)(2,1)S(1)}, bf16[16,4096]{1,0:T(8,128)(2,1)S(1)}, u32[]{:S(2)}, u32[]{:S(2)}) collective-permute-start(bf16[16,4096]{1,0:T(8,128)(2,1)S(1)} %get-tuple-element.52.refs_0_), channel_id=1, source_target_pairs={{0,1},{1,0},{2,3},{3,2},{4,5},{5,4},{6,7},{7,6},{8,9},{9,8},{10,11... | collective-permute-start | bytes 393224 | tf_op jit(solution)/shard_map/ppermute | solution.py:348
  5.2 12.7 %collective-permute-start.4 = (bf16[16,4096]{1,0:T(8,128)(2,1)S(1)}, bf16[16,4096]{1,0:T(8,128)(2,1)S(1)}, u32[]{:S(2)}, u32[]{:S(2)}) collective-permute-start(bf16[16,4096]{1,0:T(8,128)(2,1)S(1)} %get-tuple-element.52.refs_0_), channel_id=1, source_target_pairs={{0,4},{1,5},{2,6},{3,7},{4,0},{5,1},{6,2},{7,3},{8,12},{9,13},{10,... | collective-permute-start | bytes 393224 | tf_op jit(solution)/shard_map/ppermute | solution.py:348
  7.8 10.8 %collective-permute-start.6 = (bf16[16,4096]{1,0:T(8,128)(2,1)S(1)}, bf16[16,4096]{1,0:T(8,128)(2,1)S(1)}, u32[]{:S(2)}, u32[]{:S(2)}) collective-permute-start(bf16[16,4096]{1,0:T(8,128)(2,1)S(1)} %get-tuple-element.52.refs_0_), channel_id=1, source_target_pairs={{0,6},{1,7},{2,4},{3,5},{4,2},{5,3},{6,0},{7,1},{8,14},{9,15},{10,... | collective-permute-start | bytes 393224 | tf_op jit(solution)/shard_map/ppermute | solution.py:348
  9.2 10.8 %collective-permute-start = (s32[4]{0:T(128)S(1)}, s32[4]{0:T(128)S(1)}, u32[]{:S(2)}, u32[]{:S(2)}) collective-permute-start(s32[4]{0:T(128)S(1)} %get-tuple-element.56.info), channel_id=1, source_target_pairs={{0,24},{1,25},{2,26},{3,27},{4,28},{5,29},{6,30},{7,31},{8,0},{9,1... | collective-permute-start | bytes 56 | tf_op jit(solution)/shard_map/ppermute | solution.py:356
  9.3 12.3 %collective-permute-start.3 = (bf16[2,16,4096]{2,1,0:T(8,128)(2,1)}, bf16[2,16,4096]{2,1,0:T(8,128)(2,1)S(1)}, u32[]{:S(2)}, u32[]{:S(2)}) collective-permute-start(bf16[2,16,4096]{2,1,0:T(8,128)(2,1)} %bitcast.22), channel_id=1, source_target_pairs={{0,24},{1,25},{2,26},{3,27},{4,28},{5,29},{6,30},{7,31},{8,0},{9,1... | collective-permute-start | bytes 786440 | tf_op jit(solution)/shard_map/ppermute | solution.py:356
  10.8 12.4 %collective-permute-start.2 = (bf16[32,4096]{1,0:T(8,128)(2,1)S(1)}, bf16[32,4096]{1,0:T(8,128)(2,1)S(1)}, u32[]{:S(2)}, u32[]{:S(2)}) collective-permute-start(bf16[32,4096]{1,0:T(8,128)(2,1)S(1)} %pad_maximum_fusion.2), channel_id=1, source_target_pairs={{0,2},{1,3},{2,0},{3,1},{4,6},{5,7},{6,4},{7,5},{8,10},{9,11},{10,... | collective-permute-start | bytes 786440 | tf_op jit(solution)/shard_map/ppermute | solution.py:348
  11.1 1.0 copy-start.1
  12.1 0.7 copy-start.3
  12.8 7.2 %copy-start.4 = (bf16[1,2,16,4096]{3,2,1,0:T(8,128)(2,1)S(1)}, bf16[1,2,16,4096]{3,2,1,0:T(8,128)(2,1)}, u32[]{:S(2)}) copy-start(bf16[1,2,16,4096]{3,2,1,0:T(8,128)(2,1)} %param.11) | copy-start | bytes 786436
  17.9 7.6 %collective-permute-start.5 = (bf16[16,4096]{1,0:T(8,128)(2,1)S(1)}, bf16[16,4096]{1,0:T(8,128)(2,1)S(1)}, u32[]{:S(2)}, u32[]{:S(2)}) collective-permute-start(bf16[16,4096]{1,0:T(8,128)(2,1)S(1)} %collective-permute-done.4.refs_3_), channel_id=1, source_target_pairs={{0,1},{1,0},{2,3},{3,2},{4,5},{5,4},{6,7},{7,6},{8,9},{9,8},{10,11... | collective-permute-start | bytes 393224 | tf_op jit(solution)/shard_map/ppermute | solution.py:348
  18.6 6.9 %collective-permute-start.7 = (bf16[16,4096]{1,0:T(8,128)(2,1)S(1)}, bf16[16,4096]{1,0:T(8,128)(2,1)S(1)}, u32[]{:S(2)}, u32[]{:S(2)}) collective-permute-start(bf16[16,4096]{1,0:T(8,128)(2,1)S(1)} %collective-permute-done.6.refs_5_), channel_id=1, source_target_pairs={{0,1},{1,0},{2,3},{3,2},{4,5},{5,4},{6,7},{7,6},{8,9},{9,8},{10,11... | collective-permute-start | bytes 393224 | tf_op jit(solution)/shard_map/ppermute | solution.py:348
  20.0 9.2 %collective-permute-start.9 = (bf16[16,4096]{1,0:T(8,128)(2,1)S(1)}, bf16[16,4096]{1,0:T(8,128)(2,1)S(1)}, u32[]{:S(2)}, u32[]{:S(2)}) collective-permute-start(bf16[16,4096]{1,0:T(8,128)(2,1)S(1)} %get-tuple-element.64), channel_id=1, source_target_pairs={{0,2},{1,3},{2,0},{3,1},{4,6},{5,7},{6,4},{7,5},{8,10},{9,11},{10,... | collective-permute-start | bytes 393224 | tf_op jit(solution)/shard_map/ppermute | solution.py:348
  21.5 12.9 %collective-permute-start.10 = (bf16[16,4096]{1,0:T(8,128)(2,1)S(1)}, bf16[16,4096]{1,0:T(8,128)(2,1)S(1)}, u32[]{:S(2)}, u32[]{:S(2)}) collective-permute-start(bf16[16,4096]{1,0:T(8,128)(2,1)S(1)} %get-tuple-element.64), channel_id=1, source_target_pairs={{0,4},{1,5},{2,6},{3,7},{4,0},{5,1},{6,2},{7,3},{8,12},{9,13},{10,... | collective-permute-start | bytes 393224 | tf_op jit(solution)/shard_map/ppermute | solution.py:348
  23.2 11.2 %collective-permute-start.11 = (bf16[16,4096]{1,0:T(8,128)(2,1)S(1)}, bf16[16,4096]{1,0:T(8,128)(2,1)S(1)}, u32[]{:S(2)}, u32[]{:S(2)}) collective-permute-start(bf16[16,4096]{1,0:T(8,128)(2,1)S(1)} %get-tuple-element.64), channel_id=1, source_target_pairs={{0,6},{1,7},{2,4},{3,5},{4,2},{5,3},{6,0},{7,1},{8,14},{9,15},{10,... | collective-permute-start | bytes 393224 | tf_op jit(solution)/shard_map/ppermute | solution.py:348
  25.5 26.4 %copy-start.2 = (bf16[1,2,16,4096]{3,2,1,0:T(8,128)(2,1)S(1)}, bf16[1,2,16,4096]{3,2,1,0:T(8,128)(2,1)}, u32[]{:S(2)}) copy-start(bf16[1,2,16,4096]{3,2,1,0:T(8,128)(2,1)} %param.17) | copy-start | bytes 786436
  28.8 9.6 %collective-permute-start.13 = (bf16[16,4096]{1,0:T(8,128)(2,1)S(1)}, bf16[16,4096]{1,0:T(8,128)(2,1)S(1)}, u32[]{:S(2)}, u32[]{:S(2)}) collective-permute-start(bf16[16,4096]{1,0:T(8,128)(2,1)S(1)} %get-tuple-element.67), channel_id=1, source_target_pairs={{0,1},{1,0},{2,3},{3,2},{4,5},{5,4},{6,7},{7,6},{8,9},{9,8},{10,11... | collective-permute-start | bytes 393224 | tf_op jit(solution)/shard_map/ppermute | solution.py:348
  34.5 10.0 %collective-permute-start.15 = (bf16[32,4096]{1,0:T(8,128)(2,1)S(1)}, bf16[32,4096]{1,0:T(8,128)(2,1)S(1)}, u32[]{:S(2)}, u32[]{:S(2)}) collective-permute-start(bf16[32,4096]{1,0:T(8,128)(2,1)S(1)} %get-tuple-element.68), channel_id=1, source_target_pairs={{0,24},{1,25},{2,26},{3,27},{4,28},{5,29},{6,30},{7,31},{8,0},{9,1... | collective-permute-start | bytes 786440 | tf_op jit(solution)/shard_map/ppermute | solution.py:356
  34.6 11.5 %collective-permute-start.16 = (bf16[32,4096]{1,0:T(8,128)(2,1)S(1)}, bf16[32,4096]{1,0:T(8,128)(2,1)S(1)}, u32[]{:S(2)}, u32[]{:S(2)}) collective-permute-start(bf16[32,4096]{1,0:T(8,128)(2,1)S(1)} %get-tuple-element.69), channel_id=1, source_target_pairs={{0,26},{1,27},{2,24},{3,25},{4,30},{5,31},{6,28},{7,29},{8,2},{9,3... | collective-permute-start | bytes 786440 | tf_op jit(solution)/shard_map/ppermute | solution.py:356
  36.9 5.2 %collective-permute-start.8 = (bf16[16,4096]{1,0:T(8,128)(2,1)S(1)}, bf16[16,4096]{1,0:T(8,128)(2,1)S(1)}, u32[]{:S(2)}, u32[]{:S(2)}) collective-permute-start(bf16[16,4096]{1,0:T(8,128)(2,1)S(1)} %get-tuple-element.63), channel_id=1, source_target_pairs={{0,1},{1,0},{2,3},{3,2},{4,5},{5,4},{6,7},{7,6},{8,9},{9,8},{10,11... | collective-permute-start | bytes 393224 | tf_op jit(solution)/shard_map/ppermute | solution.py:348
  38.4 8.2 %collective-permute-start.14 = (bf16[16,4096]{1,0:T(8,128)(2,1)S(1)}, bf16[16,4096]{1,0:T(8,128)(2,1)S(1)}, u32[]{:S(2)}, u32[]{:S(2)}) collective-permute-start(bf16[16,4096]{1,0:T(8,128)(2,1)S(1)} %add_convert_fusion.4), channel_id=1, source_target_pairs={{0,28},{1,29},{2,30},{3,31},{4,24},{5,25},{6,26},{7,27},{8,4},{9,5... | collective-permute-start | bytes 393224 | tf_op jit(solution)/shard_map/ppermute | solution.py:356
  42.1 8.2 %collective-permute-start.12 = (bf16[16,4096]{1,0:T(8,128)(2,1)S(1)}, bf16[16,4096]{1,0:T(8,128)(2,1)S(1)}, u32[]{:S(2)}, u32[]{:S(2)}) collective-permute-start(bf16[16,4096]{1,0:T(8,128)(2,1)S(1)} %add_convert_fusion.5), channel_id=1, source_target_pairs={{0,30},{1,31},{2,28},{3,29},{4,26},{5,27},{6,24},{7,25},{8,6},{9,7... | collective-permute-start | bytes 393224 | tf_op jit(solution)/shard_map/ppermute | solution.py:356
  46.1 5.8 %collective-permute-start.17 = (bf16[16,4096]{1,0:T(8,128)(2,1)S(1)}, bf16[16,4096]{1,0:T(8,128)(2,1)S(1)}, u32[]{:S(2)}, u32[]{:S(2)}) collective-permute-start(bf16[16,4096]{1,0:T(8,128)(2,1)S(1)} %add_convert_fusion.3), channel_id=1, source_target_pairs={{0,1},{1,0},{2,3},{3,2},{4,5},{5,4},{6,7},{7,6},{8,9},{9,8},{10,11... | collective-permute-start | bytes 393224 | tf_op jit(solution)/shard_map/ppermute | solution.py:348
  52.7 5.7 %collective-permute-start.18 = (bf16[16,4096]{1,0:T(8,128)(2,1)S(1)}, bf16[16,4096]{1,0:T(8,128)(2,1)S(1)}, u32[]{:S(2)}, u32[]{:S(2)}) collective-permute-start(bf16[16,4096]{1,0:T(8,128)(2,1)S(1)} %get-tuple-element.70.refs_0_), channel_id=1, source_target_pairs={{0,1},{1,0},{2,3},{3,2},{4,5},{5,4},{6,7},{7,6},{8,9},{9,8},{10,11... | collective-permute-start | bytes 393224 | tf_op jit(solution)/shard_map/ppermute | solution.py:348
  53.4 13.8 %collective-permute-start.20 = (bf16[16,4096]{1,0:T(8,128)(2,1)S(1)}, bf16[16,4096]{1,0:T(8,128)(2,1)S(1)}, u32[]{:S(2)}, u32[]{:S(2)}) collective-permute-start(bf16[16,4096]{1,0:T(8,128)(2,1)S(1)} %get-tuple-element.70.refs_0_), channel_id=1, source_target_pairs={{0,4},{1,5},{2,6},{3,7},{4,0},{5,1},{6,2},{7,3},{8,12},{9,13},{10,... | collective-permute-start | bytes 393224 | tf_op jit(solution)/shard_map/ppermute | solution.py:348
  57.2 10.9 %collective-permute-start.22 = (bf16[16,4096]{1,0:T(8,128)(2,1)S(1)}, bf16[16,4096]{1,0:T(8,128)(2,1)S(1)}, u32[]{:S(2)}, u32[]{:S(2)}) collective-permute-start(bf16[16,4096]{1,0:T(8,128)(2,1)S(1)} %get-tuple-element.70.refs_0_), channel_id=1, source_target_pairs={{0,6},{1,7},{2,4},{3,5},{4,2},{5,3},{6,0},{7,1},{8,14},{9,15},{10,... | collective-permute-start | bytes 393224 | tf_op jit(solution)/shard_map/ppermute | solution.py:348
  58.4 16.8 %collective-permute-start.19 = (bf16[32,4096]{1,0:T(8,128)(2,1)S(1)}, bf16[32,4096]{1,0:T(8,128)(2,1)S(1)}, u32[]{:S(2)}, u32[]{:S(2)}) collective-permute-start(bf16[32,4096]{1,0:T(8,128)(2,1)S(1)} %pad_maximum_fusion.3), channel_id=1, source_target_pairs={{0,2},{1,3},{2,0},{3,1},{4,6},{5,7},{6,4},{7,5},{8,10},{9,11},{10,... | collective-permute-start | bytes 786440 | tf_op jit(solution)/shard_map/ppermute | solution.py:348
  67.3 5.0 %collective-permute-start.21 = (bf16[16,4096]{1,0:T(8,128)(2,1)S(1)}, bf16[16,4096]{1,0:T(8,128)(2,1)S(1)}, u32[]{:S(2)}, u32[]{:S(2)}) collective-permute-start(bf16[16,4096]{1,0:T(8,128)(2,1)S(1)} %collective-permute-done.20.refs_3_), channel_id=1, source_target_pairs={{0,1},{1,0},{2,3},{3,2},{4,5},{5,4},{6,7},{7,6},{8,9},{9,8},{10,11... | collective-permute-start | bytes 393224 | tf_op jit(solution)/shard_map/ppermute | solution.py:348
  68.2 5.5 %collective-permute-start.23 = (bf16[16,4096]{1,0:T(8,128)(2,1)S(1)}, bf16[16,4096]{1,0:T(8,128)(2,1)S(1)}, u32[]{:S(2)}, u32[]{:S(2)}) collective-permute-start(bf16[16,4096]{1,0:T(8,128)(2,1)S(1)} %collective-permute-done.22.refs_5_), channel_id=1, source_target_pairs={{0,1},{1,0},{2,3},{3,2},{4,5},{5,4},{6,7},{7,6},{8,9},{9,8},{10,11... | collective-permute-start | bytes 393224 | tf_op jit(solution)/shard_map/ppermute | solution.py:348
  69.3 9.8 %collective-permute-start.25 = (bf16[16,4096]{1,0:T(8,128)(2,1)S(1)}, bf16[16,4096]{1,0:T(8,128)(2,1)S(1)}, u32[]{:S(2)}, u32[]{:S(2)}) collective-permute-start(bf16[16,4096]{1,0:T(8,128)(2,1)S(1)} %get-tuple-element.73), channel_id=1, source_target_pairs={{0,2},{1,3},{2,0},{3,1},{4,6},{5,7},{6,4},{7,5},{8,10},{9,11},{10,... | collective-permute-start | bytes 393224 | tf_op jit(solution)/shard_map/ppermute | solution.py:348
  70.9 11.6 %collective-permute-start.26 = (bf16[16,4096]{1,0:T(8,128)(2,1)S(1)}, bf16[16,4096]{1,0:T(8,128)(2,1)S(1)}, u32[]{:S(2)}, u32[]{:S(2)}) collective-permute-start(bf16[16,4096]{1,0:T(8,128)(2,1)S(1)} %get-tuple-element.73), channel_id=1, source_target_pairs={{0,4},{1,5},{2,6},{3,7},{4,0},{5,1},{6,2},{7,3},{8,12},{9,13},{10,... | collective-permute-start | bytes 393224 | tf_op jit(solution)/shard_map/ppermute | solution.py:348
  72.2 10.3 %collective-permute-start.27 = (bf16[16,4096]{1,0:T(8,128)(2,1)S(1)}, bf16[16,4096]{1,0:T(8,128)(2,1)S(1)}, u32[]{:S(2)}, u32[]{:S(2)}) collective-permute-start(bf16[16,4096]{1,0:T(8,128)(2,1)S(1)} %get-tuple-element.73), channel_id=1, source_target_pairs={{0,6},{1,7},{2,4},{3,5},{4,2},{5,3},{6,0},{7,1},{8,14},{9,15},{10,... | collective-permute-start | bytes 393224 | tf_op jit(solution)/shard_map/ppermute | solution.py:348
  73.7 39.3 %collective-permute-start.38 = (bf16[4,16,4096]{2,1,0:T(8,128)(2,1)S(1)}, bf16[4,16,4096]{2,1,0:T(8,128)(2,1)S(1)}, u32[]{:S(2)}, u32[]{:S(2)}) collective-permute-start(bf16[4,16,4096]{2,1,0:T(8,128)(2,1)S(1)} %pad_maximum_fusion.refs_2_), channel_id=1, source_target_pairs={{0,1},{1,0},{2,3},{3,2},{4,5},{5,4},{6,7},{7,6},{8,9},{9,8},{10,11... | collective-permute-start | bytes 1572872 | tf_op jit(solution)/shard_map/ppermute | solution.py:348
  78.4 33.0 %copy-start = (bf16[1,2,16,4096]{3,2,1,0:T(8,128)(2,1)S(1)}, bf16[1,2,16,4096]{3,2,1,0:T(8,128)(2,1)}, u32[]{:S(2)}) copy-start(bf16[1,2,16,4096]{3,2,1,0:T(8,128)(2,1)} %param.16) | copy-start | bytes 786436
  78.4 11.5 %collective-permute-start.24 = (bf16[16,4096]{1,0:T(8,128)(2,1)S(1)}, bf16[16,4096]{1,0:T(8,128)(2,1)S(1)}, u32[]{:S(2)}, u32[]{:S(2)}) collective-permute-start(bf16[16,4096]{1,0:T(8,128)(2,1)S(1)} %get-tuple-element.72), channel_id=1, source_target_pairs={{0,1},{1,0},{2,3},{3,2},{4,5},{5,4},{6,7},{7,6},{8,9},{9,8},{10,11... | collective-permute-start | bytes 393224 | tf_op jit(solution)/shard_map/ppermute | solution.py:348
  82.6 10.2 %collective-permute-start.29 = (bf16[16,4096]{1,0:T(8,128)(2,1)S(1)}, bf16[16,4096]{1,0:T(8,128)(2,1)S(1)}, u32[]{:S(2)}, u32[]{:S(2)}) collective-permute-start(bf16[16,4096]{1,0:T(8,128)(2,1)S(1)} %get-tuple-element.76), channel_id=1, source_target_pairs={{0,1},{1,0},{2,3},{3,2},{4,5},{5,4},{6,7},{7,6},{8,9},{9,8},{10,11... | collective-permute-start | bytes 393224 | tf_op jit(solution)/shard_map/ppermute | solution.py:348
  83.6 11.5 %collective-permute-start.31 = (bf16[32,4096]{1,0:T(8,128)(2,1)S(1)}, bf16[32,4096]{1,0:T(8,128)(2,1)S(1)}, u32[]{:S(2)}, u32[]{:S(2)}) collective-permute-start(bf16[32,4096]{1,0:T(8,128)(2,1)S(1)} %get-tuple-element.78), channel_id=1, source_target_pairs={{0,2},{1,3},{2,0},{3,1},{4,6},{5,7},{6,4},{7,5},{8,10},{9,11},{10,... | collective-permute-start | bytes 786440 | tf_op jit(solution)/shard_map/ppermute | solution.py:348
  90.0 7.1 %collective-permute-start.28 = (bf16[16,4096]{1,0:T(8,128)(2,1)S(1)}, bf16[16,4096]{1,0:T(8,128)(2,1)S(1)}, u32[]{:S(2)}, u32[]{:S(2)}) collective-permute-start(bf16[16,4096]{1,0:T(8,128)(2,1)S(1)} %add_convert_fusion.2), channel_id=1, source_target_pairs={{0,6},{1,7},{2,4},{3,5},{4,2},{5,3},{6,0},{7,1},{8,14},{9,15},{10,... | collective-permute-start | bytes 393224 | tf_op jit(solution)/shard_map/ppermute | solution.py:348
  91.5 3.6 %collective-permute-start.34 = (f32[2,128]{1,0:T(2,128)S(1)}, f32[2,128]{1,0:T(2,128)S(1)}, u32[]{:S(2)}, u32[]{:S(2)}) collective-permute-start(f32[2,128]{1,0:T(2,128)S(1)} %pad_maximum_fusion.4), channel_id=1, source_target_pairs={{0,1},{1,0},{2,3},{3,2},{4,5},{5,4},{6,7},{7,6},{8,9},{9,8},{10,11... | collective-permute-start | bytes 3080 | tf_op jit(solution)/shard_map/ppermute | solution.py:348
  92.8 8.5 %collective-permute-start.30 = (bf16[16,4096]{1,0:T(8,128)(2,1)S(1)}, bf16[16,4096]{1,0:T(8,128)(2,1)S(1)}, u32[]{:S(2)}, u32[]{:S(2)}) collective-permute-start(bf16[16,4096]{1,0:T(8,128)(2,1)S(1)} %add_convert_fusion.1), channel_id=1, source_target_pairs={{0,4},{1,5},{2,6},{3,7},{4,0},{5,1},{6,2},{7,3},{8,12},{9,13},{10,... | collective-permute-start | bytes 393224 | tf_op jit(solution)/shard_map/ppermute | solution.py:348
  95.1 4.4 %collective-permute-start.33 = (bf16[16,4096]{1,0:T(8,128)(2,1)S(1)}, bf16[16,4096]{1,0:T(8,128)(2,1)S(1)}, u32[]{:S(2)}, u32[]{:S(2)}) collective-permute-start(bf16[16,4096]{1,0:T(8,128)(2,1)S(1)} %get-tuple-element.81), channel_id=1, source_target_pairs={{0,8},{1,9},{2,10},{3,11},{4,12},{5,13},{6,14},{7,15},{8,16},{9,17... | collective-permute-start | bytes 393224 | tf_op jit(solution)/shard_map/ppermute | solution.py:356
  95.1 17.9 %collective-permute-start.39 = (bf16[4,16,4096]{2,1,0:T(8,128)(2,1)S(1)}, bf16[4,16,4096]{2,1,0:T(8,128)(2,1)S(1)}, u32[]{:S(2)}, u32[]{:S(2)}) collective-permute-start(bf16[4,16,4096]{2,1,0:T(8,128)(2,1)S(1)} %pad_maximum_fusion.1.refs_4_), channel_id=1, source_target_pairs={{0,1},{1,0},{2,3},{3,2},{4,5},{5,4},{6,7},{7,6},{8,9},{9,8},{10,11... | collective-permute-start | bytes 1572872 | tf_op jit(solution)/shard_map/ppermute | solution.py:348
  97.1 14.4 %collective-permute-start.32 = (bf16[16,4096]{1,0:T(8,128)(2,1)S(1)}, bf16[16,4096]{1,0:T(8,128)(2,1)S(1)}, u32[]{:S(2)}, u32[]{:S(2)}) collective-permute-start(bf16[16,4096]{1,0:T(8,128)(2,1)S(1)} %add_convert_fusion), channel_id=1, source_target_pairs={{0,1},{1,0},{2,3},{3,2},{4,5},{5,4},{6,7},{7,6},{8,9},{9,8},{10,11... | collective-permute-start | bytes 393224 | tf_op jit(solution)/shard_map/ppermute | solution.py:348
  99.5 3.6 %collective-permute-start.35 = (f32[2,128]{1,0:T(2,128)S(1)}, f32[2,128]{1,0:T(2,128)S(1)}, u32[]{:S(2)}, u32[]{:S(2)}) collective-permute-start(f32[2,128]{1,0:T(2,128)S(1)} %add.27.refs_8_), channel_id=1, source_target_pairs={{0,2},{1,3},{2,0},{3,1},{4,6},{5,7},{6,4},{7,5},{8,10},{9,11},{10,... | collective-permute-start | bytes 3080 | tf_op jit(solution)/shard_map/ppermute | solution.py:348
  101.3 9.2 %collective-permute-start.36 = (f32[2,128]{1,0:T(2,128)S(1)}, f32[2,128]{1,0:T(2,128)S(1)}, u32[]{:S(2)}, u32[]{:S(2)}) collective-permute-start(f32[2,128]{1,0:T(2,128)S(1)} %add.27.refs_8_), channel_id=1, source_target_pairs={{0,4},{1,5},{2,6},{3,7},{4,0},{5,1},{6,2},{7,3},{8,12},{9,13},{10,... | collective-permute-start | bytes 3080 | tf_op jit(solution)/shard_map/ppermute | solution.py:348
  103.0 7.4 %collective-permute-start.37 = (f32[2,128]{1,0:T(2,128)S(1)}, f32[2,128]{1,0:T(2,128)S(1)}, u32[]{:S(2)}, u32[]{:S(2)}) collective-permute-start(f32[2,128]{1,0:T(2,128)S(1)} %add.27.refs_8_), channel_id=1, source_target_pairs={{0,6},{1,7},{2,4},{3,5},{4,2},{5,3},{6,0},{7,1},{8,14},{9,15},{10,... | collective-permute-start | bytes 3080 | tf_op jit(solution)/shard_map/ppermute | solution.py:348

commit v3 on v2

--- a/solution.py
+++ b/solution.py
@@ -67,10 +67,6 @@
     return jnp.broadcast_to(row, (128, row.shape[1])).T[:, :1]
 
 
-def as_row(column):
-    return jnp.broadcast_to(column, (column.shape[0], 128)).T[:1]
-
-
 def prepare_kernel(devices, info, hidden, gates, w_out, w_in, out_v, in_v, active_ref, scale_ref, weighted_ref, scales, sems):
     units = w_out.shape[0]
     piece = units // PIECES
@@ -123,8 +119,8 @@
 def expert_kernel(devices, inner, tick, inputs, *refs):
     chunks = refs[:inputs]
     w_out, w_in, active_ref, scale_ref = refs[inputs : inputs + 4]
-    parts = refs[inputs + 4 : -4]
-    rows_ref, hid_ref, gate_ref, sums = refs[-4:]
+    parts = refs[inputs + 4 : -3]
+    rows_ref, hid_ref, upstream_ref = refs[-3:]
     tokens = rows_ref.shape[0]
     rows = tokens // devices
     start = 0
@@ -134,8 +130,8 @@
     upstream = lax.dot_general(
         rows_ref[...], w_out[...], (((1,), (1,)), ((), ())), preferred_element_type=F32
     )
-    active = active_ref[tick]
-    hid_grad = jnp.where(active > 0, upstream * scale_ref[tick], 0.0).astype(BF16)
+    upstream_ref[...] = upstream
+    hid_grad = jnp.where(active_ref[tick] > 0, upstream * scale_ref[tick], 0.0).astype(BF16)
     width = w_in.shape[1]
     tile = column_tile(width)
     for first in range(0, width, tile):
@@ -145,13 +141,43 @@
         for ref in parts:
             ref[:, cols] = part[start : start + ref.shape[0]]
             start += ref.shape[0]
-    gate_sum = jnp.sum(active * upstream, axis=1, keepdims=True)
     outer = devices // inner
+    for k in range(devices):
+        hid_ref[k % inner * outer + k // inner] = hid_grad[k * rows : (k + 1) * rows]
+
+
+def gate_part_kernel(active, *refs):
+    upstream = refs[:-2]
+    gate_ref, products = refs[-2:]
+    ticks, tokens, units = active.shape
+    devices, rows, _ = products.shape
     me = lax.axis_index("dp")
-    for k in range(devices):
-        sums[me ^ k] = gate_sum[k * rows : (k + 1) * rows]
-        hid_ref[k % inner * outer + k // inner] = hid_grad[k * rows : (k + 1) * rows]
-    gate_ref[...] = as_row(sums[...].reshape(tokens, 1))
+    ones = jnp.ones((8, units), F32)
+    for t in range(ticks):
+        for k in range(devices):
+            own = pl.ds(k * rows, rows)
+            products[me ^ k] = active[t, own, :] * upstream[t][own, :]
+        total = lax.dot_general(
+            ones,
+            products[...].reshape(tokens, units),
+            (((1,), (1,)), ((), ())),
+            precision=lax.Precision.HIGHEST,
+            preferred_element_type=F32,
+        )
+        gate_ref[t : t + 1] = total[:1]
+
+
+def gate_part(active, upstream, devices):
+    ticks, tokens, units = active.shape
+    return pl.pallas_call(
+        gate_part_kernel,
+        in_specs=[VMEM] * (ticks + 1),
+        out_specs=VMEM,
+        out_shape=jax.ShapeDtypeStruct((ticks, tokens), F32),
+        scratch_shapes=[pltpu.VMEM((devices, tokens // devices, units), F32)],
+        compiler_params=PARAMS,
+        name="gate_part",
+    )(active, *upstream)
 
 
 def expert(tick, chunks, w_out, w_in, active, scale, devices, inner):
@@ -167,9 +193,8 @@
         + [
             jax.ShapeDtypeStruct((tokens, width), BF16),
             jax.ShapeDtypeStruct((devices, rows, units), BF16),
-            jax.ShapeDtypeStruct((1, tokens), F32),
+            jax.ShapeDtypeStruct((tokens, units), F32),
         ],
-        scratch_shapes=[pltpu.VMEM((devices, rows, 1), F32)],
         compiler_params=PARAMS,
         cost_estimate=pl.CostEstimate(
             flops=4 * tokens * units * width, bytes_accessed=2 * 2**20, transcendentals=0
@@ -182,13 +207,10 @@
     tile = bufs.shape[2]
     copies = []
     for step, start in enumerate(range(first, last, tile)):
-        buf = step % 2
-        if step >= 2:
-            copies[step - 2].wait()
-        bufs[buf] = jnp.dot(left_ref[...], right_of(start, tile), preferred_element_type=F32).astype(BF16)
-        copies.append(pltpu.make_async_copy(bufs.at[buf], out.at[:, pl.ds(start, tile)], sems.at[buf]))
+        bufs[step] = jnp.dot(left_ref[...], right_of(start, tile), preferred_element_type=F32).astype(BF16)
+        copies.append(pltpu.make_async_copy(bufs.at[step], out.at[:, pl.ds(start, tile)], sems.at[step]))
         copies[-1].start()
-    for copy in copies[max(len(copies) - 2, 0) :]:
+    for copy in copies:
         copy.wait()
 
 
@@ -232,6 +254,7 @@
 def grad_call(kernel, shape, depth, columns, args, name, scratch=(), scalars=0, onto=None):
     units, width = shape
     tile = column_tile(columns[1] - columns[0])
+    steps = (columns[1] - columns[0]) // tile
     more = [] if onto is None else [onto]
     return pl.pallas_call(
         kernel,
@@ -241,8 +264,8 @@
         scratch_shapes=list(scratch)
         + [
             pltpu.VMEM((units, depth), BF16),
-            pltpu.VMEM((2, units, tile), BF16),
-            pltpu.SemaphoreType.DMA((2,)),
+            pltpu.VMEM((steps, units, tile), BF16),
+            pltpu.SemaphoreType.DMA((steps,)),
         ],
         input_output_aliases={len(args): 0} if more else {},
         compiler_params=PARAMS,
@@ -384,6 +407,8 @@
                 after(info, mine[-1]), hidden, gate_stash, w_out[0], w_in[0]
             )
             column[far[-1]] = after(column[far[-1]], active)
+        if t > 0:
+            column[far[-1]] = after(column[far[-1]], saved[-1])
         chunks = {a: along_inner(column[a]) for a in far}
         stash = None
         if t == 0 or last:
@@ -416,6 +441,12 @@
             pieces_a = parts[2 + (a - 2) * inner :][:inner]
             got = [swap(pieces_a[b], b).astype(F32) for b in range(1, inner)]
             sums[a] = sum(got, pieces_a[0].astype(F32)).astype(BF16)
+        if last:
+            gate = gate_part(active, gate_parts, devices)
+            step = 1
+            while step < inner:
+                gate = gate + swap(gate, step)
+                step *= 2
         crossing = [
             swap((kept[b * rows :][:rows].astype(F32) + direct[b * rows :][:rows].astype(F32)).astype(BF16), b)
             for b in range(1, inner)
@@ -423,7 +454,9 @@
         if stash is not None:
             stash = jnp.stack(stash)
             sums[far[0]], stash = lax.optimization_barrier((sums[far[0]], stash))
-            saved += along_inner(after(stash, sums[far[-1]]))
+            late = after(stash, sums[far[-1]])
+            if last:
+                saved += along_inner(after(late, gate))
         totals = [send(sums[a], a * inner) for a in far] + [kept, direct] + crossing
         if not last:
             above_done, following, own = hand_on(
@@ -431,13 +464,9 @@
             )
             done.append(above_done)
             incoming.append(following)
+            saved += along_inner(after(late, own))
     done = [shift(after(value, sums[far[-1]]), 1) for value in done]
     depth = ticks * tokens
-    gate = after(jnp.concatenate(gate_parts), sums[far[0]])
-    step = 1
-    while step < inner:
-        gate = gate + swap(gate, step)
-        step *= 2
     rows_list[-1] = after(rows_list[-1], done[0])
     grad_out = grad_call(
         functools.partial(grad_out_kernel, 0, width),
@@ -447,7 +476,7 @@
         (weighted, *rows_list),
         "grad_out",
     )
-    gate = after(gate, totals[0])
+    gate = after(gate, direct)
     gates = [gate] + [swap(gate, a * inner) for a in range(1, outer)]
     grad_in = grad_call(
         functools.partial(grad_in_kernel, ticks, inner, pieces, 0, width),

time: 120 us -> 112 us (0.933); the launches traced: 119 us -> 112 us
  waiting for transfers between devices: 36.7 us -> 32 us
  Pallas kernels: 25.8 us -> 22 us
  starting transfers between devices: 53.3 us -> 55 us
    pallas_call x2, Pallas kernels: 10.7 us -> 6.14 us  [grad_call(): pl.pallas_call(kernel, in_specs=[SMEM] * scalars + [VMEM] * (len(args) -...]
    ppermute x33, waiting for transfers between devices: 29.9 us -> 26.2 us  [swap(): return lax.ppermute(value, 'dp', [(i, i ^ step) for i in range(devices)])]
    ppermute x7, starting transfers between devices: 7.84 us -> 9.69 us  [shift(): return lax.ppermute(value, ('section', 'dp'), route)]
  transfers between devices with their start and end apart: 40 -> 40, of which waited for: 17 -> 14; matrix products, arithmetic and copies ran while one was open for 0% -> 0% of each run, Pallas kernels for 15% -> 15%
where the time goes in v3:
time: 112 us
  starting transfers between devices  55 us (49%)
  waiting for transfers between devices  32 us (29%)
  Pallas kernels  22 us (20%)
  local copies, waits for them, and re-layouts  1.68 us (2%)
    ppermute x33, starting transfers between devices, swap(): return lax.ppermute(value, 'dp', [(i, i ^ step) for i in range(devices)])  45.3 us
    ppermute x33, waiting for transfers between devices, swap(): return lax.ppermute(value, 'dp', [(i, i ^ step) for i in range(devices)])  26.2 us
    ppermute x7, starting transfers between devices, shift(): return lax.ppermute(value, ('section', 'dp'), route)  9.69 us
    pallas_call x2, Pallas kernels, expert(): pl.pallas_call(functools.partial(expert_kernel, devices, inner, tick, len...  6.43 us
    pallas_call x2, Pallas kernels, grad_call(): pl.pallas_call(kernel, in_specs=[SMEM] * scalars + [VMEM] * (len(args) -...  6.14 us
    ppermute x7, waiting for transfers between devices, shift(): return lax.ppermute(value, ('section', 'dp'), route)  5.85 us
    pallas_call x1, Pallas kernels, prepare(): pl.pallas_call(functools.partial(prepare_kernel, devices), in_specs=[SMEM...  4.77 us
  transfers between devices with their start and end apart: 40, of which 14 were waited for; matrix products, arithmetic and copies ran while one was open for 0% of the time, Pallas kernels for 15%

profile of v3, /device:TPU:0, one launch (start us, length us, event | category | flops | bytes accessed | tf_op | source)
XLA Modules:
  0.0 112.0 jit_solution(5508796487620620057)
XLA Ops:
  0.6 1.6 %pick.1 = (bf16[16,4096]{1,0:T(8,128)(2,1)S(1)}, s32[4]{0:T(128)S(1)}) custom-call(s32[1,2]{1,0:T(1,128)} %slot_hbm.1, s32[1,2]{1,0:T(1,128)} %block_hbm.1, bf16[2,16,4096]{2,1,0:T(8,128)(2,1)} %bitcast.21), custom_call_target="tpu_custom_call" | custom-call | tf_op jit(solution)/shard_map/pick/pallas_call | solution.py:44
  2.2 3.0 %collective-permute-start.1 = (bf16[16,4096]{1,0:T(8,128)(2,1)S(1)}, bf16[16,4096]{1,0:T(8,128)(2,1)S(1)}, u32[]{:S(2)}, u32[]{:S(2)}) collective-permute-start(bf16[16,4096]{1,0:T(8,128)(2,1)S(1)} %get-tuple-element.54.refs_0_), channel_id=1, source_target_pairs={{0,1},{1,0},{2,3},{3,2},{4,5},{5,4},{6,7},{7,6},{8,9},{9,8},{10,11... | collective-permute-start | bytes 393224 | tf_op jit(solution)/shard_map/ppermute | solution.py:371
  5.2 2.6 %collective-permute-start.4 = (bf16[16,4096]{1,0:T(8,128)(2,1)S(1)}, bf16[16,4096]{1,0:T(8,128)(2,1)S(1)}, u32[]{:S(2)}, u32[]{:S(2)}) collective-permute-start(bf16[16,4096]{1,0:T(8,128)(2,1)S(1)} %get-tuple-element.54.refs_0_), channel_id=1, source_target_pairs={{0,4},{1,5},{2,6},{3,7},{4,0},{5,1},{6,2},{7,3},{8,12},{9,13},{10,... | collective-permute-start | bytes 393224 | tf_op jit(solution)/shard_map/ppermute | solution.py:371
  7.8 1.3 %collective-permute-start.6 = (bf16[16,4096]{1,0:T(8,128)(2,1)S(1)}, bf16[16,4096]{1,0:T(8,128)(2,1)S(1)}, u32[]{:S(2)}, u32[]{:S(2)}) collective-permute-start(bf16[16,4096]{1,0:T(8,128)(2,1)S(1)} %get-tuple-element.54.refs_0_), channel_id=1, source_target_pairs={{0,6},{1,7},{2,4},{3,5},{4,2},{5,3},{6,0},{7,1},{8,14},{9,15},{10,... | collective-permute-start | bytes 393224 | tf_op jit(solution)/shard_map/ppermute | solution.py:371
  9.3 1.5 %collective-permute-start.3 = (bf16[2,16,4096]{2,1,0:T(8,128)(2,1)}, bf16[2,16,4096]{2,1,0:T(8,128)(2,1)S(1)}, u32[]{:S(2)}, u32[]{:S(2)}) collective-permute-start(bf16[2,16,4096]{2,1,0:T(8,128)(2,1)} %bitcast.22), channel_id=1, source_target_pairs={{0,24},{1,25},{2,26},{3,27},{4,28},{5,29},{6,30},{7,31},{8,0},{9,1... | collective-permute-start | bytes 786440 | tf_op jit(solution)/shard_map/ppermute | solution.py:379
  11.1 1.0 copy-done.1
  12.8 4.8 %prepare.1 = (bf16[640,4096]{1,0:T(8,128)(2,1)S(1)}, bf16[640,4096]{1,0:T(8,128)(2,1)S(1)}, f32[2,128,640]{2,1,0:T(8,128)S(1)}, f32[2,128,1]{2,1,0:T(8,128)S(1)}, bf16[2,128,640]{2,1,0:T(8,128)(2,1)S(1)}) custom-call(s32[4]{0:T(128)S(1)} %get-tuple-element.58.info, bf16[2,8,16,640]{3,2,1,0:T(8,128)(2,1)S(1)} %bitcast.24, f32[1,2,128]{2,1,0:T(2,128)S(1)} %copy-done.3, ...), custom_call_target="tpu_custom_call" | custom-call | flops 327680 | bytes 10485760 | tf_op jit(solution)/shard_map/prepare/pallas_call | solution.py:99
  17.9 0.7 collective-permute-start.5
  18.6 1.3 %collective-permute-start.7 = (bf16[16,4096]{1,0:T(8,128)(2,1)S(1)}, bf16[16,4096]{1,0:T(8,128)(2,1)S(1)}, u32[]{:S(2)}, u32[]{:S(2)}) collective-permute-start(bf16[16,4096]{1,0:T(8,128)(2,1)S(1)} %collective-permute-done.6.refs_5_), channel_id=1, source_target_pairs={{0,1},{1,0},{2,3},{3,2},{4,5},{5,4},{6,7},{7,6},{8,9},{9,8},{10,11... | collective-permute-start | bytes 393224 | tf_op jit(solution)/shard_map/ppermute | solution.py:371
  20.0 1.6 %collective-permute-start.9 = (bf16[16,4096]{1,0:T(8,128)(2,1)S(1)}, bf16[16,4096]{1,0:T(8,128)(2,1)S(1)}, u32[]{:S(2)}, u32[]{:S(2)}) collective-permute-start(bf16[16,4096]{1,0:T(8,128)(2,1)S(1)} %get-tuple-element.66), channel_id=1, source_target_pairs={{0,2},{1,3},{2,0},{3,1},{4,6},{5,7},{6,4},{7,5},{8,10},{9,11},{10,... | collective-permute-start | bytes 393224 | tf_op jit(solution)/shard_map/ppermute | solution.py:371
  21.5 1.7 %collective-permute-start.10 = (bf16[16,4096]{1,0:T(8,128)(2,1)S(1)}, bf16[16,4096]{1,0:T(8,128)(2,1)S(1)}, u32[]{:S(2)}, u32[]{:S(2)}) collective-permute-start(bf16[16,4096]{1,0:T(8,128)(2,1)S(1)} %get-tuple-element.66), channel_id=1, source_target_pairs={{0,4},{1,5},{2,6},{3,7},{4,0},{5,1},{6,2},{7,3},{8,12},{9,13},{10,... | collective-permute-start | bytes 393224 | tf_op jit(solution)/shard_map/ppermute | solution.py:371
  23.2 2.3 %collective-permute-start.11 = (bf16[16,4096]{1,0:T(8,128)(2,1)S(1)}, bf16[16,4096]{1,0:T(8,128)(2,1)S(1)}, u32[]{:S(2)}, u32[]{:S(2)}) collective-permute-start(bf16[16,4096]{1,0:T(8,128)(2,1)S(1)} %get-tuple-element.66), channel_id=1, source_target_pairs={{0,6},{1,7},{2,4},{3,5},{4,2},{5,3},{6,0},{7,1},{8,14},{9,15},{10,... | collective-permute-start | bytes 393224 | tf_op jit(solution)/shard_map/ppermute | solution.py:371
  25.5 3.2 %expert_tick.2 = (bf16[32,4096]{1,0:T(8,128)(2,1)S(1)}, bf16[32,4096]{1,0:T(8,128)(2,1)S(1)}, bf16[16,4096]{1,0:T(8,128)(2,1)S(1)}, bf16[16,4096]{1,0:T(8,128)(2...) custom-call(bf16[16,4096]{1,0:T(8,128)(2,1)S(1)} %get-tuple-element., ...), custom_call_target="tpu_custom_call" | custom-call | flops 1342177280 | bytes 2097152 | tf_op jit(solution)/shard_map/expert_tick/pallas_call | solution.py:188
  29.2 5.3 %collective-permute-done.10 = bf16[16,4096]{1,0:T(8,128)(2,1)S(1)} collective-permute-done((bf16[16,4096]{1,0:T(8,128)(2,1)S(1)}, bf16[16,4096]{1,0:T(8,128)(2,1)S(1)}, u32[]{:S(2)}, u32[]{:S(2)}) %collective-permute-start.10) | collective-permute-done | bytes 131104 | tf_op jit(solution)/shard_map/ppermute | solution.py:371
  34.7 3.7 %collective-permute-start.16 = (bf16[32,4096]{1,0:T(8,128)(2,1)S(1)}, bf16[32,4096]{1,0:T(8,128)(2,1)S(1)}, u32[]{:S(2)}, u32[]{:S(2)}) collective-permute-start(bf16[32,4096]{1,0:T(8,128)(2,1)S(1)} %get-tuple-element.71), channel_id=1, source_target_pairs={{0,26},{1,27},{2,24},{3,25},{4,30},{5,31},{6,28},{7,29},{8,2},{9,3... | collective-permute-start | bytes 786440 | tf_op jit(solution)/shard_map/ppermute | solution.py:379
  38.5 1.1 collective-permute-done.8
  39.6 1.7 %collective-permute-start.14 = (bf16[16,4096]{1,0:T(8,128)(2,1)S(1)}, bf16[16,4096]{1,0:T(8,128)(2,1)S(1)}, u32[]{:S(2)}, u32[]{:S(2)}) collective-permute-start(bf16[16,4096]{1,0:T(8,128)(2,1)S(1)} %add_convert_fusion.4), channel_id=1, source_target_pairs={{0,28},{1,29},{2,30},{3,31},{4,24},{5,25},{6,26},{7,27},{8,4},{9,5... | collective-permute-start | bytes 393224 | tf_op jit(solution)/shard_map/ppermute | solution.py:379
  41.3 2.7 %collective-permute-start.12 = (bf16[16,4096]{1,0:T(8,128)(2,1)S(1)}, bf16[16,4096]{1,0:T(8,128)(2,1)S(1)}, u32[]{:S(2)}, u32[]{:S(2)}) collective-permute-start(bf16[16,4096]{1,0:T(8,128)(2,1)S(1)} %add_convert_fusion.5), channel_id=1, source_target_pairs={{0,30},{1,31},{2,28},{3,29},{4,26},{5,27},{6,24},{7,25},{8,6},{9,7... | collective-permute-start | bytes 393224 | tf_op jit(solution)/shard_map/ppermute | solution.py:379
  43.9 1.9 %collective-permute-done.16.refs_3_ = bf16[32,4096]{1,0:T(8,128)(2,1)S(1)} collective-permute-done((bf16[32,4096]{1,0:T(8,128)(2,1)S(1)}, bf16[32,4096]{1,0:T(8,128)(2,1)S(1)}, u32[]{:S(2)}, u32[]{:S(2)}) %collective-permute-start.16) | collective-permute-done | bytes 262176 | tf_op jit(solution)/shard_map/ppermute | solution.py:379
  45.9 1.5 %collective-permute-start.17 = (bf16[16,4096]{1,0:T(8,128)(2,1)S(1)}, bf16[16,4096]{1,0:T(8,128)(2,1)S(1)}, u32[]{:S(2)}, u32[]{:S(2)}) collective-permute-start(bf16[16,4096]{1,0:T(8,128)(2,1)S(1)} %add_convert_fusion.3), channel_id=1, source_target_pairs={{0,1},{1,0},{2,3},{3,2},{4,5},{5,4},{6,7},{7,6},{8,9},{9,8},{10,11... | collective-permute-start | bytes 393224 | tf_op jit(solution)/shard_map/ppermute | solution.py:371
  47.4 3.9 %collective-permute-done.12.refs_0_ = bf16[16,4096]{1,0:T(8,128)(2,1)S(1)} collective-permute-done((bf16[16,4096]{1,0:T(8,128)(2,1)S(1)}, bf16[16,4096]{1,0:T(8,128)(2,1)S(1)}, u32[]{:S(2)}, u32[]{:S(2)}) %collective-permute-start.12) | collective-permute-done | bytes 131104 | tf_op jit(solution)/shard_map/ppermute | solution.py:379
  51.3 0.7 hand_on.1
  52.0 2.5 %collective-permute-start.18 = (bf16[16,4096]{1,0:T(8,128)(2,1)S(1)}, bf16[16,4096]{1,0:T(8,128)(2,1)S(1)}, u32[]{:S(2)}, u32[]{:S(2)}) collective-permute-start(bf16[16,4096]{1,0:T(8,128)(2,1)S(1)} %get-tuple-element.72.refs_0_), channel_id=1, source_target_pairs={{0,1},{1,0},{2,3},{3,2},{4,5},{5,4},{6,7},{7,6},{8,9},{9,8},{10,11... | collective-permute-start | bytes 393224 | tf_op jit(solution)/shard_map/ppermute | solution.py:371
  54.5 3.0 %collective-permute-start.20 = (bf16[16,4096]{1,0:T(8,128)(2,1)S(1)}, bf16[16,4096]{1,0:T(8,128)(2,1)S(1)}, u32[]{:S(2)}, u32[]{:S(2)}) collective-permute-start(bf16[16,4096]{1,0:T(8,128)(2,1)S(1)} %get-tuple-element.72.refs_0_), channel_id=1, source_target_pairs={{0,4},{1,5},{2,6},{3,7},{4,0},{5,1},{6,2},{7,3},{8,12},{9,13},{10,... | collective-permute-start | bytes 393224 | tf_op jit(solution)/shard_map/ppermute | solution.py:371
  58.0 1.9 %collective-permute-start.21 = (bf16[4,16,4096]{2,1,0:T(8,128)(2,1)S(1)}, bf16[4,16,4096]{2,1,0:T(8,128)(2,1)S(1)}, u32[]{:S(2)}, u32[]{:S(2)}) collective-permute-start(bf16[4,16,4096]{2,1,0:T(8,128)(2,1)S(1)} %pad_maximum_fusion.refs_2_), channel_id=1, source_target_pairs={{0,1},{1,0},{2,3},{3,2},{4,5},{5,4},{6,7},{7,6},{8,9},{9,8},{10,11... | collective-permute-start | bytes 1572872 | tf_op jit(solution)/shard_map/ppermute | solution.py:371
  60.0 1.7 %collective-permute-start.19 = (bf16[32,4096]{1,0:T(8,128)(2,1)S(1)}, bf16[32,4096]{1,0:T(8,128)(2,1)S(1)}, u32[]{:S(2)}, u32[]{:S(2)}) collective-permute-start(bf16[32,4096]{1,0:T(8,128)(2,1)S(1)} %pad_maximum_fusion.3), channel_id=1, source_target_pairs={{0,2},{1,3},{2,0},{3,1},{4,6},{5,7},{6,4},{7,5},{8,10},{9,11},{10,... | collective-permute-start | bytes 786440 | tf_op jit(solution)/shard_map/ppermute | solution.py:371
  61.7 4.2 %collective-permute-done.23.refs_5_ = bf16[16,4096]{1,0:T(8,128)(2,1)S(1)} collective-permute-done((bf16[16,4096]{1,0:T(8,128)(2,1)S(1)}, bf16[16,4096]{1,0:T(8,128)(2,1)S(1)}, u32[]{:S(2)}, u32[]{:S(2)}) %collective-permute-start.23) | collective-permute-done | bytes 131104 | tf_op jit(solution)/shard_map/ppermute | solution.py:371
  65.8 1.1 %collective-permute-start.24 = (bf16[16,4096]{1,0:T(8,128)(2,1)S(1)}, bf16[16,4096]{1,0:T(8,128)(2,1)S(1)}, u32[]{:S(2)}, u32[]{:S(2)}) collective-permute-start(bf16[16,4096]{1,0:T(8,128)(2,1)S(1)} %collective-permute-done.23.refs_5_), channel_id=1, source_target_pairs={{0,1},{1,0},{2,3},{3,2},{4,5},{5,4},{6,7},{7,6},{8,9},{9,8},{10,11... | collective-permute-start | bytes 393224 | tf_op jit(solution)/shard_map/ppermute | solution.py:371
  67.5 5.3 %collective-permute-done.21.refs_3_ = bf16[4,16,4096]{2,1,0:T(8,128)(2,1)S(1)} collective-permute-done((bf16[4,16,4096]{2,1,0:T(8,128)(2,1)S(1)}, bf16[4,16,4096]{2,1,0:T(8,128)(2,1)S(1)}, u32[]{:S(2)}, u32[]{:S(2)}) %collective-permute-start.21) | collective-permute-done | bytes 524320 | tf_op jit(solution)/shard_map/ppermute | solution.py:371
  72.7 1.7 %collective-permute-start.22 = (bf16[16,4096]{1,0:T(8,128)(2,1)S(1)}, bf16[16,4096]{1,0:T(8,128)(2,1)S(1)}, u32[]{:S(2)}, u32[]{:S(2)}) collective-permute-start(bf16[16,4096]{1,0:T(8,128)(2,1)S(1)} %collective-permute-done.20.refs_3_), channel_id=1, source_target_pairs={{0,1},{1,0},{2,3},{3,2},{4,5},{5,4},{6,7},{7,6},{8,9},{9,8},{10,11... | collective-permute-start | bytes 393224 | tf_op jit(solution)/shard_map/ppermute | solution.py:371
  74.4 3.5 %collective-permute-start.27 = (bf16[16,4096]{1,0:T(8,128)(2,1)S(1)}, bf16[16,4096]{1,0:T(8,128)(2,1)S(1)}, u32[]{:S(2)}, u32[]{:S(2)}) collective-permute-start(bf16[16,4096]{1,0:T(8,128)(2,1)S(1)} %get-tuple-element.79), channel_id=1, source_target_pairs={{0,4},{1,5},{2,6},{3,7},{4,0},{5,1},{6,2},{7,3},{8,12},{9,13},{10,... | collective-permute-start | bytes 393224 | tf_op jit(solution)/shard_map/ppermute | solution.py:371
  77.9 0.9 collective-permute-start.28
  78.8 3.2 %expert_tick.3 = (bf16[32,4096]{1,0:T(8,128)(2,1)S(1)}, bf16[32,4096]{1,0:T(8,128)(2,1)S(1)}, bf16[16,4096]{1,0:T(8,128)(2,1)S(1)}, bf16[16,4096]{1,0:T(8,128)(2...) custom-call(bf16[16,4096]{1,0:T(8,128)(2,1)S(1)} %get-tuple-element., ...), custom_call_target="tpu_custom_call" | custom-call | flops 1342177280 | bytes 2097152 | tf_op jit(solution)/shard_map/expert_tick/pallas_call | solution.py:188
  82.0 0.7 collective-permute-start.30
  82.7 1.4 %collective-permute-start.25 = (bf16[16,4096]{1,0:T(8,128)(2,1)S(1)}, bf16[16,4096]{1,0:T(8,128)(2,1)S(1)}, u32[]{:S(2)}, u32[]{:S(2)}) collective-permute-start(bf16[16,4096]{1,0:T(8,128)(2,1)S(1)} %get-tuple-element.78), channel_id=1, source_target_pairs={{0,1},{1,0},{2,3},{3,2},{4,5},{5,4},{6,7},{7,6},{8,9},{9,8},{10,11... | collective-permute-start | bytes 393224 | tf_op jit(solution)/shard_map/ppermute | solution.py:371
  84.1 0.8 gate_part.1
  85.8 2.9 %collective-permute-done.35 = f32[2,128]{1,0:T(2,128)S(1)} collective-permute-done((f32[2,128]{1,0:T(2,128)S(1)}, f32[2,128]{1,0:T(2,128)S(1)}, u32[]{:S(2)}, u32[]{:S(2)}) %collective-permute-start.35) | collective-permute-done | bytes 1056 | tf_op jit(solution)/shard_map/ppermute | solution.py:371
  88.7 0.8 collective-permute-start.31
  89.6 1.4 %collective-permute-start.39 = (bf16[4,16,4096]{2,1,0:T(8,128)(2,1)S(1)}, bf16[4,16,4096]{2,1,0:T(8,128)(2,1)S(1)}, u32[]{:S(2)}, u32[]{:S(2)}) collective-permute-start(bf16[4,16,4096]{2,1,0:T(8,128)(2,1)S(1)} %pad_maximum_fusion.1.refs_4_), channel_id=1, source_target_pairs={{0,1},{1,0},{2,3},{3,2},{4,5},{5,4},{6,7},{7,6},{8,9},{9,8},{10,11... | collective-permute-start | bytes 1572872 | tf_op jit(solution)/shard_map/ppermute | solution.py:371
  91.0 1.8 %collective-permute-start.29 = (bf16[16,4096]{1,0:T(8,128)(2,1)S(1)}, bf16[16,4096]{1,0:T(8,128)(2,1)S(1)}, u32[]{:S(2)}, u32[]{:S(2)}) collective-permute-start(bf16[16,4096]{1,0:T(8,128)(2,1)S(1)} %add_convert_fusion.2), channel_id=1, source_target_pairs={{0,6},{1,7},{2,4},{3,5},{4,2},{5,3},{6,0},{7,1},{8,14},{9,15},{10,... | collective-permute-start | bytes 393224 | tf_op jit(solution)/shard_map/ppermute | solution.py:371
  92.8 1.2 %collective-permute-done.32.refs_3_ = bf16[32,4096]{1,0:T(8,128)(2,1)S(1)} collective-permute-done((bf16[32,4096]{1,0:T(8,128)(2,1)S(1)}, bf16[32,4096]{1,0:T(8,128)(2,1)S(1)}, u32[]{:S(2)}, u32[]{:S(2)}) %collective-permute-start.32) | collective-permute-done | bytes 262176 | tf_op jit(solution)/shard_map/ppermute | solution.py:371
  94.1 1.7 %collective-permute-start.33 = (bf16[16,4096]{1,0:T(8,128)(2,1)S(1)}, bf16[16,4096]{1,0:T(8,128)(2,1)S(1)}, u32[]{:S(2)}, u32[]{:S(2)}) collective-permute-start(bf16[16,4096]{1,0:T(8,128)(2,1)S(1)} %add_convert_fusion), channel_id=1, source_target_pairs={{0,1},{1,0},{2,3},{3,2},{4,5},{5,4},{6,7},{7,6},{8,9},{9,8},{10,11... | collective-permute-start | bytes 393224 | tf_op jit(solution)/shard_map/ppermute | solution.py:371
  96.9 2.3 %collective-permute-done.29.refs_0_ = bf16[16,4096]{1,0:T(8,128)(2,1)S(1)} collective-permute-done((bf16[16,4096]{1,0:T(8,128)(2,1)S(1)}, bf16[16,4096]{1,0:T(8,128)(2,1)S(1)}, u32[]{:S(2)}, u32[]{:S(2)}) %collective-permute-start.29) | collective-permute-done | bytes 131104 | tf_op jit(solution)/shard_map/ppermute | solution.py:371
  99.2 1.9 %collective-permute-start.38 = (f32[2,128]{1,0:T(2,128)S(1)}, f32[2,128]{1,0:T(2,128)S(1)}, u32[]{:S(2)}, u32[]{:S(2)}) collective-permute-start(f32[2,128]{1,0:T(2,128)S(1)} %add.27.refs_8_), channel_id=1, source_target_pairs={{0,6},{1,7},{2,4},{3,5},{4,2},{5,3},{6,0},{7,1},{8,14},{9,15},{10,... | collective-permute-start | bytes 3080 | tf_op jit(solution)/shard_map/ppermute | solution.py:371
  101.1 2.8 %grad_out.1 = bf16[640,4096]{1,0:T(8,128)(2,1)} custom-call(bf16[2,128,640]{2,1,0:T(8,128)(2,1)S(1)} %get-tuple-element.97.weighted, bf16[128,4096]{1,0:T(8,128)(2,1)S(1)} %get-tuple-element.98.refs_0_, bf16[128,4096]{1,0:T(8,128)(2,1)S(1)} %get-tuple-element.100.refs_1_), custom_call_target="tpu_custom_call" | custom-call | flops 1342177280 | bytes 5242880 | tf_op jit(solution)/shard_map/grad_out/pallas_call | solution.py:259
  104.6 2.4 %collective-permute-done.33.refs_4_ = bf16[16,4096]{1,0:T(8,128)(2,1)S(1)} collective-permute-done((bf16[16,4096]{1,0:T(8,128)(2,1)S(1)}, bf16[16,4096]{1,0:T(8,128)(2,1)S(1)}, u32[]{:S(2)}, u32[]{:S(2)}) %collective-permute-start.33) | collective-permute-done | bytes 131104 | tf_op jit(solution)/shard_map/ppermute | solution.py:371
  107.0 1.5 %finish.1 = (bf16[2,2,16,4096]{3,2,1,0:T(8,128)(2,1)}, f32[2,1,128]{2,1,0:T(1,128)}) custom-call(s32[4]{0:T(128)S(1)} %get-tuple-element.58.info, bf16[16,4096]{1,0:T(8,128)(2,1)S(1)} %collective-permute-done.29.refs_0_, bf16[16,4096]{1,0:T(8,128)(2,1)S(1)} %collective-permute-done.31.refs_1_, bf16[32,4096]{1,0:T(8,128)(2,1)S(1)} %get-tuple-element.83.refs_2_, ...), custom_call_target="tpu_custom_call" | custom-call | tf_op jit(solution)/shard_map/finish/pallas_call | solution.py:340
  108.5 3.4 %grad_in.1 = bf16[640,4096]{1,0:T(8,128)(2,1)} custom-call(s32[4]{0:T(128)S(1)} %get-tuple-element.58.info, bf16[8,16,640]{2,1,0:T(8,128)(2,1)S(1)} %get-tuple-element.92.refs_0_, bf16[8,16,640]{2,1,0:T(8,128)(2,1)S(1)} %get-tuple-element.93.refs_1_, bf16[4,16,4096]{2,1,0:T(8,128)(2,1)S(1)} %pad_maximum_fusion.refs_2_, ...), custom_call_target="tpu_custom_call" | custom-call | flops 1342177280 | bytes 5242880 | tf_op jit(solution)/shard_map/grad_in/pallas_call | solution.py:259
  (63 shorter events, 6.1 us)
Async XLA Ops:
  2.2 8.6 %collective-permute-start.1 = (bf16[16,4096]{1,0:T(8,128)(2,1)S(1)}, bf16[16,4096]{1,0:T(8,128)(2,1)S(1)}, u32[]{:S(2)}, u32[]{:S(2)}) collective-permute-start(bf16[16,4096]{1,0:T(8,128)(2,1)S(1)} %get-tuple-element.54.refs_0_), channel_id=1, source_target_pairs={{0,1},{1,0},{2,3},{3,2},{4,5},{5,4},{6,7},{7,6},{8,9},{9,8},{10,11... | collective-permute-start | bytes 393224 | tf_op jit(solution)/shard_map/ppermute | solution.py:371
  5.2 12.7 %collective-permute-start.4 = (bf16[16,4096]{1,0:T(8,128)(2,1)S(1)}, bf16[16,4096]{1,0:T(8,128)(2,1)S(1)}, u32[]{:S(2)}, u32[]{:S(2)}) collective-permute-start(bf16[16,4096]{1,0:T(8,128)(2,1)S(1)} %get-tuple-element.54.refs_0_), channel_id=1, source_target_pairs={{0,4},{1,5},{2,6},{3,7},{4,0},{5,1},{6,2},{7,3},{8,12},{9,13},{10,... | collective-permute-start | bytes 393224 | tf_op jit(solution)/shard_map/ppermute | solution.py:371
  7.8 10.8 %collective-permute-start.6 = (bf16[16,4096]{1,0:T(8,128)(2,1)S(1)}, bf16[16,4096]{1,0:T(8,128)(2,1)S(1)}, u32[]{:S(2)}, u32[]{:S(2)}) collective-permute-start(bf16[16,4096]{1,0:T(8,128)(2,1)S(1)} %get-tuple-element.54.refs_0_), channel_id=1, source_target_pairs={{0,6},{1,7},{2,4},{3,5},{4,2},{5,3},{6,0},{7,1},{8,14},{9,15},{10,... | collective-permute-start | bytes 393224 | tf_op jit(solution)/shard_map/ppermute | solution.py:371
  9.2 10.8 %collective-permute-start = (s32[4]{0:T(128)S(1)}, s32[4]{0:T(128)S(1)}, u32[]{:S(2)}, u32[]{:S(2)}) collective-permute-start(s32[4]{0:T(128)S(1)} %get-tuple-element.58.info), channel_id=1, source_target_pairs={{0,24},{1,25},{2,26},{3,27},{4,28},{5,29},{6,30},{7,31},{8,0},{9,1... | collective-permute-start | bytes 56 | tf_op jit(solution)/shard_map/ppermute | solution.py:379
  9.3 12.3 %collective-permute-start.3 = (bf16[2,16,4096]{2,1,0:T(8,128)(2,1)}, bf16[2,16,4096]{2,1,0:T(8,128)(2,1)S(1)}, u32[]{:S(2)}, u32[]{:S(2)}) collective-permute-start(bf16[2,16,4096]{2,1,0:T(8,128)(2,1)} %bitcast.22), channel_id=1, source_target_pairs={{0,24},{1,25},{2,26},{3,27},{4,28},{5,29},{6,30},{7,31},{8,0},{9,1... | collective-permute-start | bytes 786440 | tf_op jit(solution)/shard_map/ppermute | solution.py:379
  10.8 12.4 %collective-permute-start.2 = (bf16[32,4096]{1,0:T(8,128)(2,1)S(1)}, bf16[32,4096]{1,0:T(8,128)(2,1)S(1)}, u32[]{:S(2)}, u32[]{:S(2)}) collective-permute-start(bf16[32,4096]{1,0:T(8,128)(2,1)S(1)} %pad_maximum_fusion.2), channel_id=1, source_target_pairs={{0,2},{1,3},{2,0},{3,1},{4,6},{5,7},{6,4},{7,5},{8,10},{9,11},{10,... | collective-permute-start | bytes 786440 | tf_op jit(solution)/shard_map/ppermute | solution.py:371
  11.1 1.0 copy-start.1
  12.1 0.7 copy-start.3
  12.8 7.2 %copy-start.4 = (bf16[1,2,16,4096]{3,2,1,0:T(8,128)(2,1)S(1)}, bf16[1,2,16,4096]{3,2,1,0:T(8,128)(2,1)}, u32[]{:S(2)}) copy-start(bf16[1,2,16,4096]{3,2,1,0:T(8,128)(2,1)} %param.11) | copy-start | bytes 786436
  17.9 7.6 %collective-permute-start.5 = (bf16[16,4096]{1,0:T(8,128)(2,1)S(1)}, bf16[16,4096]{1,0:T(8,128)(2,1)S(1)}, u32[]{:S(2)}, u32[]{:S(2)}) collective-permute-start(bf16[16,4096]{1,0:T(8,128)(2,1)S(1)} %collective-permute-done.4.refs_3_), channel_id=1, source_target_pairs={{0,1},{1,0},{2,3},{3,2},{4,5},{5,4},{6,7},{7,6},{8,9},{9,8},{10,11... | collective-permute-start | bytes 393224 | tf_op jit(solution)/shard_map/ppermute | solution.py:371
  18.6 6.9 %collective-permute-start.7 = (bf16[16,4096]{1,0:T(8,128)(2,1)S(1)}, bf16[16,4096]{1,0:T(8,128)(2,1)S(1)}, u32[]{:S(2)}, u32[]{:S(2)}) collective-permute-start(bf16[16,4096]{1,0:T(8,128)(2,1)S(1)} %collective-permute-done.6.refs_5_), channel_id=1, source_target_pairs={{0,1},{1,0},{2,3},{3,2},{4,5},{5,4},{6,7},{7,6},{8,9},{9,8},{10,11... | collective-permute-start | bytes 393224 | tf_op jit(solution)/shard_map/ppermute | solution.py:371
  20.0 9.2 %collective-permute-start.9 = (bf16[16,4096]{1,0:T(8,128)(2,1)S(1)}, bf16[16,4096]{1,0:T(8,128)(2,1)S(1)}, u32[]{:S(2)}, u32[]{:S(2)}) collective-permute-start(bf16[16,4096]{1,0:T(8,128)(2,1)S(1)} %get-tuple-element.66), channel_id=1, source_target_pairs={{0,2},{1,3},{2,0},{3,1},{4,6},{5,7},{6,4},{7,5},{8,10},{9,11},{10,... | collective-permute-start | bytes 393224 | tf_op jit(solution)/shard_map/ppermute | solution.py:371
  21.5 12.9 %collective-permute-start.10 = (bf16[16,4096]{1,0:T(8,128)(2,1)S(1)}, bf16[16,4096]{1,0:T(8,128)(2,1)S(1)}, u32[]{:S(2)}, u32[]{:S(2)}) collective-permute-start(bf16[16,4096]{1,0:T(8,128)(2,1)S(1)} %get-tuple-element.66), channel_id=1, source_target_pairs={{0,4},{1,5},{2,6},{3,7},{4,0},{5,1},{6,2},{7,3},{8,12},{9,13},{10,... | collective-permute-start | bytes 393224 | tf_op jit(solution)/shard_map/ppermute | solution.py:371
  23.2 11.2 %collective-permute-start.11 = (bf16[16,4096]{1,0:T(8,128)(2,1)S(1)}, bf16[16,4096]{1,0:T(8,128)(2,1)S(1)}, u32[]{:S(2)}, u32[]{:S(2)}) collective-permute-start(bf16[16,4096]{1,0:T(8,128)(2,1)S(1)} %get-tuple-element.66), channel_id=1, source_target_pairs={{0,6},{1,7},{2,4},{3,5},{4,2},{5,3},{6,0},{7,1},{8,14},{9,15},{10,... | collective-permute-start | bytes 393224 | tf_op jit(solution)/shard_map/ppermute | solution.py:371
  25.5 25.8 %copy-start.2 = (bf16[1,2,16,4096]{3,2,1,0:T(8,128)(2,1)S(1)}, bf16[1,2,16,4096]{3,2,1,0:T(8,128)(2,1)}, u32[]{:S(2)}) copy-start(bf16[1,2,16,4096]{3,2,1,0:T(8,128)(2,1)} %param.17) | copy-start | bytes 786436
  28.8 9.7 %collective-permute-start.13 = (bf16[16,4096]{1,0:T(8,128)(2,1)S(1)}, bf16[16,4096]{1,0:T(8,128)(2,1)S(1)}, u32[]{:S(2)}, u32[]{:S(2)}) collective-permute-start(bf16[16,4096]{1,0:T(8,128)(2,1)S(1)} %get-tuple-element.69), channel_id=1, source_target_pairs={{0,1},{1,0},{2,3},{3,2},{4,5},{5,4},{6,7},{7,6},{8,9},{9,8},{10,11... | collective-permute-start | bytes 393224 | tf_op jit(solution)/shard_map/ppermute | solution.py:371
  34.5 5.0 %collective-permute-start.8 = (bf16[16,4096]{1,0:T(8,128)(2,1)S(1)}, bf16[16,4096]{1,0:T(8,128)(2,1)S(1)}, u32[]{:S(2)}, u32[]{:S(2)}) collective-permute-start(bf16[16,4096]{1,0:T(8,128)(2,1)S(1)} %get-tuple-element.65), channel_id=1, source_target_pairs={{0,1},{1,0},{2,3},{3,2},{4,5},{5,4},{6,7},{7,6},{8,9},{9,8},{10,11... | collective-permute-start | bytes 393224 | tf_op jit(solution)/shard_map/ppermute | solution.py:371
  34.7 9.2 %collective-permute-start.15 = (bf16[32,4096]{1,0:T(8,128)(2,1)S(1)}, bf16[32,4096]{1,0:T(8,128)(2,1)S(1)}, u32[]{:S(2)}, u32[]{:S(2)}) collective-permute-start(bf16[32,4096]{1,0:T(8,128)(2,1)S(1)} %get-tuple-element.70), channel_id=1, source_target_pairs={{0,24},{1,25},{2,26},{3,27},{4,28},{5,29},{6,30},{7,31},{8,0},{9,1... | collective-permute-start | bytes 786440 | tf_op jit(solution)/shard_map/ppermute | solution.py:379
  34.7 11.1 %collective-permute-start.16 = (bf16[32,4096]{1,0:T(8,128)(2,1)S(1)}, bf16[32,4096]{1,0:T(8,128)(2,1)S(1)}, u32[]{:S(2)}, u32[]{:S(2)}) collective-permute-start(bf16[32,4096]{1,0:T(8,128)(2,1)S(1)} %get-tuple-element.71), channel_id=1, source_target_pairs={{0,26},{1,27},{2,24},{3,25},{4,30},{5,31},{6,28},{7,29},{8,2},{9,3... | collective-permute-start | bytes 786440 | tf_op jit(solution)/shard_map/ppermute | solution.py:379
  39.6 7.8 %collective-permute-start.14 = (bf16[16,4096]{1,0:T(8,128)(2,1)S(1)}, bf16[16,4096]{1,0:T(8,128)(2,1)S(1)}, u32[]{:S(2)}, u32[]{:S(2)}) collective-permute-start(bf16[16,4096]{1,0:T(8,128)(2,1)S(1)} %add_convert_fusion.4), channel_id=1, source_target_pairs={{0,28},{1,29},{2,30},{3,31},{4,24},{5,25},{6,26},{7,27},{8,4},{9,5... | collective-permute-start | bytes 393224 | tf_op jit(solution)/shard_map/ppermute | solution.py:379
  41.3 10.0 %collective-permute-start.12 = (bf16[16,4096]{1,0:T(8,128)(2,1)S(1)}, bf16[16,4096]{1,0:T(8,128)(2,1)S(1)}, u32[]{:S(2)}, u32[]{:S(2)}) collective-permute-start(bf16[16,4096]{1,0:T(8,128)(2,1)S(1)} %add_convert_fusion.5), channel_id=1, source_target_pairs={{0,30},{1,31},{2,28},{3,29},{4,26},{5,27},{6,24},{7,25},{8,6},{9,7... | collective-permute-start | bytes 393224 | tf_op jit(solution)/shard_map/ppermute | solution.py:379
  45.9 5.4 %collective-permute-start.17 = (bf16[16,4096]{1,0:T(8,128)(2,1)S(1)}, bf16[16,4096]{1,0:T(8,128)(2,1)S(1)}, u32[]{:S(2)}, u32[]{:S(2)}) collective-permute-start(bf16[16,4096]{1,0:T(8,128)(2,1)S(1)} %add_convert_fusion.3), channel_id=1, source_target_pairs={{0,1},{1,0},{2,3},{3,2},{4,5},{5,4},{6,7},{7,6},{8,9},{9,8},{10,11... | collective-permute-start | bytes 393224 | tf_op jit(solution)/shard_map/ppermute | solution.py:371
  52.0 7.9 %collective-permute-start.18 = (bf16[16,4096]{1,0:T(8,128)(2,1)S(1)}, bf16[16,4096]{1,0:T(8,128)(2,1)S(1)}, u32[]{:S(2)}, u32[]{:S(2)}) collective-permute-start(bf16[16,4096]{1,0:T(8,128)(2,1)S(1)} %get-tuple-element.72.refs_0_), channel_id=1, source_target_pairs={{0,1},{1,0},{2,3},{3,2},{4,5},{5,4},{6,7},{7,6},{8,9},{9,8},{10,11... | collective-permute-start | bytes 393224 | tf_op jit(solution)/shard_map/ppermute | solution.py:371
  54.5 13.0 %collective-permute-start.20 = (bf16[16,4096]{1,0:T(8,128)(2,1)S(1)}, bf16[16,4096]{1,0:T(8,128)(2,1)S(1)}, u32[]{:S(2)}, u32[]{:S(2)}) collective-permute-start(bf16[16,4096]{1,0:T(8,128)(2,1)S(1)} %get-tuple-element.72.refs_0_), channel_id=1, source_target_pairs={{0,4},{1,5},{2,6},{3,7},{4,0},{5,1},{6,2},{7,3},{8,12},{9,13},{10,... | collective-permute-start | bytes 393224 | tf_op jit(solution)/shard_map/ppermute | solution.py:371
  57.5 8.3 %collective-permute-start.23 = (bf16[16,4096]{1,0:T(8,128)(2,1)S(1)}, bf16[16,4096]{1,0:T(8,128)(2,1)S(1)}, u32[]{:S(2)}, u32[]{:S(2)}) collective-permute-start(bf16[16,4096]{1,0:T(8,128)(2,1)S(1)} %get-tuple-element.72.refs_0_), channel_id=1, source_target_pairs={{0,6},{1,7},{2,4},{3,5},{4,2},{5,3},{6,0},{7,1},{8,14},{9,15},{10,... | collective-permute-start | bytes 393224 | tf_op jit(solution)/shard_map/ppermute | solution.py:371
  58.0 14.7 %collective-permute-start.21 = (bf16[4,16,4096]{2,1,0:T(8,128)(2,1)S(1)}, bf16[4,16,4096]{2,1,0:T(8,128)(2,1)S(1)}, u32[]{:S(2)}, u32[]{:S(2)}) collective-permute-start(bf16[4,16,4096]{2,1,0:T(8,128)(2,1)S(1)} %pad_maximum_fusion.refs_2_), channel_id=1, source_target_pairs={{0,1},{1,0},{2,3},{3,2},{4,5},{5,4},{6,7},{7,6},{8,9},{9,8},{10,11... | collective-permute-start | bytes 1572872 | tf_op jit(solution)/shard_map/ppermute | solution.py:371
  60.0 18.8 %collective-permute-start.19 = (bf16[32,4096]{1,0:T(8,128)(2,1)S(1)}, bf16[32,4096]{1,0:T(8,128)(2,1)S(1)}, u32[]{:S(2)}, u32[]{:S(2)}) collective-permute-start(bf16[32,4096]{1,0:T(8,128)(2,1)S(1)} %pad_maximum_fusion.3), channel_id=1, source_target_pairs={{0,2},{1,3},{2,0},{3,1},{4,6},{5,7},{6,4},{7,5},{8,10},{9,11},{10,... | collective-permute-start | bytes 786440 | tf_op jit(solution)/shard_map/ppermute | solution.py:371
  65.8 12.0 %collective-permute-start.24 = (bf16[16,4096]{1,0:T(8,128)(2,1)S(1)}, bf16[16,4096]{1,0:T(8,128)(2,1)S(1)}, u32[]{:S(2)}, u32[]{:S(2)}) collective-permute-start(bf16[16,4096]{1,0:T(8,128)(2,1)S(1)} %collective-permute-done.23.refs_5_), channel_id=1, source_target_pairs={{0,1},{1,0},{2,3},{3,2},{4,5},{5,4},{6,7},{7,6},{8,9},{9,8},{10,11... | collective-permute-start | bytes 393224 | tf_op jit(solution)/shard_map/ppermute | solution.py:371
  72.7 6.1 %collective-permute-start.22 = (bf16[16,4096]{1,0:T(8,128)(2,1)S(1)}, bf16[16,4096]{1,0:T(8,128)(2,1)S(1)}, u32[]{:S(2)}, u32[]{:S(2)}) collective-permute-start(bf16[16,4096]{1,0:T(8,128)(2,1)S(1)} %collective-permute-done.20.refs_3_), channel_id=1, source_target_pairs={{0,1},{1,0},{2,3},{3,2},{4,5},{5,4},{6,7},{7,6},{8,9},{9,8},{10,11... | collective-permute-start | bytes 393224 | tf_op jit(solution)/shard_map/ppermute | solution.py:371
  74.4 10.5 %collective-permute-start.26 = (bf16[16,4096]{1,0:T(8,128)(2,1)S(1)}, bf16[16,4096]{1,0:T(8,128)(2,1)S(1)}, u32[]{:S(2)}, u32[]{:S(2)}) collective-permute-start(bf16[16,4096]{1,0:T(8,128)(2,1)S(1)} %get-tuple-element.79), channel_id=1, source_target_pairs={{0,2},{1,3},{2,0},{3,1},{4,6},{5,7},{6,4},{7,5},{8,10},{9,11},{10,... | collective-permute-start | bytes 393224 | tf_op jit(solution)/shard_map/ppermute | solution.py:371
  74.4 11.3 %collective-permute-start.27 = (bf16[16,4096]{1,0:T(8,128)(2,1)S(1)}, bf16[16,4096]{1,0:T(8,128)(2,1)S(1)}, u32[]{:S(2)}, u32[]{:S(2)}) collective-permute-start(bf16[16,4096]{1,0:T(8,128)(2,1)S(1)} %get-tuple-element.79), channel_id=1, source_target_pairs={{0,4},{1,5},{2,6},{3,7},{4,0},{5,1},{6,2},{7,3},{8,12},{9,13},{10,... | collective-permute-start | bytes 393224 | tf_op jit(solution)/shard_map/ppermute | solution.py:371
  77.9 7.8 %collective-permute-start.28 = (bf16[16,4096]{1,0:T(8,128)(2,1)S(1)}, bf16[16,4096]{1,0:T(8,128)(2,1)S(1)}, u32[]{:S(2)}, u32[]{:S(2)}) collective-permute-start(bf16[16,4096]{1,0:T(8,128)(2,1)S(1)} %get-tuple-element.79), channel_id=1, source_target_pairs={{0,6},{1,7},{2,4},{3,5},{4,2},{5,3},{6,0},{7,1},{8,14},{9,15},{10,... | collective-permute-start | bytes 393224 | tf_op jit(solution)/shard_map/ppermute | solution.py:371
  82.0 6.7 %collective-permute-start.30 = (bf16[16,4096]{1,0:T(8,128)(2,1)S(1)}, bf16[16,4096]{1,0:T(8,128)(2,1)S(1)}, u32[]{:S(2)}, u32[]{:S(2)}) collective-permute-start(bf16[16,4096]{1,0:T(8,128)(2,1)S(1)} %get-tuple-element.82), channel_id=1, source_target_pairs={{0,1},{1,0},{2,3},{3,2},{4,5},{5,4},{6,7},{7,6},{8,9},{9,8},{10,11... | collective-permute-start | bytes 393224 | tf_op jit(solution)/shard_map/ppermute | solution.py:371
  82.7 6.8 %collective-permute-start.25 = (bf16[16,4096]{1,0:T(8,128)(2,1)S(1)}, bf16[16,4096]{1,0:T(8,128)(2,1)S(1)}, u32[]{:S(2)}, u32[]{:S(2)}) collective-permute-start(bf16[16,4096]{1,0:T(8,128)(2,1)S(1)} %get-tuple-element.78), channel_id=1, source_target_pairs={{0,1},{1,0},{2,3},{3,2},{4,5},{5,4},{6,7},{7,6},{8,9},{9,8},{10,11... | collective-permute-start | bytes 393224 | tf_op jit(solution)/shard_map/ppermute | solution.py:371
  84.9 22.1 %copy-start = (bf16[1,2,16,4096]{3,2,1,0:T(8,128)(2,1)S(1)}, bf16[1,2,16,4096]{3,2,1,0:T(8,128)(2,1)}, u32[]{:S(2)}) copy-start(bf16[1,2,16,4096]{3,2,1,0:T(8,128)(2,1)} %param.16) | copy-start | bytes 786436
  84.9 3.8 %collective-permute-start.35 = (f32[2,128]{1,0:T(2,128)S(1)}, f32[2,128]{1,0:T(2,128)S(1)}, u32[]{:S(2)}, u32[]{:S(2)}) collective-permute-start(f32[2,128]{1,0:T(2,128)S(1)} %gate_part.1), channel_id=1, source_target_pairs={{0,1},{1,0},{2,3},{3,2},{4,5},{5,4},{6,7},{7,6},{8,9},{9,8},{10,11... | collective-permute-start | bytes 3080 | tf_op jit(solution)/shard_map/ppermute | solution.py:371
  85.7 8.3 %collective-permute-start.32 = (bf16[32,4096]{1,0:T(8,128)(2,1)S(1)}, bf16[32,4096]{1,0:T(8,128)(2,1)S(1)}, u32[]{:S(2)}, u32[]{:S(2)}) collective-permute-start(bf16[32,4096]{1,0:T(8,128)(2,1)S(1)} %get-tuple-element.84), channel_id=1, source_target_pairs={{0,2},{1,3},{2,0},{3,1},{4,6},{5,7},{6,4},{7,5},{8,10},{9,11},{10,... | collective-permute-start | bytes 786440 | tf_op jit(solution)/shard_map/ppermute | solution.py:371
  88.7 7.8 %collective-permute-start.31 = (bf16[16,4096]{1,0:T(8,128)(2,1)S(1)}, bf16[16,4096]{1,0:T(8,128)(2,1)S(1)}, u32[]{:S(2)}, u32[]{:S(2)}) collective-permute-start(bf16[16,4096]{1,0:T(8,128)(2,1)S(1)} %add_convert_fusion.1), channel_id=1, source_target_pairs={{0,4},{1,5},{2,6},{3,7},{4,0},{5,1},{6,2},{7,3},{8,12},{9,13},{10,... | collective-permute-start | bytes 393224 | tf_op jit(solution)/shard_map/ppermute | solution.py:371
  89.5 6.3 %collective-permute-start.34 = (bf16[16,4096]{1,0:T(8,128)(2,1)S(1)}, bf16[16,4096]{1,0:T(8,128)(2,1)S(1)}, u32[]{:S(2)}, u32[]{:S(2)}) collective-permute-start(bf16[16,4096]{1,0:T(8,128)(2,1)S(1)} %get-tuple-element.87), channel_id=1, source_target_pairs={{0,8},{1,9},{2,10},{3,11},{4,12},{5,13},{6,14},{7,15},{8,16},{9,17... | collective-permute-start | bytes 393224 | tf_op jit(solution)/shard_map/ppermute | solution.py:379
  89.6 18.9 %collective-permute-start.39 = (bf16[4,16,4096]{2,1,0:T(8,128)(2,1)S(1)}, bf16[4,16,4096]{2,1,0:T(8,128)(2,1)S(1)}, u32[]{:S(2)}, u32[]{:S(2)}) collective-permute-start(bf16[4,16,4096]{2,1,0:T(8,128)(2,1)S(1)} %pad_maximum_fusion.1.refs_4_), channel_id=1, source_target_pairs={{0,1},{1,0},{2,3},{3,2},{4,5},{5,4},{6,7},{7,6},{8,9},{9,8},{10,11... | collective-permute-start | bytes 1572872 | tf_op jit(solution)/shard_map/ppermute | solution.py:371
  91.0 8.2 %collective-permute-start.29 = (bf16[16,4096]{1,0:T(8,128)(2,1)S(1)}, bf16[16,4096]{1,0:T(8,128)(2,1)S(1)}, u32[]{:S(2)}, u32[]{:S(2)}) collective-permute-start(bf16[16,4096]{1,0:T(8,128)(2,1)S(1)} %add_convert_fusion.2), channel_id=1, source_target_pairs={{0,6},{1,7},{2,4},{3,5},{4,2},{5,3},{6,0},{7,1},{8,14},{9,15},{10,... | collective-permute-start | bytes 393224 | tf_op jit(solution)/shard_map/ppermute | solution.py:371
  94.1 12.9 %collective-permute-start.33 = (bf16[16,4096]{1,0:T(8,128)(2,1)S(1)}, bf16[16,4096]{1,0:T(8,128)(2,1)S(1)}, u32[]{:S(2)}, u32[]{:S(2)}) collective-permute-start(bf16[16,4096]{1,0:T(8,128)(2,1)S(1)} %add_convert_fusion), channel_id=1, source_target_pairs={{0,1},{1,0},{2,3},{3,2},{4,5},{5,4},{6,7},{7,6},{8,9},{9,8},{10,11... | collective-permute-start | bytes 393224 | tf_op jit(solution)/shard_map/ppermute | solution.py:371
  95.8 8.1 %collective-permute-start.36 = (f32[2,128]{1,0:T(2,128)S(1)}, f32[2,128]{1,0:T(2,128)S(1)}, u32[]{:S(2)}, u32[]{:S(2)}) collective-permute-start(f32[2,128]{1,0:T(2,128)S(1)} %add.27.refs_8_), channel_id=1, source_target_pairs={{0,2},{1,3},{2,0},{3,1},{4,6},{5,7},{6,4},{7,5},{8,10},{9,11},{10,... | collective-permute-start | bytes 3080 | tf_op jit(solution)/shard_map/ppermute | solution.py:371
  96.5 7.4 %collective-permute-start.37 = (f32[2,128]{1,0:T(2,128)S(1)}, f32[2,128]{1,0:T(2,128)S(1)}, u32[]{:S(2)}, u32[]{:S(2)}) collective-permute-start(f32[2,128]{1,0:T(2,128)S(1)} %add.27.refs_8_), channel_id=1, source_target_pairs={{0,4},{1,5},{2,6},{3,7},{4,0},{5,1},{6,2},{7,3},{8,12},{9,13},{10,... | collective-permute-start | bytes 3080 | tf_op jit(solution)/shard_map/ppermute | solution.py:371
  99.2 5.4 %collective-permute-start.38 = (f32[2,128]{1,0:T(2,128)S(1)}, f32[2,128]{1,0:T(2,128)S(1)}, u32[]{:S(2)}, u32[]{:S(2)}) collective-permute-start(f32[2,128]{1,0:T(2,128)S(1)} %add.27.refs_8_), channel_id=1, source_target_pairs={{0,6},{1,7},{2,4},{3,5},{4,2},{5,3},{6,0},{7,1},{8,14},{9,15},{10,... | collective-permute-start | bytes 3080 | tf_op jit(solution)/shard_map/ppermute | solution.py:371

commit v4 on v3

--- a/solution.py
+++ b/solution.py
@@ -67,9 +67,17 @@
     return jnp.broadcast_to(row, (128, row.shape[1])).T[:, :1]
 
 
-def prepare_kernel(devices, info, hidden, gates, w_out, w_in, out_v, in_v, active_ref, scale_ref, weighted_ref, scales, sems):
+def prepare_kernel(
+    devices, info, hidden_hbm, gates_hbm, w_out, w_in, out_v, in_v, active_ref, scale_ref, weighted_ref, hidden, gates, scales, sems, small_sems
+):
     units = w_out.shape[0]
     piece = units // PIECES
+    small = [
+        pltpu.make_async_copy(hidden_hbm, hidden, small_sems.at[0]),
+        pltpu.make_async_copy(gates_hbm, gates, small_sems.at[1]),
+    ]
+    for copy in small:
+        copy.start()
     copies = []
     for w, (source, target) in enumerate(((w_out, out_v), (w_in, in_v))):
         for p in range(PIECES):
@@ -78,6 +86,8 @@
             copies[-1].start()
     ticks, _, rows, _ = hidden.shape
     me = lax.axis_index("dp")
+    for copy in small:
+        copy.wait()
     for t in range(ticks):
         slot = info[t]
         scales[...] = as_column(gates[0, pl.ds(slot, 1), :]).reshape(devices, rows, 1)
@@ -98,7 +108,7 @@
     tokens = devices * rows
     return pl.pallas_call(
         functools.partial(prepare_kernel, devices),
-        in_specs=[SMEM, VMEM, VMEM, HBM, HBM],
+        in_specs=[SMEM, HBM, HBM, HBM, HBM],
         out_specs=[VMEM] * 5,
         out_shape=[
             pltpu.VMEM(w_out.shape, BF16),
@@ -107,20 +117,26 @@
             jax.ShapeDtypeStruct((ticks, tokens, 1), F32),
             jax.ShapeDtypeStruct((ticks, tokens, units), BF16),
         ],
-        scratch_shapes=[pltpu.VMEM((devices, rows, 1), F32), pltpu.SemaphoreType.DMA((2, PIECES))],
+        scratch_shapes=[
+            pltpu.VMEM(hidden.shape, BF16),
+            pltpu.VMEM(gates.shape, F32),
+            pltpu.VMEM((devices, rows, 1), F32),
+            pltpu.SemaphoreType.DMA((2, PIECES)),
+            pltpu.SemaphoreType.DMA((2,)),
+        ],
         compiler_params=PARAMS,
         cost_estimate=pl.CostEstimate(
             flops=2 * ticks * tokens * units, bytes_accessed=4 * w_out.size, transcendentals=0
         ),
         name="prepare",
-    )(info, hidden, gates, in_hbm(w_out), in_hbm(w_in))
+    )(info, in_hbm(hidden), in_hbm(gates), in_hbm(w_out), in_hbm(w_in))
 
 
 def expert_kernel(devices, inner, tick, inputs, *refs):
     chunks = refs[:inputs]
     w_out, w_in, active_ref, scale_ref = refs[inputs : inputs + 4]
-    parts = refs[inputs + 4 : -3]
-    rows_ref, hid_ref, upstream_ref = refs[-3:]
+    parts = refs[inputs + 4 : -4]
+    rows_ref, hid_ref, upstream_ref, left_ref = refs[-4:]
     tokens = rows_ref.shape[0]
     rows = tokens // devices
     start = 0
@@ -133,17 +149,20 @@
     upstream_ref[...] = upstream
     hid_grad = jnp.where(active_ref[tick] > 0, upstream * scale_ref[tick], 0.0).astype(BF16)
     width = w_in.shape[1]
-    tile = column_tile(width)
-    for first in range(0, width, tile):
-        cols = pl.ds(first, tile)
-        part = jnp.dot(hid_grad, w_in[:, cols], preferred_element_type=F32).astype(BF16)
+    tile = width // 2 if width % 256 == 0 else width
+    outer = devices // inner
+    for k in range(devices):
+        hid_ref[k % inner * outer + k // inner] = hid_grad[k * rows : (k + 1) * rows]
+    left_ref[...] = hid_grad
+
+    @pl.loop(0, width // tile)
+    def _(step):
+        cols = pl.ds(pl.multiple_of(step * tile, tile), tile)
+        part = jnp.dot(left_ref[...], w_in[:, cols], preferred_element_type=F32).astype(BF16)
         start = 0
         for ref in parts:
             ref[:, cols] = part[start : start + ref.shape[0]]
             start += ref.shape[0]
-    outer = devices // inner
-    for k in range(devices):
-        hid_ref[k % inner * outer + k // inner] = hid_grad[k * rows : (k + 1) * rows]
 
 
 def gate_part_kernel(active, *refs):
@@ -195,6 +214,7 @@
             jax.ShapeDtypeStruct((devices, rows, units), BF16),
             jax.ShapeDtypeStruct((tokens, units), F32),
         ],
+        scratch_shapes=[pltpu.VMEM((tokens, units), BF16)],
         compiler_params=PARAMS,
         cost_estimate=pl.CostEstimate(
             flops=4 * tokens * units * width, bytes_accessed=2 * 2**20, transcendentals=0
@@ -453,7 +473,8 @@
         ]
         if stash is not None:
             stash = jnp.stack(stash)
-            sums[far[0]], stash = lax.optimization_barrier((sums[far[0]], stash))
+            tie = far[0] if last else far[-1]
+            sums[tie], stash = lax.optimization_barrier((sums[tie], stash))
             late = after(stash, sums[far[-1]])
             if last:
                 saved += along_inner(after(late, gate))
@@ -464,7 +485,7 @@
             )
             done.append(above_done)
             incoming.append(following)
-            saved += along_inner(after(late, own))
+            saved += along_inner(after(late, totals[1]))
     done = [shift(after(value, sums[far[-1]]), 1) for value in done]
     depth = ticks * tokens
     rows_list[-1] = after(rows_list[-1], done[0])

time: 112 us -> 111 us (level)
  starting transfers between devices: 55 us -> 61.9 us
  waiting for transfers between devices: 32 us -> 25.7 us
  local copies, waits for them, and re-layouts: 1.68 us -> 0.03 us
    ppermute x33, starting transfers between devices: 45.3 us -> 52.5 us  [swap(): return lax.ppermute(value, 'dp', [(i, i ^ step) for i in range(devices)])]
    ppermute x33, waiting for transfers between devices: 26.2 us -> 21.9 us  [swap(): return lax.ppermute(value, 'dp', [(i, i ^ step) for i in range(devices)])]
    ppermute x7, waiting for transfers between devices: 5.85 us -> 3.8 us  [shift(): return lax.ppermute(value, ('section', 'dp'), route)]
    unnamed x10 -> x6, local copies, waits for them, and re-layouts: 1.66 us -> 0.01 us
  transfers between devices with their start and end apart: 40 -> 40, of which waited for: 14 -> 10; matrix products, arithmetic and copies ran while one was open for 0% -> 0% of each run, Pallas kernels for 15% -> 14%
where the time goes in v4:
time: 111 us; the launch traced here: 110 us
  starting transfers between devices  61.9 us (56%)
  waiting for transfers between devices  25.7 us (23%)
  Pallas kernels  21.3 us (19%)
    ppermute x33, starting transfers between devices, swap(): return lax.ppermute(value, 'dp', [(i, i ^ step) for i in range(devices)])  52.5 us
    ppermute x33, waiting for transfers between devices, swap(): return lax.ppermute(value, 'dp', [(i, i ^ step) for i in range(devices)])  21.9 us
    ppermute x7, starting transfers between devices, shift(): return lax.ppermute(value, ('section', 'dp'), route)  9.43 us
    pallas_call x2, Pallas kernels, grad_call(): pl.pallas_call(kernel, in_specs=[SMEM] * scalars + [VMEM] * (len(args) -...  6.14 us
    pallas_call x2, Pallas kernels, expert(): pl.pallas_call(functools.partial(expert_kernel, devices, inner, tick, len...  5.81 us
    pallas_call x1, Pallas kernels, prepare(): pl.pallas_call(functools.partial(prepare_kernel, devices), in_specs=[SMEM...  4.74 us
    ppermute x7, waiting for transfers between devices, shift(): return lax.ppermute(value, ('section', 'dp'), route)  3.8 us
  transfers between devices with their start and end apart: 40, of which 10 were waited for; matrix products, arithmetic and copies ran while one was open for 0% of the time, Pallas kernels for 14%

profile of v4, /device:TPU:0, one launch (start us, length us, event | category | flops | bytes accessed | tf_op | source)
XLA Modules:
  0.0 110.2 jit_solution(7228925092996609189)
XLA Ops:
  0.6 1.6 %pick.1 = (bf16[16,4096]{1,0:T(8,128)(2,1)S(1)}, s32[4]{0:T(128)S(1)}) custom-call(s32[1,2]{1,0:T(1,128)} %slot_hbm.1, s32[1,2]{1,0:T(1,128)} %block_hbm.1, bf16[2,16,4096]{2,1,0:T(8,128)(2,1)} %bitcast.21), custom_call_target="tpu_custom_call" | custom-call | tf_op jit(solution)/shard_map/pick/pallas_call | solution.py:44
  2.2 3.0 %collective-permute-start.1 = (bf16[16,4096]{1,0:T(8,128)(2,1)S(1)}, bf16[16,4096]{1,0:T(8,128)(2,1)S(1)}, u32[]{:S(2)}, u32[]{:S(2)}) collective-permute-start(bf16[16,4096]{1,0:T(8,128)(2,1)S(1)} %get-tuple-element.54.refs_0_), channel_id=1, source_target_pairs={{0,1},{1,0},{2,3},{3,2},{4,5},{5,4},{6,7},{7,6},{8,9},{9,8},{10,11... | collective-permute-start | bytes 393224 | tf_op jit(solution)/shard_map/ppermute | solution.py:391
  5.2 2.6 %collective-permute-start.4 = (bf16[16,4096]{1,0:T(8,128)(2,1)S(1)}, bf16[16,4096]{1,0:T(8,128)(2,1)S(1)}, u32[]{:S(2)}, u32[]{:S(2)}) collective-permute-start(bf16[16,4096]{1,0:T(8,128)(2,1)S(1)} %get-tuple-element.54.refs_0_), channel_id=1, source_target_pairs={{0,4},{1,5},{2,6},{3,7},{4,0},{5,1},{6,2},{7,3},{8,12},{9,13},{10,... | collective-permute-start | bytes 393224 | tf_op jit(solution)/shard_map/ppermute | solution.py:391
  7.8 1.3 %collective-permute-start.6 = (bf16[16,4096]{1,0:T(8,128)(2,1)S(1)}, bf16[16,4096]{1,0:T(8,128)(2,1)S(1)}, u32[]{:S(2)}, u32[]{:S(2)}) collective-permute-start(bf16[16,4096]{1,0:T(8,128)(2,1)S(1)} %get-tuple-element.54.refs_0_), channel_id=1, source_target_pairs={{0,6},{1,7},{2,4},{3,5},{4,2},{5,3},{6,0},{7,1},{8,14},{9,15},{10,... | collective-permute-start | bytes 393224 | tf_op jit(solution)/shard_map/ppermute | solution.py:391
  9.3 1.5 %collective-permute-start.3 = (bf16[2,16,4096]{2,1,0:T(8,128)(2,1)}, bf16[2,16,4096]{2,1,0:T(8,128)(2,1)S(1)}, u32[]{:S(2)}, u32[]{:S(2)}) collective-permute-start(bf16[2,16,4096]{2,1,0:T(8,128)(2,1)} %bitcast.22), channel_id=1, source_target_pairs={{0,24},{1,25},{2,26},{3,27},{4,28},{5,29},{6,30},{7,31},{8,0},{9,1... | collective-permute-start | bytes 786440 | tf_op jit(solution)/shard_map/ppermute | solution.py:399
  11.1 4.7 %prepare.1 = (bf16[640,4096]{1,0:T(8,128)(2,1)S(1)}, bf16[640,4096]{1,0:T(8,128)(2,1)S(1)}, f32[2,128,640]{2,1,0:T(8,128)S(1)}, f32[2,128,1]{2,1,0:T(8,128)S(1)}, bf16[2,128,640]{2,1,0:T(8,128)(2,1)S(1)}) custom-call(s32[4]{0:T(128)S(1)} %get-tuple-element.58.info, bf16[2,8,16,640]{3,2,1,0:T(8,128)(2,1)} %bitcast.31, f32[1,2,128]{2,1,0:T(2,128)} %gates_hbm.1, ...), custom_call_target="tpu_custom_call" | custom-call | flops 327680 | bytes 10485760 | tf_op jit(solution)/shard_map/prepare/pallas_call | solution.py:109
  15.9 2.0 %collective-permute-done.4.refs_3_ = bf16[16,4096]{1,0:T(8,128)(2,1)S(1)} collective-permute-done((bf16[16,4096]{1,0:T(8,128)(2,1)S(1)}, bf16[16,4096]{1,0:T(8,128)(2,1)S(1)}, u32[]{:S(2)}, u32[]{:S(2)}) %collective-permute-start.4) | collective-permute-done | bytes 131104 | tf_op jit(solution)/shard_map/ppermute | solution.py:391
  17.9 0.5 collective-permute-start.5
  18.4 1.6 %collective-permute-start.7 = (bf16[16,4096]{1,0:T(8,128)(2,1)S(1)}, bf16[16,4096]{1,0:T(8,128)(2,1)S(1)}, u32[]{:S(2)}, u32[]{:S(2)}) collective-permute-start(bf16[16,4096]{1,0:T(8,128)(2,1)S(1)} %collective-permute-done.6.refs_5_), channel_id=1, source_target_pairs={{0,1},{1,0},{2,3},{3,2},{4,5},{5,4},{6,7},{7,6},{8,9},{9,8},{10,11... | collective-permute-start | bytes 393224 | tf_op jit(solution)/shard_map/ppermute | solution.py:391
  20.0 0.9 collective-permute-start.11
  20.9 2.2 %collective-permute-start.12 = (bf16[16,4096]{1,0:T(8,128)(2,1)S(1)}, bf16[16,4096]{1,0:T(8,128)(2,1)S(1)}, u32[]{:S(2)}, u32[]{:S(2)}) collective-permute-start(bf16[16,4096]{1,0:T(8,128)(2,1)S(1)} %get-tuple-element.68), channel_id=1, source_target_pairs={{0,4},{1,5},{2,6},{3,7},{4,0},{5,1},{6,2},{7,3},{8,12},{9,13},{10,... | collective-permute-start | bytes 393224 | tf_op jit(solution)/shard_map/ppermute | solution.py:391
  23.0 2.5 %collective-permute-start.13 = (bf16[16,4096]{1,0:T(8,128)(2,1)S(1)}, bf16[16,4096]{1,0:T(8,128)(2,1)S(1)}, u32[]{:S(2)}, u32[]{:S(2)}) collective-permute-start(bf16[16,4096]{1,0:T(8,128)(2,1)S(1)} %get-tuple-element.68), channel_id=1, source_target_pairs={{0,6},{1,7},{2,4},{3,5},{4,2},{5,3},{6,0},{7,1},{8,14},{9,15},{10,... | collective-permute-start | bytes 393224 | tf_op jit(solution)/shard_map/ppermute | solution.py:391
  25.5 2.9 %expert_tick.2 = (bf16[32,4096]{1,0:T(8,128)(2,1)S(1)}, bf16[32,4096]{1,0:T(8,128)(2,1)S(1)}, bf16[16,4096]{1,0:T(8,128)(2,1)S(1)}, bf16[16,4096]{1,0:T(8,128)(2...) custom-call(bf16[16,4096]{1,0:T(8,128)(2,1)S(1)} %get-tuple-element., ...), custom_call_target="tpu_custom_call" | custom-call | flops 1342177280 | bytes 2097152 | tf_op jit(solution)/shard_map/expert_tick/pallas_call | solution.py:207
  28.8 4.3 %collective-permute-done.12 = bf16[16,4096]{1,0:T(8,128)(2,1)S(1)} collective-permute-done((bf16[16,4096]{1,0:T(8,128)(2,1)S(1)}, bf16[16,4096]{1,0:T(8,128)(2,1)S(1)}, u32[]{:S(2)}, u32[]{:S(2)}) %collective-permute-start.12) | collective-permute-done | bytes 131104 | tf_op jit(solution)/shard_map/ppermute | solution.py:391
  33.2 3.7 %collective-permute-start.16 = (bf16[32,4096]{1,0:T(8,128)(2,1)S(1)}, bf16[32,4096]{1,0:T(8,128)(2,1)S(1)}, u32[]{:S(2)}, u32[]{:S(2)}) collective-permute-start(bf16[32,4096]{1,0:T(8,128)(2,1)S(1)} %get-tuple-element.71), channel_id=1, source_target_pairs={{0,26},{1,27},{2,24},{3,25},{4,30},{5,31},{6,28},{7,29},{8,2},{9,3... | collective-permute-start | bytes 786440 | tf_op jit(solution)/shard_map/ppermute | solution.py:399
  36.9 1.5 %collective-permute-start.8 = (bf16[16,4096]{1,0:T(8,128)(2,1)S(1)}, bf16[16,4096]{1,0:T(8,128)(2,1)S(1)}, u32[]{:S(2)}, u32[]{:S(2)}) collective-permute-start(bf16[16,4096]{1,0:T(8,128)(2,1)S(1)} %get-tuple-element.65), channel_id=1, source_target_pairs={{0,1},{1,0},{2,3},{3,2},{4,5},{5,4},{6,7},{7,6},{8,9},{9,8},{10,11... | collective-permute-start | bytes 393224 | tf_op jit(solution)/shard_map/ppermute | solution.py:391
  38.4 1.5 %collective-permute-start.14 = (bf16[16,4096]{1,0:T(8,128)(2,1)S(1)}, bf16[16,4096]{1,0:T(8,128)(2,1)S(1)}, u32[]{:S(2)}, u32[]{:S(2)}) collective-permute-start(bf16[16,4096]{1,0:T(8,128)(2,1)S(1)} %add_convert_fusion.4), channel_id=1, source_target_pairs={{0,28},{1,29},{2,30},{3,31},{4,24},{5,25},{6,26},{7,27},{8,4},{9,5... | collective-permute-start | bytes 393224 | tf_op jit(solution)/shard_map/ppermute | solution.py:399
  39.9 2.0 %collective-permute-done.8 = bf16[16,4096]{1,0:T(8,128)(2,1)S(1)} collective-permute-done((bf16[16,4096]{1,0:T(8,128)(2,1)S(1)}, bf16[16,4096]{1,0:T(8,128)(2,1)S(1)}, u32[]{:S(2)}, u32[]{:S(2)}) %collective-permute-start.8) | collective-permute-done | bytes 131104 | tf_op jit(solution)/shard_map/ppermute | solution.py:391
  41.9 2.6 %collective-permute-start.9 = (bf16[16,4096]{1,0:T(8,128)(2,1)S(1)}, bf16[16,4096]{1,0:T(8,128)(2,1)S(1)}, u32[]{:S(2)}, u32[]{:S(2)}) collective-permute-start(bf16[16,4096]{1,0:T(8,128)(2,1)S(1)} %add_convert_fusion.5), channel_id=1, source_target_pairs={{0,30},{1,31},{2,28},{3,29},{4,26},{5,27},{6,24},{7,25},{8,6},{9,7... | collective-permute-start | bytes 393224 | tf_op jit(solution)/shard_map/ppermute | solution.py:399
  44.6 2.0 %collective-permute-start.17 = (bf16[16,4096]{1,0:T(8,128)(2,1)S(1)}, bf16[16,4096]{1,0:T(8,128)(2,1)S(1)}, u32[]{:S(2)}, u32[]{:S(2)}) collective-permute-start(bf16[16,4096]{1,0:T(8,128)(2,1)S(1)} %add_convert_fusion.3), channel_id=1, source_target_pairs={{0,1},{1,0},{2,3},{3,2},{4,5},{5,4},{6,7},{7,6},{8,9},{9,8},{10,11... | collective-permute-start | bytes 393224 | tf_op jit(solution)/shard_map/ppermute | solution.py:391
  46.6 3.8 %collective-permute-done.9.refs_0_ = bf16[16,4096]{1,0:T(8,128)(2,1)S(1)} collective-permute-done((bf16[16,4096]{1,0:T(8,128)(2,1)S(1)}, bf16[16,4096]{1,0:T(8,128)(2,1)S(1)}, u32[]{:S(2)}, u32[]{:S(2)}) %collective-permute-start.9) | collective-permute-done | bytes 131104 | tf_op jit(solution)/shard_map/ppermute | solution.py:399
  50.4 0.7 hand_on.1
  51.1 2.3 %collective-permute-start.18 = (bf16[16,4096]{1,0:T(8,128)(2,1)S(1)}, bf16[16,4096]{1,0:T(8,128)(2,1)S(1)}, u32[]{:S(2)}, u32[]{:S(2)}) collective-permute-start(bf16[16,4096]{1,0:T(8,128)(2,1)S(1)} %get-tuple-element.72.refs_0_), channel_id=1, source_target_pairs={{0,1},{1,0},{2,3},{3,2},{4,5},{5,4},{6,7},{7,6},{8,9},{9,8},{10,11... | collective-permute-start | bytes 393224 | tf_op jit(solution)/shard_map/ppermute | solution.py:391
  53.5 5.2 %collective-permute-start.20 = (bf16[16,4096]{1,0:T(8,128)(2,1)S(1)}, bf16[16,4096]{1,0:T(8,128)(2,1)S(1)}, u32[]{:S(2)}, u32[]{:S(2)}) collective-permute-start(bf16[16,4096]{1,0:T(8,128)(2,1)S(1)} %get-tuple-element.72.refs_0_), channel_id=1, source_target_pairs={{0,4},{1,5},{2,6},{3,7},{4,0},{5,1},{6,2},{7,3},{8,12},{9,13},{10,... | collective-permute-start | bytes 393224 | tf_op jit(solution)/shard_map/ppermute | solution.py:391
  58.7 0.7 collective-permute-start.23
  59.4 2.1 %collective-permute-start.19 = (bf16[32,4096]{1,0:T(8,128)(2,1)S(1)}, bf16[32,4096]{1,0:T(8,128)(2,1)S(1)}, u32[]{:S(2)}, u32[]{:S(2)}) collective-permute-start(bf16[32,4096]{1,0:T(8,128)(2,1)S(1)} %pad_maximum_fusion.3), channel_id=1, source_target_pairs={{0,2},{1,3},{2,0},{3,1},{4,6},{5,7},{6,4},{7,5},{8,10},{9,11},{10,... | collective-permute-start | bytes 786440 | tf_op jit(solution)/shard_map/ppermute | solution.py:391
  61.5 5.4 %collective-permute-done.23.refs_5_ = bf16[16,4096]{1,0:T(8,128)(2,1)S(1)} collective-permute-done((bf16[16,4096]{1,0:T(8,128)(2,1)S(1)}, bf16[16,4096]{1,0:T(8,128)(2,1)S(1)}, u32[]{:S(2)}, u32[]{:S(2)}) %collective-permute-start.23) | collective-permute-done | bytes 131104 | tf_op jit(solution)/shard_map/ppermute | solution.py:391
  66.9 0.6 collective-permute-start.24
  67.9 0.6 collective-permute-done.21.refs_3_
  68.5 2.5 %collective-permute-start.22 = (bf16[16,4096]{1,0:T(8,128)(2,1)S(1)}, bf16[16,4096]{1,0:T(8,128)(2,1)S(1)}, u32[]{:S(2)}, u32[]{:S(2)}) collective-permute-start(bf16[16,4096]{1,0:T(8,128)(2,1)S(1)} %collective-permute-done.20.refs_3_), channel_id=1, source_target_pairs={{0,1},{1,0},{2,3},{3,2},{4,5},{5,4},{6,7},{7,6},{8,9},{9,8},{10,11... | collective-permute-start | bytes 393224 | tf_op jit(solution)/shard_map/ppermute | solution.py:391
  71.0 1.8 %collective-permute-start.26 = (bf16[16,4096]{1,0:T(8,128)(2,1)S(1)}, bf16[16,4096]{1,0:T(8,128)(2,1)S(1)}, u32[]{:S(2)}, u32[]{:S(2)}) collective-permute-start(bf16[16,4096]{1,0:T(8,128)(2,1)S(1)} %get-tuple-element.79), channel_id=1, source_target_pairs={{0,2},{1,3},{2,0},{3,1},{4,6},{5,7},{6,4},{7,5},{8,10},{9,11},{10,... | collective-permute-start | bytes 393224 | tf_op jit(solution)/shard_map/ppermute | solution.py:391
  72.8 1.5 %collective-permute-start.27 = (bf16[16,4096]{1,0:T(8,128)(2,1)S(1)}, bf16[16,4096]{1,0:T(8,128)(2,1)S(1)}, u32[]{:S(2)}, u32[]{:S(2)}) collective-permute-start(bf16[16,4096]{1,0:T(8,128)(2,1)S(1)} %get-tuple-element.79), channel_id=1, source_target_pairs={{0,4},{1,5},{2,6},{3,7},{4,0},{5,1},{6,2},{7,3},{8,12},{9,13},{10,... | collective-permute-start | bytes 393224 | tf_op jit(solution)/shard_map/ppermute | solution.py:391
  74.3 1.7 %collective-permute-start.28 = (bf16[16,4096]{1,0:T(8,128)(2,1)S(1)}, bf16[16,4096]{1,0:T(8,128)(2,1)S(1)}, u32[]{:S(2)}, u32[]{:S(2)}) collective-permute-start(bf16[16,4096]{1,0:T(8,128)(2,1)S(1)} %get-tuple-element.79), channel_id=1, source_target_pairs={{0,6},{1,7},{2,4},{3,5},{4,2},{5,3},{6,0},{7,1},{8,14},{9,15},{10,... | collective-permute-start | bytes 393224 | tf_op jit(solution)/shard_map/ppermute | solution.py:391
  76.0 2.9 %expert_tick.3 = (bf16[32,4096]{1,0:T(8,128)(2,1)S(1)}, bf16[32,4096]{1,0:T(8,128)(2,1)S(1)}, bf16[16,4096]{1,0:T(8,128)(2,1)S(1)}, bf16[16,4096]{1,0:T(8,128)(2...) custom-call(bf16[16,4096]{1,0:T(8,128)(2,1)S(1)} %get-tuple-element., ...), custom_call_target="tpu_custom_call" | custom-call | flops 1342177280 | bytes 2097152 | tf_op jit(solution)/shard_map/expert_tick/pallas_call | solution.py:207
  78.9 1.9 %collective-permute-start.30 = (bf16[16,4096]{1,0:T(8,128)(2,1)S(1)}, bf16[16,4096]{1,0:T(8,128)(2,1)S(1)}, u32[]{:S(2)}, u32[]{:S(2)}) collective-permute-start(bf16[16,4096]{1,0:T(8,128)(2,1)S(1)} %get-tuple-element.82), channel_id=1, source_target_pairs={{0,1},{1,0},{2,3},{3,2},{4,5},{5,4},{6,7},{7,6},{8,9},{9,8},{10,11... | collective-permute-start | bytes 393224 | tf_op jit(solution)/shard_map/ppermute | solution.py:391
  81.0 0.8 gate_part.1
  81.8 1.8 %collective-permute-start.35 = (f32[2,128]{1,0:T(2,128)S(1)}, f32[2,128]{1,0:T(2,128)S(1)}, u32[]{:S(2)}, u32[]{:S(2)}) collective-permute-start(f32[2,128]{1,0:T(2,128)S(1)} %gate_part.1), channel_id=1, source_target_pairs={{0,1},{1,0},{2,3},{3,2},{4,5},{5,4},{6,7},{7,6},{8,9},{9,8},{10,11... | collective-permute-start | bytes 3080 | tf_op jit(solution)/shard_map/ppermute | solution.py:391
  83.6 0.6 collective-permute-done.27
  84.2 0.7 collective-permute-start.32
  84.9 0.8 collective-permute-done.35
  85.8 2.9 %collective-permute-start.31 = (bf16[16,4096]{1,0:T(8,128)(2,1)S(1)}, bf16[16,4096]{1,0:T(8,128)(2,1)S(1)}, u32[]{:S(2)}, u32[]{:S(2)}) collective-permute-start(bf16[16,4096]{1,0:T(8,128)(2,1)S(1)} %add_convert_fusion.1), channel_id=1, source_target_pairs={{0,4},{1,5},{2,6},{3,7},{4,0},{5,1},{6,2},{7,3},{8,12},{9,13},{10,... | collective-permute-start | bytes 393224 | tf_op jit(solution)/shard_map/ppermute | solution.py:391
  88.8 0.7 collective-permute-start.39
  89.5 2.7 %collective-permute-start.29 = (bf16[16,4096]{1,0:T(8,128)(2,1)S(1)}, bf16[16,4096]{1,0:T(8,128)(2,1)S(1)}, u32[]{:S(2)}, u32[]{:S(2)}) collective-permute-start(bf16[16,4096]{1,0:T(8,128)(2,1)S(1)} %add_convert_fusion.2), channel_id=1, source_target_pairs={{0,6},{1,7},{2,4},{3,5},{4,2},{5,3},{6,0},{7,1},{8,14},{9,15},{10,... | collective-permute-start | bytes 393224 | tf_op jit(solution)/shard_map/ppermute | solution.py:391
  92.2 5.8 %collective-permute-done.32.refs_3_ = bf16[32,4096]{1,0:T(8,128)(2,1)S(1)} collective-permute-done((bf16[32,4096]{1,0:T(8,128)(2,1)S(1)}, bf16[32,4096]{1,0:T(8,128)(2,1)S(1)}, u32[]{:S(2)}, u32[]{:S(2)}) %collective-permute-start.32) | collective-permute-done | bytes 262176 | tf_op jit(solution)/shard_map/ppermute | solution.py:391
  98.2 4.3 %collective-permute-start.38 = (f32[2,128]{1,0:T(2,128)S(1)}, f32[2,128]{1,0:T(2,128)S(1)}, u32[]{:S(2)}, u32[]{:S(2)}) collective-permute-start(f32[2,128]{1,0:T(2,128)S(1)} %add.27.refs_8_), channel_id=1, source_target_pairs={{0,6},{1,7},{2,4},{3,5},{4,2},{5,3},{6,0},{7,1},{8,14},{9,15},{10,... | collective-permute-start | bytes 3080 | tf_op jit(solution)/shard_map/ppermute | solution.py:391
  102.5 2.8 %grad_out.1 = bf16[640,4096]{1,0:T(8,128)(2,1)} custom-call(bf16[2,128,640]{2,1,0:T(8,128)(2,1)S(1)} %get-tuple-element.97.weighted, bf16[128,4096]{1,0:T(8,128)(2,1)S(1)} %get-tuple-element.98.refs_0_, bf16[128,4096]{1,0:T(8,128)(2,1)S(1)} %get-tuple-element.100.refs_1_), custom_call_target="tpu_custom_call" | custom-call | flops 1342177280 | bytes 5242880 | tf_op jit(solution)/shard_map/grad_out/pallas_call | solution.py:279
  105.4 1.5 %finish.1 = (bf16[2,2,16,4096]{3,2,1,0:T(8,128)(2,1)}, f32[2,1,128]{2,1,0:T(1,128)}) custom-call(s32[4]{0:T(128)S(1)} %get-tuple-element.58.info, bf16[16,4096]{1,0:T(8,128)(2,1)S(1)} %collective-permute-done.29.refs_0_, bf16[16,4096]{1,0:T(8,128)(2,1)S(1)} %collective-permute-done.31.refs_1_, bf16[32,4096]{1,0:T(8,128)(2,1)S(1)} %get-tuple-element.83.refs_2_, ...), custom_call_target="tpu_custom_call" | custom-call | tf_op jit(solution)/shard_map/finish/pallas_call | solution.py:360
  106.9 3.4 %grad_in.1 = bf16[640,4096]{1,0:T(8,128)(2,1)} custom-call(s32[4]{0:T(128)S(1)} %get-tuple-element.58.info, bf16[8,16,640]{2,1,0:T(8,128)(2,1)S(1)} %get-tuple-element.92.refs_0_, bf16[8,16,640]{2,1,0:T(8,128)(2,1)S(1)} %get-tuple-element.93.refs_1_, bf16[4,16,4096]{2,1,0:T(8,128)(2,1)S(1)} %pad_maximum_fusion.refs_2_, ...), custom_call_target="tpu_custom_call" | custom-call | flops 1342177280 | bytes 5242880 | tf_op jit(solution)/shard_map/grad_in/pallas_call | solution.py:279
  (59 shorter events, 2.3 us)
Async XLA Ops:
  2.2 8.6 %collective-permute-start.1 = (bf16[16,4096]{1,0:T(8,128)(2,1)S(1)}, bf16[16,4096]{1,0:T(8,128)(2,1)S(1)}, u32[]{:S(2)}, u32[]{:S(2)}) collective-permute-start(bf16[16,4096]{1,0:T(8,128)(2,1)S(1)} %get-tuple-element.54.refs_0_), channel_id=1, source_target_pairs={{0,1},{1,0},{2,3},{3,2},{4,5},{5,4},{6,7},{7,6},{8,9},{9,8},{10,11... | collective-permute-start | bytes 393224 | tf_op jit(solution)/shard_map/ppermute | solution.py:391
  5.2 12.7 %collective-permute-start.4 = (bf16[16,4096]{1,0:T(8,128)(2,1)S(1)}, bf16[16,4096]{1,0:T(8,128)(2,1)S(1)}, u32[]{:S(2)}, u32[]{:S(2)}) collective-permute-start(bf16[16,4096]{1,0:T(8,128)(2,1)S(1)} %get-tuple-element.54.refs_0_), channel_id=1, source_target_pairs={{0,4},{1,5},{2,6},{3,7},{4,0},{5,1},{6,2},{7,3},{8,12},{9,13},{10,... | collective-permute-start | bytes 393224 | tf_op jit(solution)/shard_map/ppermute | solution.py:391
  7.8 10.6 %collective-permute-start.6 = (bf16[16,4096]{1,0:T(8,128)(2,1)S(1)}, bf16[16,4096]{1,0:T(8,128)(2,1)S(1)}, u32[]{:S(2)}, u32[]{:S(2)}) collective-permute-start(bf16[16,4096]{1,0:T(8,128)(2,1)S(1)} %get-tuple-element.54.refs_0_), channel_id=1, source_target_pairs={{0,6},{1,7},{2,4},{3,5},{4,2},{5,3},{6,0},{7,1},{8,14},{9,15},{10,... | collective-permute-start | bytes 393224 | tf_op jit(solution)/shard_map/ppermute | solution.py:391
  9.2 10.8 %collective-permute-start = (s32[4]{0:T(128)S(1)}, s32[4]{0:T(128)S(1)}, u32[]{:S(2)}, u32[]{:S(2)}) collective-permute-start(s32[4]{0:T(128)S(1)} %get-tuple-element.58.info), channel_id=1, source_target_pairs={{0,24},{1,25},{2,26},{3,27},{4,28},{5,29},{6,30},{7,31},{8,0},{9,1... | collective-permute-start | bytes 56 | tf_op jit(solution)/shard_map/ppermute | solution.py:399
  9.3 11.6 %collective-permute-start.3 = (bf16[2,16,4096]{2,1,0:T(8,128)(2,1)}, bf16[2,16,4096]{2,1,0:T(8,128)(2,1)S(1)}, u32[]{:S(2)}, u32[]{:S(2)}) collective-permute-start(bf16[2,16,4096]{2,1,0:T(8,128)(2,1)} %bitcast.22), channel_id=1, source_target_pairs={{0,24},{1,25},{2,26},{3,27},{4,28},{5,29},{6,30},{7,31},{8,0},{9,1... | collective-permute-start | bytes 786440 | tf_op jit(solution)/shard_map/ppermute | solution.py:399
  10.8 12.2 %collective-permute-start.2 = (bf16[32,4096]{1,0:T(8,128)(2,1)S(1)}, bf16[32,4096]{1,0:T(8,128)(2,1)S(1)}, u32[]{:S(2)}, u32[]{:S(2)}) collective-permute-start(bf16[32,4096]{1,0:T(8,128)(2,1)S(1)} %pad_maximum_fusion.2), channel_id=1, source_target_pairs={{0,2},{1,3},{2,0},{3,1},{4,6},{5,7},{6,4},{7,5},{8,10},{9,11},{10,... | collective-permute-start | bytes 786440 | tf_op jit(solution)/shard_map/ppermute | solution.py:391
  11.1 8.8 %copy-start.2 = (bf16[1,2,16,4096]{3,2,1,0:T(8,128)(2,1)S(1)}, bf16[1,2,16,4096]{3,2,1,0:T(8,128)(2,1)}, u32[]{:S(2)}) copy-start(bf16[1,2,16,4096]{3,2,1,0:T(8,128)(2,1)} %param.11) | copy-start | bytes 786436
  17.9 7.6 %collective-permute-start.5 = (bf16[16,4096]{1,0:T(8,128)(2,1)S(1)}, bf16[16,4096]{1,0:T(8,128)(2,1)S(1)}, u32[]{:S(2)}, u32[]{:S(2)}) collective-permute-start(bf16[16,4096]{1,0:T(8,128)(2,1)S(1)} %collective-permute-done.4.refs_3_), channel_id=1, source_target_pairs={{0,1},{1,0},{2,3},{3,2},{4,5},{5,4},{6,7},{7,6},{8,9},{9,8},{10,11... | collective-permute-start | bytes 393224 | tf_op jit(solution)/shard_map/ppermute | solution.py:391
  18.4 7.2 %collective-permute-start.7 = (bf16[16,4096]{1,0:T(8,128)(2,1)S(1)}, bf16[16,4096]{1,0:T(8,128)(2,1)S(1)}, u32[]{:S(2)}, u32[]{:S(2)}) collective-permute-start(bf16[16,4096]{1,0:T(8,128)(2,1)S(1)} %collective-permute-done.6.refs_5_), channel_id=1, source_target_pairs={{0,1},{1,0},{2,3},{3,2},{4,5},{5,4},{6,7},{7,6},{8,9},{9,8},{10,11... | collective-permute-start | bytes 393224 | tf_op jit(solution)/shard_map/ppermute | solution.py:391
  20.0 8.9 %collective-permute-start.11 = (bf16[16,4096]{1,0:T(8,128)(2,1)S(1)}, bf16[16,4096]{1,0:T(8,128)(2,1)S(1)}, u32[]{:S(2)}, u32[]{:S(2)}) collective-permute-start(bf16[16,4096]{1,0:T(8,128)(2,1)S(1)} %get-tuple-element.68), channel_id=1, source_target_pairs={{0,2},{1,3},{2,0},{3,1},{4,6},{5,7},{6,4},{7,5},{8,10},{9,11},{10,... | collective-permute-start | bytes 393224 | tf_op jit(solution)/shard_map/ppermute | solution.py:391
  20.9 12.2 %collective-permute-start.12 = (bf16[16,4096]{1,0:T(8,128)(2,1)S(1)}, bf16[16,4096]{1,0:T(8,128)(2,1)S(1)}, u32[]{:S(2)}, u32[]{:S(2)}) collective-permute-start(bf16[16,4096]{1,0:T(8,128)(2,1)S(1)} %get-tuple-element.68), channel_id=1, source_target_pairs={{0,4},{1,5},{2,6},{3,7},{4,0},{5,1},{6,2},{7,3},{8,12},{9,13},{10,... | collective-permute-start | bytes 393224 | tf_op jit(solution)/shard_map/ppermute | solution.py:391
  23.0 10.1 %collective-permute-start.13 = (bf16[16,4096]{1,0:T(8,128)(2,1)S(1)}, bf16[16,4096]{1,0:T(8,128)(2,1)S(1)}, u32[]{:S(2)}, u32[]{:S(2)}) collective-permute-start(bf16[16,4096]{1,0:T(8,128)(2,1)S(1)} %get-tuple-element.68), channel_id=1, source_target_pairs={{0,6},{1,7},{2,4},{3,5},{4,2},{5,3},{6,0},{7,1},{8,14},{9,15},{10,... | collective-permute-start | bytes 393224 | tf_op jit(solution)/shard_map/ppermute | solution.py:391
  25.5 24.9 %copy-start.1 = (bf16[1,2,16,4096]{3,2,1,0:T(8,128)(2,1)S(1)}, bf16[1,2,16,4096]{3,2,1,0:T(8,128)(2,1)}, u32[]{:S(2)}) copy-start(bf16[1,2,16,4096]{3,2,1,0:T(8,128)(2,1)} %param.17) | copy-start | bytes 786436
  28.4 10.0 %collective-permute-start.10 = (bf16[16,4096]{1,0:T(8,128)(2,1)S(1)}, bf16[16,4096]{1,0:T(8,128)(2,1)S(1)}, u32[]{:S(2)}, u32[]{:S(2)}) collective-permute-start(bf16[16,4096]{1,0:T(8,128)(2,1)S(1)} %get-tuple-element.67), channel_id=1, source_target_pairs={{0,1},{1,0},{2,3},{3,2},{4,5},{5,4},{6,7},{7,6},{8,9},{9,8},{10,11... | collective-permute-start | bytes 393224 | tf_op jit(solution)/shard_map/ppermute | solution.py:391
  33.2 11.3 %collective-permute-start.15 = (bf16[32,4096]{1,0:T(8,128)(2,1)S(1)}, bf16[32,4096]{1,0:T(8,128)(2,1)S(1)}, u32[]{:S(2)}, u32[]{:S(2)}) collective-permute-start(bf16[32,4096]{1,0:T(8,128)(2,1)S(1)} %get-tuple-element.70), channel_id=1, source_target_pairs={{0,24},{1,25},{2,26},{3,27},{4,28},{5,29},{6,30},{7,31},{8,0},{9,1... | collective-permute-start | bytes 786440 | tf_op jit(solution)/shard_map/ppermute | solution.py:399
  33.2 11.3 %collective-permute-start.16 = (bf16[32,4096]{1,0:T(8,128)(2,1)S(1)}, bf16[32,4096]{1,0:T(8,128)(2,1)S(1)}, u32[]{:S(2)}, u32[]{:S(2)}) collective-permute-start(bf16[32,4096]{1,0:T(8,128)(2,1)S(1)} %get-tuple-element.71), channel_id=1, source_target_pairs={{0,26},{1,27},{2,24},{3,25},{4,30},{5,31},{6,28},{7,29},{8,2},{9,3... | collective-permute-start | bytes 786440 | tf_op jit(solution)/shard_map/ppermute | solution.py:399
  36.9 5.0 %collective-permute-start.8 = (bf16[16,4096]{1,0:T(8,128)(2,1)S(1)}, bf16[16,4096]{1,0:T(8,128)(2,1)S(1)}, u32[]{:S(2)}, u32[]{:S(2)}) collective-permute-start(bf16[16,4096]{1,0:T(8,128)(2,1)S(1)} %get-tuple-element.65), channel_id=1, source_target_pairs={{0,1},{1,0},{2,3},{3,2},{4,5},{5,4},{6,7},{7,6},{8,9},{9,8},{10,11... | collective-permute-start | bytes 393224 | tf_op jit(solution)/shard_map/ppermute | solution.py:391
  38.4 8.2 %collective-permute-start.14 = (bf16[16,4096]{1,0:T(8,128)(2,1)S(1)}, bf16[16,4096]{1,0:T(8,128)(2,1)S(1)}, u32[]{:S(2)}, u32[]{:S(2)}) collective-permute-start(bf16[16,4096]{1,0:T(8,128)(2,1)S(1)} %add_convert_fusion.4), channel_id=1, source_target_pairs={{0,28},{1,29},{2,30},{3,31},{4,24},{5,25},{6,26},{7,27},{8,4},{9,5... | collective-permute-start | bytes 393224 | tf_op jit(solution)/shard_map/ppermute | solution.py:399
  41.9 8.5 %collective-permute-start.9 = (bf16[16,4096]{1,0:T(8,128)(2,1)S(1)}, bf16[16,4096]{1,0:T(8,128)(2,1)S(1)}, u32[]{:S(2)}, u32[]{:S(2)}) collective-permute-start(bf16[16,4096]{1,0:T(8,128)(2,1)S(1)} %add_convert_fusion.5), channel_id=1, source_target_pairs={{0,30},{1,31},{2,28},{3,29},{4,26},{5,27},{6,24},{7,25},{8,6},{9,7... | collective-permute-start | bytes 393224 | tf_op jit(solution)/shard_map/ppermute | solution.py:399
  44.6 5.8 %collective-permute-start.17 = (bf16[16,4096]{1,0:T(8,128)(2,1)S(1)}, bf16[16,4096]{1,0:T(8,128)(2,1)S(1)}, u32[]{:S(2)}, u32[]{:S(2)}) collective-permute-start(bf16[16,4096]{1,0:T(8,128)(2,1)S(1)} %add_convert_fusion.3), channel_id=1, source_target_pairs={{0,1},{1,0},{2,3},{3,2},{4,5},{5,4},{6,7},{7,6},{8,9},{9,8},{10,11... | collective-permute-start | bytes 393224 | tf_op jit(solution)/shard_map/ppermute | solution.py:391
  51.1 8.3 %collective-permute-start.18 = (bf16[16,4096]{1,0:T(8,128)(2,1)S(1)}, bf16[16,4096]{1,0:T(8,128)(2,1)S(1)}, u32[]{:S(2)}, u32[]{:S(2)}) collective-permute-start(bf16[16,4096]{1,0:T(8,128)(2,1)S(1)} %get-tuple-element.72.refs_0_), channel_id=1, source_target_pairs={{0,1},{1,0},{2,3},{3,2},{4,5},{5,4},{6,7},{7,6},{8,9},{9,8},{10,11... | collective-permute-start | bytes 393224 | tf_op jit(solution)/shard_map/ppermute | solution.py:391
  53.4 15.1 %collective-permute-start.21 = (bf16[4,16,4096]{2,1,0:T(8,128)(2,1)S(1)}, bf16[4,16,4096]{2,1,0:T(8,128)(2,1)S(1)}, u32[]{:S(2)}, u32[]{:S(2)}) collective-permute-start(bf16[4,16,4096]{2,1,0:T(8,128)(2,1)S(1)} %pad_maximum_fusion.refs_2_), channel_id=1, source_target_pairs={{0,1},{1,0},{2,3},{3,2},{4,5},{5,4},{6,7},{7,6},{8,9},{9,8},{10,11... | collective-permute-start | bytes 1572872 | tf_op jit(solution)/shard_map/ppermute | solution.py:391
  53.5 14.4 %collective-permute-start.20 = (bf16[16,4096]{1,0:T(8,128)(2,1)S(1)}, bf16[16,4096]{1,0:T(8,128)(2,1)S(1)}, u32[]{:S(2)}, u32[]{:S(2)}) collective-permute-start(bf16[16,4096]{1,0:T(8,128)(2,1)S(1)} %get-tuple-element.72.refs_0_), channel_id=1, source_target_pairs={{0,4},{1,5},{2,6},{3,7},{4,0},{5,1},{6,2},{7,3},{8,12},{9,13},{10,... | collective-permute-start | bytes 393224 | tf_op jit(solution)/shard_map/ppermute | solution.py:391
  58.7 8.2 %collective-permute-start.23 = (bf16[16,4096]{1,0:T(8,128)(2,1)S(1)}, bf16[16,4096]{1,0:T(8,128)(2,1)S(1)}, u32[]{:S(2)}, u32[]{:S(2)}) collective-permute-start(bf16[16,4096]{1,0:T(8,128)(2,1)S(1)} %get-tuple-element.72.refs_0_), channel_id=1, source_target_pairs={{0,6},{1,7},{2,4},{3,5},{4,2},{5,3},{6,0},{7,1},{8,14},{9,15},{10,... | collective-permute-start | bytes 393224 | tf_op jit(solution)/shard_map/ppermute | solution.py:391
  59.4 16.6 %collective-permute-start.19 = (bf16[32,4096]{1,0:T(8,128)(2,1)S(1)}, bf16[32,4096]{1,0:T(8,128)(2,1)S(1)}, u32[]{:S(2)}, u32[]{:S(2)}) collective-permute-start(bf16[32,4096]{1,0:T(8,128)(2,1)S(1)} %pad_maximum_fusion.3), channel_id=1, source_target_pairs={{0,2},{1,3},{2,0},{3,1},{4,6},{5,7},{6,4},{7,5},{8,10},{9,11},{10,... | collective-permute-start | bytes 786440 | tf_op jit(solution)/shard_map/ppermute | solution.py:391
  66.9 7.4 %collective-permute-start.24 = (bf16[16,4096]{1,0:T(8,128)(2,1)S(1)}, bf16[16,4096]{1,0:T(8,128)(2,1)S(1)}, u32[]{:S(2)}, u32[]{:S(2)}) collective-permute-start(bf16[16,4096]{1,0:T(8,128)(2,1)S(1)} %collective-permute-done.23.refs_5_), channel_id=1, source_target_pairs={{0,1},{1,0},{2,3},{3,2},{4,5},{5,4},{6,7},{7,6},{8,9},{9,8},{10,11... | collective-permute-start | bytes 393224 | tf_op jit(solution)/shard_map/ppermute | solution.py:391
  68.5 7.5 %collective-permute-start.22 = (bf16[16,4096]{1,0:T(8,128)(2,1)S(1)}, bf16[16,4096]{1,0:T(8,128)(2,1)S(1)}, u32[]{:S(2)}, u32[]{:S(2)}) collective-permute-start(bf16[16,4096]{1,0:T(8,128)(2,1)S(1)} %collective-permute-done.20.refs_3_), channel_id=1, source_target_pairs={{0,1},{1,0},{2,3},{3,2},{4,5},{5,4},{6,7},{7,6},{8,9},{9,8},{10,11... | collective-permute-start | bytes 393224 | tf_op jit(solution)/shard_map/ppermute | solution.py:391
  71.0 10.8 %collective-permute-start.26 = (bf16[16,4096]{1,0:T(8,128)(2,1)S(1)}, bf16[16,4096]{1,0:T(8,128)(2,1)S(1)}, u32[]{:S(2)}, u32[]{:S(2)}) collective-permute-start(bf16[16,4096]{1,0:T(8,128)(2,1)S(1)} %get-tuple-element.79), channel_id=1, source_target_pairs={{0,2},{1,3},{2,0},{3,1},{4,6},{5,7},{6,4},{7,5},{8,10},{9,11},{10,... | collective-permute-start | bytes 393224 | tf_op jit(solution)/shard_map/ppermute | solution.py:391
  72.8 11.4 %collective-permute-start.27 = (bf16[16,4096]{1,0:T(8,128)(2,1)S(1)}, bf16[16,4096]{1,0:T(8,128)(2,1)S(1)}, u32[]{:S(2)}, u32[]{:S(2)}) collective-permute-start(bf16[16,4096]{1,0:T(8,128)(2,1)S(1)} %get-tuple-element.79), channel_id=1, source_target_pairs={{0,4},{1,5},{2,6},{3,7},{4,0},{5,1},{6,2},{7,3},{8,12},{9,13},{10,... | collective-permute-start | bytes 393224 | tf_op jit(solution)/shard_map/ppermute | solution.py:391
  74.3 10.6 %collective-permute-start.28 = (bf16[16,4096]{1,0:T(8,128)(2,1)S(1)}, bf16[16,4096]{1,0:T(8,128)(2,1)S(1)}, u32[]{:S(2)}, u32[]{:S(2)}) collective-permute-start(bf16[16,4096]{1,0:T(8,128)(2,1)S(1)} %get-tuple-element.79), channel_id=1, source_target_pairs={{0,6},{1,7},{2,4},{3,5},{4,2},{5,3},{6,0},{7,1},{8,14},{9,15},{10,... | collective-permute-start | bytes 393224 | tf_op jit(solution)/shard_map/ppermute | solution.py:391
  78.9 6.9 %collective-permute-start.30 = (bf16[16,4096]{1,0:T(8,128)(2,1)S(1)}, bf16[16,4096]{1,0:T(8,128)(2,1)S(1)}, u32[]{:S(2)}, u32[]{:S(2)}) collective-permute-start(bf16[16,4096]{1,0:T(8,128)(2,1)S(1)} %get-tuple-element.82), channel_id=1, source_target_pairs={{0,1},{1,0},{2,3},{3,2},{4,5},{5,4},{6,7},{7,6},{8,9},{9,8},{10,11... | collective-permute-start | bytes 393224 | tf_op jit(solution)/shard_map/ppermute | solution.py:391
  80.8 8.0 %collective-permute-start.25 = (bf16[16,4096]{1,0:T(8,128)(2,1)S(1)}, bf16[16,4096]{1,0:T(8,128)(2,1)S(1)}, u32[]{:S(2)}, u32[]{:S(2)}) collective-permute-start(bf16[16,4096]{1,0:T(8,128)(2,1)S(1)} %get-tuple-element.78), channel_id=1, source_target_pairs={{0,1},{1,0},{2,3},{3,2},{4,5},{5,4},{6,7},{7,6},{8,9},{9,8},{10,11... | collective-permute-start | bytes 393224 | tf_op jit(solution)/shard_map/ppermute | solution.py:391
  81.8 23.6 %copy-start = (bf16[1,2,16,4096]{3,2,1,0:T(8,128)(2,1)S(1)}, bf16[1,2,16,4096]{3,2,1,0:T(8,128)(2,1)}, u32[]{:S(2)}) copy-start(bf16[1,2,16,4096]{3,2,1,0:T(8,128)(2,1)} %param.16) | copy-start | bytes 786436
  81.8 4.0 %collective-permute-start.35 = (f32[2,128]{1,0:T(2,128)S(1)}, f32[2,128]{1,0:T(2,128)S(1)}, u32[]{:S(2)}, u32[]{:S(2)}) collective-permute-start(f32[2,128]{1,0:T(2,128)S(1)} %gate_part.1), channel_id=1, source_target_pairs={{0,1},{1,0},{2,3},{3,2},{4,5},{5,4},{6,7},{7,6},{8,9},{9,8},{10,11... | collective-permute-start | bytes 3080 | tf_op jit(solution)/shard_map/ppermute | solution.py:391
  84.2 13.8 %collective-permute-start.32 = (bf16[32,4096]{1,0:T(8,128)(2,1)S(1)}, bf16[32,4096]{1,0:T(8,128)(2,1)S(1)}, u32[]{:S(2)}, u32[]{:S(2)}) collective-permute-start(bf16[32,4096]{1,0:T(8,128)(2,1)S(1)} %get-tuple-element.84), channel_id=1, source_target_pairs={{0,2},{1,3},{2,0},{3,1},{4,6},{5,7},{6,4},{7,5},{8,10},{9,11},{10,... | collective-permute-start | bytes 786440 | tf_op jit(solution)/shard_map/ppermute | solution.py:391
  85.8 12.3 %collective-permute-start.31 = (bf16[16,4096]{1,0:T(8,128)(2,1)S(1)}, bf16[16,4096]{1,0:T(8,128)(2,1)S(1)}, u32[]{:S(2)}, u32[]{:S(2)}) collective-permute-start(bf16[16,4096]{1,0:T(8,128)(2,1)S(1)} %add_convert_fusion.1), channel_id=1, source_target_pairs={{0,4},{1,5},{2,6},{3,7},{4,0},{5,1},{6,2},{7,3},{8,12},{9,13},{10,... | collective-permute-start | bytes 393224 | tf_op jit(solution)/shard_map/ppermute | solution.py:391
  88.7 9.3 %collective-permute-start.34 = (bf16[16,4096]{1,0:T(8,128)(2,1)S(1)}, bf16[16,4096]{1,0:T(8,128)(2,1)S(1)}, u32[]{:S(2)}, u32[]{:S(2)}) collective-permute-start(bf16[16,4096]{1,0:T(8,128)(2,1)S(1)} %get-tuple-element.87), channel_id=1, source_target_pairs={{0,8},{1,9},{2,10},{3,11},{4,12},{5,13},{6,14},{7,15},{8,16},{9,17... | collective-permute-start | bytes 393224 | tf_op jit(solution)/shard_map/ppermute | solution.py:399
  88.8 18.1 %collective-permute-start.39 = (bf16[4,16,4096]{2,1,0:T(8,128)(2,1)S(1)}, bf16[4,16,4096]{2,1,0:T(8,128)(2,1)S(1)}, u32[]{:S(2)}, u32[]{:S(2)}) collective-permute-start(bf16[4,16,4096]{2,1,0:T(8,128)(2,1)S(1)} %pad_maximum_fusion.1.refs_4_), channel_id=1, source_target_pairs={{0,1},{1,0},{2,3},{3,2},{4,5},{5,4},{6,7},{7,6},{8,9},{9,8},{10,11... | collective-permute-start | bytes 1572872 | tf_op jit(solution)/shard_map/ppermute | solution.py:391
  89.5 8.7 %collective-permute-start.29 = (bf16[16,4096]{1,0:T(8,128)(2,1)S(1)}, bf16[16,4096]{1,0:T(8,128)(2,1)S(1)}, u32[]{:S(2)}, u32[]{:S(2)}) collective-permute-start(bf16[16,4096]{1,0:T(8,128)(2,1)S(1)} %add_convert_fusion.2), channel_id=1, source_target_pairs={{0,6},{1,7},{2,4},{3,5},{4,2},{5,3},{6,0},{7,1},{8,14},{9,15},{10,... | collective-permute-start | bytes 393224 | tf_op jit(solution)/shard_map/ppermute | solution.py:391
  98.0 7.4 %collective-permute-start.33 = (bf16[16,4096]{1,0:T(8,128)(2,1)S(1)}, bf16[16,4096]{1,0:T(8,128)(2,1)S(1)}, u32[]{:S(2)}, u32[]{:S(2)}) collective-permute-start(bf16[16,4096]{1,0:T(8,128)(2,1)S(1)} %add_convert_fusion), channel_id=1, source_target_pairs={{0,1},{1,0},{2,3},{3,2},{4,5},{5,4},{6,7},{7,6},{8,9},{9,8},{10,11... | collective-permute-start | bytes 393224 | tf_op jit(solution)/shard_map/ppermute | solution.py:391
  98.1 7.3 %collective-permute-start.36 = (f32[2,128]{1,0:T(2,128)S(1)}, f32[2,128]{1,0:T(2,128)S(1)}, u32[]{:S(2)}, u32[]{:S(2)}) collective-permute-start(f32[2,128]{1,0:T(2,128)S(1)} %add.27.refs_8_), channel_id=1, source_target_pairs={{0,2},{1,3},{2,0},{3,1},{4,6},{5,7},{6,4},{7,5},{8,10},{9,11},{10,... | collective-permute-start | bytes 3080 | tf_op jit(solution)/shard_map/ppermute | solution.py:391
  98.1 7.2 %collective-permute-start.37 = (f32[2,128]{1,0:T(2,128)S(1)}, f32[2,128]{1,0:T(2,128)S(1)}, u32[]{:S(2)}, u32[]{:S(2)}) collective-permute-start(f32[2,128]{1,0:T(2,128)S(1)} %add.27.refs_8_), channel_id=1, source_target_pairs={{0,4},{1,5},{2,6},{3,7},{4,0},{5,1},{6,2},{7,3},{8,12},{9,13},{10,... | collective-permute-start | bytes 3080 | tf_op jit(solution)/shard_map/ppermute | solution.py:391
  98.2 7.1 %collective-permute-start.38 = (f32[2,128]{1,0:T(2,128)S(1)}, f32[2,128]{1,0:T(2,128)S(1)}, u32[]{:S(2)}, u32[]{:S(2)}) collective-permute-start(f32[2,128]{1,0:T(2,128)S(1)} %add.27.refs_8_), channel_id=1, source_target_pairs={{0,6},{1,7},{2,4},{3,5},{4,2},{5,3},{6,0},{7,1},{8,14},{9,15},{10,... | collective-permute-start | bytes 3080 | tf_op jit(solution)/shard_map/ppermute | solution.py:391
